TPU v7x, 512 devices: a whole 4x4x16 slice. The times are simulated.
512 devices in a mesh: tm: 64 (over x, z), mp: 8 (over y, core).
Axes of the slice: x: 4, y: 4, z: 16, core: 2. Of those that a mesh axis runs over, the one named last changes fastest.
Arguments:
- mel_frames: bfloat16 [38400, 128], P('tm'), may hold values from -6 to 6
- conv_weight: bfloat16 [384, 1280], P(None, 'mp'), may hold values from -0.3125 to 0.3125
- patches: bfloat16 [49152, 1280], P('tm', 'mp'), may hold values from -6 to 6
- vit_up: bfloat16 [1280, 5120], P(None, 'mp'), may hold values from -0.15625 to 0.15625
- vit_down: bfloat16 [5120, 1280], P('mp'), may hold values from -0.078125 to 0.078125
- audio_proj: bfloat16 [1280, 3584], P('tm', 'mp'), may hold values from -0.15625 to 0.15625
- merger: bfloat16 [5120, 3584], P('tm', 'mp'), may hold values from -0.078125 to 0.078125
- text_rows: bfloat16 [512, 64, 3584], P(None, 'tm', 'mp'), may hold values from -6 to 6
- span_order: int32 [192], replicated, may hold values from 0 to 191, as said below
- offsets: int32 [192], replicated, may hold values from 0 to 32726, as said below
- audio_count: int32 [192], replicated, may hold values from 10 to 50
- video_count: int32 [192], replicated, may hold values from 32 to 64
Outputs:
- sequence_rows: bfloat16 [512, 64, 3584], P(None, 'tm', 'mp')
Inputs may be any that keep to these rules, and one draw needn't show every extreme that they name: span_order lists each span once. Listed spans take increasing, non-intersecting ranges of video_count + audio_count positions starting at offsets, all before 32768.
All inputs are finite; a program needn't handle non-finite values.
Results may differ from a plain program's by a relative error of at most 0.0034.
Values may be sent and summed in bfloat16 or wider, within the bound.
No kernel may reach another device: no remote copies, remote signals or barrier semaphores. Data moves between devices by JAX's collectives and lax.ppermute only.
A program may use at most 64 MiB of HBM per device.

v0:
```python
import jax
import jax.numpy as jnp
from jax import lax
from jax.sharding import PartitionSpec as P

AT = 50
VT = 64


def from_behind(value, axis, steps):
    count = lax.axis_size(axis)
    leading, last = (max(0, -steps), min(count, count - steps))
    return lax.ppermute(value, axis, [(source, source + steps) for source in range(leading, last)])


def span_starts(span_order, offsets):
    listed = jnp.arange(span_order.shape[0], dtype=jnp.int32)
    matches = (span_order[:, None] == listed[None, :]).astype(jnp.int32)
    return jnp.sum(matches * offsets[:, None], axis=0)


def local(
    mel_frames,
    conv_weight,
    patches,
    vit_up,
    vit_down,
    audio_proj,
    merger,
    text_rows,
    span_order,
    offsets,
    audio_count,
    video_count,
):
    owners = lax.axis_size("tm")
    position = lax.axis_index("tm")
    spans = mel_frames.shape[0] // (4 * AT)
    mel_rim = from_behind(mel_frames[-1:], "tm", 1)
    odd_rows = mel_frames[1::2]
    earlier = jnp.concatenate([mel_rim, odd_rows[:-1]], axis=0)
    stacked = jnp.concatenate([earlier, mel_frames[0::2], odd_rows], axis=1)
    active = jax.nn.gelu(
        jnp.dot(stacked, conv_weight, preferred_element_type=jnp.float32), approximate=False
    )
    pooled = (0.5 * (active[0::2] + active[1::2])).astype(jnp.bfloat16)
    patch_full, audio_full = (
        lax.all_gather(patches, "mp", axis=1, tiled=True),
        lax.all_gather(pooled, "mp", axis=1, tiled=True),
    )
    widened = patch_full.astype(jnp.float32)
    average = jnp.mean(widened, axis=1, keepdims=True)
    centred = widened - average
    spread = jnp.mean(centred * centred, axis=1, keepdims=True)
    normed = (centred * lax.rsqrt(spread + 1e-06)).astype(jnp.bfloat16)
    hidden = jax.nn.gelu(
        jnp.dot(normed, vit_up, preferred_element_type=jnp.float32), approximate=False
    ).astype(jnp.bfloat16)
    partial_value = jnp.dot(hidden, vit_down, preferred_element_type=jnp.float32)
    summed = lax.psum(partial_value, "mp")
    vit_out = (widened + summed).astype(jnp.bfloat16)
    audio_weight, merger_weight = (
        lax.all_gather(audio_proj, "tm", axis=0, tiled=True),
        lax.all_gather(merger, "tm", axis=0, tiled=True),
    )
    merged = vit_out.reshape(vit_out.shape[0] // 4, 4 * vit_out.shape[1])
    video_rows = jnp.dot(merged, merger_weight, preferred_element_type=jnp.float32).astype(
        jnp.bfloat16
    )
    audio_rows = jnp.dot(audio_full, audio_weight, preferred_element_type=jnp.float32).astype(
        jnp.bfloat16
    )
    columns = video_rows.shape[1]
    audio_slots = (AT + owners - 1) // owners
    video_slots = (VT + owners - 1) // owners
    starts = span_starts(span_order, offsets)
    first_span = position * spans
    local_start = lax.dynamic_slice_in_dim(starts, first_span, spans)[None, :, None]
    local_audio = lax.dynamic_slice_in_dim(audio_count, first_span, spans)[None, :, None]
    local_video = lax.dynamic_slice_in_dim(video_count, first_span, spans)[None, :, None]
    owner_ids = jnp.arange(owners, dtype=jnp.int32)[:, None, None]
    span_ids = jnp.arange(spans, dtype=jnp.int32)[None, :, None]
    video_steps = owners * jnp.arange(video_slots, dtype=jnp.int32)[None, None, :]
    audio_steps = owners * jnp.arange(audio_slots, dtype=jnp.int32)[None, None, :]
    video_index = jnp.mod(owner_ids - local_start, owners) + video_steps
    video_usable = video_index < local_video
    video_source = jnp.where(video_usable, span_ids * VT + video_index, 0)
    video_send = jnp.where(
        video_usable[..., None], video_rows[video_source], jnp.zeros((), jnp.bfloat16)
    )
    audio_index = jnp.mod(owner_ids - local_start - local_video, owners) + audio_steps
    audio_usable = audio_index < local_audio
    audio_source = jnp.where(audio_usable, span_ids * AT + audio_index, 0)
    audio_send = jnp.where(
        audio_usable[..., None], audio_rows[audio_source], jnp.zeros((), jnp.bfloat16)
    )
    outgoing = jnp.concatenate([video_send, audio_send], axis=2)
    incoming = lax.all_to_all(outgoing, "tm", split_axis=0, concat_axis=0, tiled=True)
    seq_count = text_rows.shape[0]
    source_start = starts.reshape(owners, spans)[:, :, None]
    source_video = video_count.reshape(owners, spans)[:, :, None]
    source_audio = audio_count.reshape(owners, spans)[:, :, None]
    video_where = jnp.mod(position - source_start, owners) + video_steps
    video_place = jnp.where(
        video_where < source_video, (source_start + video_where) // owners, seq_count
    )
    audio_where = jnp.mod(position - source_start - source_video, owners) + audio_steps
    audio_place = jnp.where(
        audio_where < source_audio, (source_start + source_video + audio_where) // owners, seq_count
    )
    slot_rows = jnp.concatenate([video_place, audio_place], axis=2).reshape(-1)
    sequence_rows = text_rows[:, 0, :].at[slot_rows].set(incoming.reshape(-1, columns), mode="drop")
    return sequence_rows[:, None, :]


def solution(mesh):
    placed = (
        P("tm", None),
        P(None, "mp"),
        P("tm", "mp"),
        P(None, "mp"),
        P("mp", None),
        P("tm", "mp"),
        P("tm", "mp"),
        P(None, "tm", "mp"),
        P(),
        P(),
        P(),
        P(),
    )
    return jax.shard_map(
        local, mesh=mesh, in_specs=placed, out_specs=P(None, "tm", "mp"), check_vma=False
    )
```

profile of v0, /device:TPU:1, one launch (start us, length us, event | category | flops | bytes accessed | tf_op | source)
XLA Modules:
  0.0 465.0 jit_solution(2557153048289407795)
XLA Ops:
  6.5 0.7 all-gather.6.cloned.1.call-update
  7.3 0.7 all-gather.10.cloned.1.call-update
  8.1 39.8 %all-gather.6.cloned.1.call-done = bf16[768,1280]{0,1:T(8,128)(2,1)} async-done(((bf16[768,160]{0,1:T(8,128)(2,1)}), bf16[768,1280]{0,1:T(8,128)(2,1)}) %all-gather.6.cloned.1.call-update) | async-done | bytes 1966096 | tf_op jit(solution)/shard_map/all_gather | solution.py:48
  47.9 4.0 copy.39
  51.9 2.0 convert_reduce_fusion
  54.0 0.6 fusion.2
  54.7 10.2 %fusion.22 = f32[768,1280]{1,0:T(8,128)} fusion(bf16[640,1280]{1,0:T(8,128)(2,1)S(1)} %copy-done, bf16[1280,640]{1,0:T(8,128)(2,1)S(1)} %copy-done.8, bf16[768,1280]{1,0:T(8,128)(2,1)} %copy.39, f32[768]{0:T(1024)S(1)} %add_rsqrt_fusion, f32[768]{0:T(1024)S(1)} %broadcast_multiply_fusion), kind=kOutput, calls=%fused_computation.33 | convolution fusion | flops 2552463360 | bytes 9181184 | tf_op jit(solution)/shard_map/dot_general | solution.py:59
  65.0 0.5 all-gather.8.cloned.1.call-update
  65.8 3.1 collective-permute-start
  70.1 0.4 slice.21
  70.5 0.7 fusion.55
  71.3 3.3 slice.22
  74.6 3.4 slice.23
  78.1 13.8 %all-gather = bf16[8,160,150]{1,2,0:T(8,128)(2,1)S(1)} all-gather(bf16[1,160,150]{1,2,0:T(8,128)(2,1)S(1)} %copy.40), channel_id=1, replica_groups=mesh['tm'=64,'mp'=8] {'mp'}, dimensions={0}, use_global_device_ids=true | all-gather | bytes 432000 | tf_op jit(solution)/shard_map/all_gather | solution.py:49
  92.0 0.7 reshape.772
  92.7 89.2 %all-gather.10.cloned.1.call-done = bf16[64,20,448]{2,1,0:T(8,128)(2,1)} async-done(((bf16[1,20,448]{2,1,0:T(8,128)(2,1)}), bf16[64,20,448]{2,1,0:T(8,128)(2,1)}) %all-gather.10.cloned.1.call-update) | async-done | bytes 1146896 | tf_op jit(solution)/shard_map/all_gather | solution.py:63
  181.9 2.5 reshape.774
  184.4 0.4 convolution_convert_fusion.1
  184.8 1.0 gather_fusion.1
  186.1 88.6 %all-reduce.2.cloned.1.call-done = f32[768,1280]{1,0:T(8,128)} async-done(((f32[768,1280]{1,0:T(8,128)}), f32[768,1280]{1,0:T(8,128)}) %all-reduce.2.cloned.1.call-update) | async-done | bytes 3932176 | tf_op jit(solution)/shard_map/psum | solution.py:60
  274.7 4.4 fusion.4
  279.1 4.1 reshape.741
  283.2 137.1 %all-gather.8.cloned.1.call-done = bf16[5120,448]{1,0:T(8,128)(2,1)} async-done(((bf16[80,448]{1,0:T(8,128)(2,1)}), bf16[5120,448]{1,0:T(8,128)(2,1)}) %all-gather.8.cloned.1.call-update) | async-done | bytes 4587536 | tf_op jit(solution)/shard_map/all_gather | solution.py:64
  420.3 4.3 convolution_convert_fusion
  424.6 1.0 gather_fusion
  426.0 0.4 pad_maximum_fusion
  426.4 1.2 copy.42
  427.6 9.3 %all-to-all-start = ((bf16[64,3,2,448]{3,2,1,0:T(2,128)(2,1)}), bf16[64,3,2,448]{3,2,1,0:T(2,128)(2,1)S(1)}, u32[]{:S(2)}, u32[]{:S(2)}) async-start(bf16[64,3,2,448]{3,2,1,0:T(2,128)(2,1)} %copy.42), calls=%async_computation | async-start | bytes 786432 | tf_op jit(solution)/shard_map/all_to_all | solution.py:98
  437.4 0.5 copy.38
  438.3 16.7 %all-to-all-done = bf16[64,3,2,448]{3,2,1,0:T(2,128)(2,1)S(1)} async-done(((bf16[64,3,2,448]{3,2,1,0:T(2,128)(2,1)}), bf16[64,3,2,448]{3,2,1,0:T(2,128)(2,1)S(1)}, u32[]{:S(2)}, u32[]{:S(2)}) %all-to-all-start) | async-done | bytes 344096 | tf_op jit(solution)/shard_map/all_to_all | solution.py:98
  455.3 2.2 scatter_fusion
  457.5 1.0 copy.43
  (57 shorter events, 3.7 us)
Async XLA Ops:
  6.5 48.1 %copy-start = (bf16[640,1280]{1,0:T(8,128)(2,1)S(1)}, bf16[640,1280]{1,0:T(8,128)(2,1)}, u32[]{:S(2)}) copy-start(bf16[640,1280]{1,0:T(8,128)(2,1)} %param.16) | copy-start | bytes 4915204
  6.5 41.4 %all-gather.6.cloned.1.call-start = ((), (), s32[]{:S(2)}) async-start(), calls=%async_computation.1 | async-start | bytes 2211840 | tf_op jit(solution)/shard_map/all_gather | solution.py:48
  7.3 174.7 %all-gather.10.cloned.1.call-start = ((), (), s32[]{:S(2)}) async-start(), calls=%async_computation.4 | async-start | bytes 1597440 | tf_op jit(solution)/shard_map/all_gather | solution.py:63
  8.0 266.7 %all-reduce.2.cloned.1.call-start = ((), (), s32[]{:S(2)}) async-start(), calls=%async_computation.2 | async-start | bytes 7864320 | tf_op jit(solution)/shard_map/psum | solution.py:60
  51.9 2.1 copy-start.1
  51.9 2.8 copy-start.8
  64.9 0.9 copy-start.3
  64.9 4.1 copy-start.4
  64.9 4.1 copy-start.5
  64.9 4.3 copy-start.6
  64.9 4.4 copy-start.7
  64.9 5.6 %copy-start.9 = (bf16[384,160]{0,1:T(8,128)(2,1)S(1)}, bf16[384,160]{0,1:T(8,128)(2,1)}, u32[]{:S(2)}) copy-start(bf16[384,160]{0,1:T(8,128)(2,1)} %param.13) | copy-start | bytes 368644
  64.9 355.4 %all-gather.8.cloned.1.call-start = ((), (), s32[]{:S(2)}) async-start(), calls=%async_computation.3 | async-start | bytes 5324800 | tf_op jit(solution)/shard_map/all_gather | solution.py:64
  65.8 4.7 %collective-permute-start = (bf16[1,128]{1,0:T(2,128)(2,1)S(1)}, bf16[1,128]{1,0:T(2,128)(2,1)S(1)}, u32[]{:S(2)}, u32[]{:S(2)}) collective-permute-start(bf16[1,128]{1,0:T(2,128)(2,1)S(1)} %slice.18), channel_id=1, source_target_pairs={{0,8},{8,16},{16,24},{24,32},{32,40},{40,48},{48,56},{56,64},{64,7... | collective-permute-start | bytes 776 | tf_op jit(solution)/shard_map/ppermute | solution.py:13
  425.7 12.3 %copy-start.2 = (bf16[512,1,448]{0,2,1:T(8,128)(2,1)S(1)}, bf16[512,1,448]{0,2,1:T(8,128)(2,1)}, u32[]{:S(2)}) copy-start(bf16[512,1,448]{0,2,1:T(8,128)(2,1)} %param.19) | copy-start | bytes 1376260
  427.6 27.4 %all-to-all-start = ((bf16[64,3,2,448]{3,2,1,0:T(2,128)(2,1)}), bf16[64,3,2,448]{3,2,1,0:T(2,128)(2,1)S(1)}, u32[]{:S(2)}, u32[]{:S(2)}) async-start(bf16[64,3,2,448]{3,2,1,0:T(2,128)(2,1)} %copy.42), calls=%async_computation | async-start | bytes 786432 | tf_op jit(solution)/shard_map/all_to_all | solution.py:98
Sparse Core Ops, SparseCore 0:
  9.5 38.3 all-gather.5
  50.8 131.0 all-gather.9
  184.3 90.3 all-reduce.1
  277.5 142.7 all-gather.7
where the time goes:
time: 474 us; the launch traced here: 465 us
  waiting for transfers between devices  373 us (79%)
  local copies, waits for them, and re-layouts  28.1 us (6%)
  matrix products  15.6 us (3%)
  blocking collectives  13.8 us (3%)
  between operations  13.5 us (3%)
  starting transfers between devices  12.5 us (3%)
  other arithmetic  8.25 us (2%)
    all_gather x1, waiting for transfers between devices, local(): lax.all_gather(merger, 'tm', axis=0, tiled=True)  137 us
    all_gather x1, waiting for transfers between devices, local(): lax.all_gather(audio_proj, 'tm', axis=0, tiled=True)  89.2 us
    psum x1, waiting for transfers between devices, local(): summed = lax.psum(partial_value, 'mp')  88.6 us
    all_gather x1, waiting for transfers between devices, local(): lax.all_gather(patches, 'mp', axis=1, tiled=True)  39.8 us
    all_to_all x1, waiting for transfers between devices, local(): lax.all_to_all(outgoing, 'tm', split_axis=0, concat_axis=0, tiled=True)  16.7 us
    all_gather x1, blocking collectives, local(): lax.all_gather(pooled, 'mp', axis=1, tiled=True)  13.8 us
    dot_general x1, matrix products, local(): jnp.dot(hidden, vit_down, preferred_element_type=jnp.float32)  10.2 us
  transfers between devices with their start and end apart: 6, of which 5 were waited for; matrix products, arithmetic and copies ran while one was open for 9% of the time, Pallas kernels for 0%

commit v1 on v0

v1 whole, which is shorter than its diff:
```python
import jax
import jax.numpy as jnp
from jax import lax
from jax.sharding import Mesh, PartitionSpec as P

AT = 50
VT = 64
BF = jnp.bfloat16
F32 = jnp.float32
TM = ("x", "z")
MP = ("y", "core")


def span_starts(span_order, offsets):
    listed = jnp.arange(span_order.shape[0], dtype=jnp.int32)
    matches = (span_order[:, None] == listed[None, :]).astype(jnp.int32)
    return jnp.sum(matches * offsets[:, None], axis=0)


def ring(value, axis, step):
    count = lax.axis_size(axis)
    return lax.ppermute(value, axis, [(i, (i + step) % count) for i in range(count)])


def gather_x(value):
    return [value] + [ring(value, "x", k) for k in (1, 3, 2)]


def gelu(value):
    return jax.nn.gelu(value, approximate=False)


def dot(a, b):
    return jnp.dot(a, b, preferred_element_type=F32)


def local(
    mel_frames,
    conv_weight,
    patches,
    vit_up,
    vit_down,
    audio_proj,
    merger,
    text_rows,
    span_order,
    offsets,
    audio_count,
    video_count,
):
    owners = lax.axis_size("x") * lax.axis_size("z")
    nx, nz, ny = (lax.axis_size(a) for a in ("x", "z", "y"))
    position = lax.axis_index(TM)
    my_x, my_y, my_core = (lax.axis_index(a) for a in ("x", "y", "core"))
    spans = mel_frames.shape[0] // (4 * AT)
    tokens = spans * owners
    half = tokens // 2
    columns = merger.shape[1]

    with jax.named_scope("weights_x"):
        own = jnp.concatenate([merger, audio_proj], axis=0)
        parts = gather_x(own)
        rows_m, rows_a = merger.shape[0], audio_proj.shape[0]
        block = jnp.concatenate([p[:rows_m] for p in parts] + [p[rows_m:] for p in parts], axis=0)
    with jax.named_scope("weights_z"):
        weights = lax.all_gather(block, "z", axis=0, tiled=False)

    with jax.named_scope("route"):
        starts = span_starts(span_order, offsets)
        first_span = position * spans
        local_start = lax.dynamic_slice_in_dim(starts, first_span, spans)[None, :]
        local_video = lax.dynamic_slice_in_dim(video_count, first_span, spans)[None, :]
        owner_ids = jnp.arange(owners, dtype=jnp.int32)[:, None]
        span_ids = jnp.arange(spans, dtype=jnp.int32)[None, :]
        video_index = jnp.mod(owner_ids - local_start, owners) + span_ids * VT
        token_rows = patches.reshape(spans * VT, -1)
        video_send = token_rows[video_index.reshape(-1)].reshape(owners, spans, -1)
        video_in = lax.all_to_all(video_send, TM, 0, 0, tiled=True).reshape(tokens, -1)

    with jax.named_scope("audio_conv"):
        last = owners - 1
        rim = lax.ppermute(mel_frames[-1:], TM, [(i, i + 1) for i in range(last)])
        f0, f1, f2, f3 = (mel_frames[k::4] for k in range(4))
        before = jnp.concatenate([rim, f3[:-1]], axis=0)
        even = dot(jnp.concatenate([before, f0, f1], axis=1), conv_weight)
        odd = dot(jnp.concatenate([f1, f2, f3], axis=1), conv_weight)
        pooled = (0.5 * (gelu(even) + gelu(odd))).astype(BF)
        audio_index = jnp.minimum(jnp.mod(owner_ids - local_start - local_video, owners), AT - 1)
        audio_index = (audio_index + span_ids * AT).reshape(-1)
        audio_send = pooled[audio_index].reshape(owners, spans, -1)
        audio_in = lax.all_to_all(audio_send, TM, 0, 0, tiled=True).reshape(tokens, -1)

    with jax.named_scope("core_swap"):
        swap = lambda v: lax.ppermute(v, "core", [(0, 1), (1, 0)])
        up_other, down_other = swap(vit_up), swap(vit_down)

        def pair(value, width):
            mine = lax.dynamic_slice_in_dim(value, my_core * half, half)
            theirs = swap(lax.dynamic_slice_in_dim(value, (1 - my_core) * half, half))
            mine, theirs = (v.reshape(half, -1, width) for v in (mine, theirs))
            first = jnp.where(my_core == 0, mine, theirs)
            second = jnp.where(my_core == 0, theirs, mine)
            return jnp.concatenate([first, second], axis=2).reshape(half, -1)

        width = patches.shape[1]
        video_pair = pair(video_in, width)
        audio_pair = pair(audio_in, width)

    with jax.named_scope("gather_y"):
        video_y = lax.all_gather(video_pair, "y", axis=0, tiled=False)
        video_y = video_y.reshape(ny, half, 4, 2 * width)
        rows = jnp.transpose(video_y, (2, 1, 0, 3)).reshape(4 * half, ny * 2 * width)

    with jax.named_scope("vision"):
        widened = rows.astype(F32)
        average = jnp.mean(widened, axis=1, keepdims=True)
        centred = widened - average
        spread = jnp.mean(centred * centred, axis=1, keepdims=True)
        normed = (centred * lax.rsqrt(spread + 1e-06)).astype(BF)
        hidden = gelu(dot(normed, vit_up)).astype(BF)
        hidden_other = gelu(dot(normed, up_other)).astype(BF)
        partial_sum = dot(hidden, vit_down) + dot(hidden_other, down_other)
        partial_sum = partial_sum.astype(BF).reshape(4, half, -1)

    with jax.named_scope("sum_y"):
        full_width = partial_sum.shape[2]
        audio_flat = audio_pair.reshape(-1, full_width)
        audio_rows_n = audio_flat.shape[0]
        pad = -audio_rows_n % 16
        audio_flat = jnp.pad(audio_flat, ((0, pad), (0, 0)))
        audio_all = jnp.broadcast_to(audio_flat, (ny,) + audio_flat.shape)
        outgoing = jnp.concatenate([partial_sum, audio_all], axis=1)
        incoming = lax.all_to_all(outgoing, "y", 0, 0, tiled=True)
        residual = lax.dynamic_index_in_dim(rows.reshape(4, half, -1), my_y, 0, keepdims=False)
        summed = jnp.sum(incoming[:, :half].astype(F32), axis=0)
        vit_out = (residual.astype(F32) + summed).astype(BF)
        audio_y = incoming[:, half : half + audio_rows_n].reshape(ny, half, 2 * width)
        audio_tok = jnp.transpose(audio_y, (1, 0, 2)).reshape(half, -1)

    with jax.named_scope("gather_vit"):
        vit_y = lax.all_gather(vit_out, "y", axis=0, tiled=False)
        both = jnp.concatenate([vit_y, audio_tok[None]], axis=0)
        other = swap(both)
        low = jnp.where(my_core == 0, both, other)
        high = jnp.where(my_core == 0, other, both)
        both = jnp.concatenate([low, high], axis=1)

    with jax.named_scope("project"):
        zm = nx * rows_m
        merge_w = weights[:, :zm].reshape(nz, nx, rows_m, columns)
        audio_w = weights[:, zm:].reshape(nz, nx, rows_a, columns)
        order = jnp.array([0, 1, 3, 2], jnp.int32)
        slot = order[jnp.mod(my_x - jnp.arange(nx), nx)]
        merge_w = jnp.transpose(merge_w[:, slot], (1, 0, 2, 3)).reshape(-1, columns)
        audio_w = jnp.transpose(audio_w[:, slot], (1, 0, 2, 3)).reshape(-1, columns)
        merged = jnp.transpose(both[:4], (1, 0, 2)).reshape(tokens, -1)
        video_rows = dot(merged, merge_w).astype(BF)
        audio_rows = dot(both[4], audio_w).astype(BF)

    with jax.named_scope("place"):
        seq_count = text_rows.shape[0]
        video_where = jnp.mod(position - starts, owners)
        video_place = jnp.where(
            video_where < video_count, (starts + video_where) // owners, seq_count
        )
        audio_where = jnp.mod(position - starts - video_count, owners)
        audio_place = jnp.where(
            audio_where < audio_count, (starts + video_count + audio_where) // owners, seq_count
        )
        slot_rows = jnp.concatenate([video_place, audio_place])
        media = jnp.concatenate([video_rows, audio_rows], axis=0)
        sequence_rows = text_rows[:, 0, :].at[slot_rows].set(media, mode="drop")
    return sequence_rows[:, None, :]


def solution(mesh):
    grid = Mesh(mesh.devices.reshape(4, 16, 4, 2), ("x", "z", "y", "core"))
    placed = (
        P(TM, None),
        P(None, MP),
        P(TM, MP),
        P(None, MP),
        P(MP, None),
        P(TM, MP),
        P(TM, MP),
        P(None, TM, MP),
        P(),
        P(),
        P(),
        P(),
    )
    return jax.shard_map(
        local, mesh=grid, in_specs=placed, out_specs=P(None, TM, MP), check_vma=False
    )
```

time: 474 us -> 234 us (0.49); the launches traced: 465 us -> 233 us
  waiting for transfers between devices: 373 us -> 39.2 us
  starting transfers between devices: 12.5 us -> 63.4 us
  local copies, waits for them, and re-layouts: 28.1 us -> 59.3 us
  blocking collectives: 13.8 us -> 25.7 us
  matrix products: 15.6 us -> 21 us
    all_gather x3 -> x1, waiting for transfers between devices: 266 us -> 0.01 us  [local(): weights = lax.all_gather(block, 'z', axis=0, tiled=False)]
    psum x1 -> x0, waiting for transfers between devices: 88.6 us -> none  [local(): summed = lax.psum(partial_value, 'mp')]
    ppermute x1 -> x9, starting transfers between devices: 3.15 us -> 38.3 us  [the longest x5 24 us: local(): swap = lambda v: lax.ppermute(v, 'core', [(0, 1), (1, 0)])]
    all_to_all x1 -> x3, waiting for transfers between devices: 16.7 us -> 36.8 us  [the longest x1 14.5 us: local(): lax.all_to_all(video_send, TM, 0, 0, tiled=True).reshape(tokens, -1)]
    all_to_all x1 -> x3, starting transfers between devices: 9.27 us -> 25.1 us  [the longest x1 16.7 us: local(): lax.all_to_all(audio_send, TM, 0, 0, tiled=True).reshape(tokens, -1)]
    gather x4 -> x6, local copies, waits for them, and re-layouts: 2.25 us -> 14.6 us  [the longest x2 6.23 us: local(): audio_w = jnp.transpose(audio_w[:, slot], (1, 0, 2, 3)).reshape(-1, columns)]
    all_gather x1 -> x2, blocking collectives: 13.8 us -> 25.7 us  [the longest x1 13.6 us: local(): video_y = lax.all_gather(video_pair, 'y', axis=0, tiled=False)]
    reshape x3 -> x13, local copies, waits for them, and re-layouts: 4.57 us -> 11 us  [the longest x1 3.47 us: local(): audio_w = jnp.transpose(audio_w[:, slot], (1, 0, 2, 3)).reshape(-1, columns)]
  transfers between devices with their start and end apart: 6 -> 13, of which waited for: 5 -> 5; matrix products, arithmetic and copies ran while one was open for 9% -> 24% of each run, Pallas kernels for 0% -> 0%
where the time goes in v1:
time: 234 us; the launch traced here: 233 us
  starting transfers between devices  63.4 us (27%)
  local copies, waits for them, and re-layouts  59.3 us (25%)
  waiting for transfers between devices  39.2 us (17%)
  blocking collectives  25.7 us (11%)
  matrix products  21 us (9%)
  between operations  14 us (6%)
  other arithmetic  9.89 us (4%)
    ppermute x5, starting transfers between devices, local(): swap = lambda v: lax.ppermute(v, 'core', [(0, 1), (1, 0)])  24 us
    dot_general x6, matrix products, dot(): return jnp.dot(a, b, preferred_element_type=F32)  21 us
    all_to_all x1, starting transfers between devices, local(): lax.all_to_all(audio_send, TM, 0, 0, tiled=True).reshape(tokens, -1)  16.7 us
    all_to_all x1, waiting for transfers between devices, local(): lax.all_to_all(video_send, TM, 0, 0, tiled=True).reshape(tokens, -1)  14.5 us
    all_gather x1, blocking collectives, local(): video_y = lax.all_gather(video_pair, 'y', axis=0, tiled=False)  13.6 us
    all_gather x1, blocking collectives, local(): vit_y = lax.all_gather(vit_out, 'y', axis=0, tiled=False)  12.2 us
    all_to_all x1, waiting for transfers between devices, local(): incoming = lax.all_to_all(outgoing, 'y', 0, 0, tiled=True)  11.3 us
    all_to_all x1, waiting for transfers between devices, local(): lax.all_to_all(audio_send, TM, 0, 0, tiled=True).reshape(tokens, -1)  11 us
  transfers between devices with their start and end apart: 13, of which 5 were waited for; matrix products, arithmetic and copies ran while one was open for 24% of the time, Pallas kernels for 0%

profile of v1, /device:TPU:1, one launch (start us, length us, event | category | flops | bytes accessed | tf_op | source)
XLA Modules:
  0.0 232.5 jit_solution(16097762287224131770)
XLA Ops:
  8.2 5.5 %collective-permute-start.8 = (bf16[100,448]{1,0:T(8,128)(2,1)S(1)}, bf16[100,448]{1,0:T(8,128)(2,1)S(1)}, u32[]{:S(2)}, u32[]{:S(2)}) collective-permute-start(bf16[100,448]{1,0:T(8,128)(2,1)S(1)} %constant_dynamic-update-slice_fusion.2), channel_id=1, source_target_pairs={{0,256},{128,384},{256,0},{384,128},{1,257},{129,385},{257,1},{385... | collective-permute-start | bytes 268808 | tf_op jit(solution)/shard_map/weights_x/ppermute | solution.py:22
  13.7 2.8 %collective-permute-start.7 = (bf16[100,448]{1,0:T(8,128)(2,1)S(1)}, bf16[100,448]{1,0:T(8,128)(2,1)S(1)}, u32[]{:S(2)}, u32[]{:S(2)}) collective-permute-start(bf16[100,448]{1,0:T(8,128)(2,1)S(1)} %constant_dynamic-update-slice_fusion.2), channel_id=1, source_target_pairs={{0,384},{128,0},{256,128},{384,256},{1,385},{129,1},{257,129},{385... | collective-permute-start | bytes 268808 | tf_op jit(solution)/shard_map/weights_x/ppermute | solution.py:22
  16.5 2.5 %collective-permute-start.6 = (bf16[100,448]{1,0:T(8,128)(2,1)S(1)}, bf16[100,448]{1,0:T(8,128)(2,1)S(1)}, u32[]{:S(2)}, u32[]{:S(2)}) collective-permute-start(bf16[100,448]{1,0:T(8,128)(2,1)S(1)} %constant_dynamic-update-slice_fusion.2), channel_id=1, source_target_pairs={{0,128},{128,256},{256,384},{384,0},{1,129},{129,257},{257,385},{3... | collective-permute-start | bytes 268808 | tf_op jit(solution)/shard_map/weights_x/ppermute | solution.py:22
  19.7 3.5 %collective-permute-start.3 = (bf16[1,128]{1,0:T(2,128)(2,1)S(1)}, bf16[1,128]{1,0:T(2,128)(2,1)S(1)}, u32[]{:S(2)}, u32[]{:S(2)}) collective-permute-start(bf16[1,128]{1,0:T(2,128)(2,1)S(1)} %slice.54), channel_id=1, source_target_pairs={{0,8},{8,16},{16,24},{24,32},{32,40},{40,48},{48,56},{56,64},{64,7... | collective-permute-start | bytes 776 | tf_op jit(solution)/shard_map/audio_conv/ppermute | solution.py:82
  29.8 6.6 %concatenate.71 = bf16[400,448]{1,0:T(8,128)(2,1)} concatenate(bf16[80,448]{1,0:T(8,128)(2,1)S(1)} %copy-done.6, bf16[80,448]{1,0:T(8,128)(2,1)S(1)} %slice.87, bf16[80,448]{1,0:T(8,128)(2,1)S(1)} %slice.88, bf16[80,448]{1,0:T(8,128)(2,1)S(1)} %slice.89, bf16[20,448]{1,0:T(8,128)(2,1)S(1)} %copy-done.8, bf16[20,448]{1,0:T(8,128)(2,1)S(1)} %slice.90, bf16[20,448]{1,0:T(8,128)(2,1)S(1)} %slice.91, ...), dimensions={0} | concatenate | bytes 716800 | tf_op jit(solution)/shard_map/weights_x/concatenate | solution.py:64
  39.0 16.7 %all-to-all-start.1 = ((bf16[64,2,240]{2,1,0:T(2,128)(2,1)}), bf16[64,2,240]{2,1,0:T(2,128)(2,1)S(1)}, u32[]{:S(2)}, u32[]{:S(2)}) async-start(bf16[64,2,240]{2,1,0:T(2,128)(2,1)} %reshape.478), calls=%async_computation.1 | async-start | bytes 131072 | tf_op jit(solution)/shard_map/audio_conv/all_to_all | solution.py:91
  58.3 11.0 %all-to-all-done.1 = bf16[64,2,240]{2,1,0:T(2,128)(2,1)S(1)} async-done(((bf16[64,2,240]{2,1,0:T(2,128)(2,1)}), bf16[64,2,240]{2,1,0:T(2,128)(2,1)S(1)}, u32[]{:S(2)}, u32[]{:S(2)}) %all-to-all-start.1) | async-done | bytes 61472 | tf_op jit(solution)/shard_map/audio_conv/all_to_all | solution.py:91
  69.2 4.6 %all-to-all-start = ((bf16[64,3,640]{2,1,0:T(4,128)(2,1)}), bf16[64,3,640]{2,1,0:T(4,128)(2,1)S(1)}, u32[]{:S(2)}, u32[]{:S(2)}) async-start(bf16[64,3,640]{2,1,0:T(4,128)(2,1)} %reshape.409), calls=%async_computation | async-start | bytes 655360 | tf_op jit(solution)/shard_map/route/all_to_all | solution.py:78
  73.9 5.3 %collective-permute-start.1 = (bf16[1280,640]{1,0:T(8,128)(2,1)}, bf16[1280,640]{1,0:T(8,128)(2,1)}, u32[]{:S(2)}, u32[]{:S(2)}) collective-permute-start(bf16[1280,640]{1,0:T(8,128)(2,1)} %param.16), channel_id=1, source_target_pairs={{0,1},{1,0},{2,3},{3,2},{4,5},{5,4},{6,7},{7,6},{8,9},{9,8},{10,11... | collective-permute-start | bytes 4915208 | tf_op jit(solution)/shard_map/core_swap/ppermute | solution.py:94
  79.2 1.9 collective-permute-start.2
  81.4 2.4 %collective-permute-start.4 = (bf16[96,160]{1,0:T(8,128)(2,1)S(1)}, bf16[96,160]{1,0:T(8,128)(2,1)S(1)}, u32[]{:S(2)}, u32[]{:S(2)}) collective-permute-start(bf16[96,160]{1,0:T(8,128)(2,1)S(1)} %constant_dynamic-slice_fusion), channel_id=1, source_target_pairs={{0,1},{1,0},{2,3},{3,2},{4,5},{5,4},{6,7},{7,6},{8,9},{9,8},{10,11... | collective-permute-start | bytes 92168 | tf_op jit(solution)/shard_map/core_swap/ppermute | solution.py:94
  83.8 14.5 %all-to-all-done = bf16[64,3,640]{2,1,0:T(4,128)(2,1)S(1)} async-done(((bf16[64,3,640]{2,1,0:T(4,128)(2,1)}), bf16[64,3,640]{2,1,0:T(4,128)(2,1)S(1)}, u32[]{:S(2)}, u32[]{:S(2)}) %all-to-all-start) | async-done | bytes 245792 | tf_op jit(solution)/shard_map/route/all_to_all | solution.py:78
  98.6 7.4 %collective-permute-start = (bf16[96,640]{1,0:T(8,128)(2,1)S(1)}, bf16[96,640]{1,0:T(8,128)(2,1)S(1)}, u32[]{:S(2)}, u32[]{:S(2)}) collective-permute-start(bf16[96,640]{1,0:T(8,128)(2,1)S(1)} %constant_dynamic-slice_fusion.1), channel_id=1, source_target_pairs={{0,1},{1,0},{2,3},{3,2},{4,5},{5,4},{6,7},{7,6},{8,9},{9,8},{10,11... | collective-permute-start | bytes 368648 | tf_op jit(solution)/shard_map/core_swap/ppermute | solution.py:94
  107.6 13.6 %all_gather.13 = bf16[4,96,1280]{2,1,0:T(8,128)(2,1)S(1)} all-gather(bf16[1,96,1280]{2,1,0:T(8,128)(2,1)S(1)} %copy.67), channel_id=1, replica_groups=mesh['x'=4,'z'=16,'y'=4,'core'=2] {'y'}, dimensions={0}, use_global_device_ids=true | all-gather | bytes 1228800 | tf_op jit(solution)/shard_map/gather_y/all_gather | solution.py:110
  124.7 3.0 %copy.69 = f32[4,96,4,320]{3,2,1,0:T(4,128)} copy(f32[4,96,4,320]{3,0,1,2:T(4,128)S(1)} %bitcast_convert_fusion) | data formatting | bytes 3932160 | tf_op jit(solution)/shard_map/vision/convert_element_type | solution.py:115
  127.7 2.7 %reshape.425 = f32[384,1280]{1,0:T(8,128)S(1)} reshape(f32[4,96,4,320]{3,2,1,0:T(4,128)} %copy.69) | data formatting | bytes 3932160 | tf_op jit(solution)/shard_map/vision/convert_element_type | solution.py:115
  130.4 7.0 %fusion.24 = f32[384,1280]{1,0:T(8,128)} fusion(bf16[640,1280]{1,0:T(8,128)(2,1)} %param.17, bf16[1280,640]{1,0:T(8,128)(2,1)} %param.16, f32[384,1280]{1,0:T(8,128)S(1)} %reshape.425, f32[384]{0:T(512)S(1)} %rsqrt.12, f32[384]{0:T(512)S(1)} %div.36), kind=kOutput, calls=%fused_computation.59 | convolution fusion | flops 1275740160 | bytes 7212032 | tf_op jit(solution)/shard_map/vision/dot_general | solution.py:34
  137.5 7.4 %fusion = bf16[384,1280]{1,0:T(8,128)(2,1)} fusion(f32[384,1280]{1,0:T(8,128)} %fusion.24, bf16[640,1280]{1,0:T(8,128)(2,1)} %collective-permute-done.2, bf16[1280,640]{1,0:T(8,128)(2,1)} %collective-permute-done.1, f32[384,1280]{1,0:T(8,128)S(1)} %reshape.425, f32[384]{0:T(512)S(1)} %rsqrt.12, f32[384]{0:T(512)S(1)} %div.36), kind=kOutput, calls=%fused_computation.7 | convolution fusion | flops 1276723200 | bytes 8195072 | tf_op jit(solution)/shard_map/vision/dot_general | solution.py:34
  144.9 2.4 %pad_maximum_fusion = bf16[4,128,1280]{2,1,0:T(8,128)(2,1)} fusion(bf16[4,32,1280]{2,1,0:T(8,128)(2,1)S(1)} %broadcast_in_dim.9, bf16[4,96,1280]{2,1,0:T(8,128)(2,1)} %bitcast.64), kind=kLoop, calls=%fused_computation.17 | loop fusion | flops 2621440 | bytes 2621440 | tf_op jit(solution)/shard_map/sum_y/concatenate | solution.py:132
  147.2 3.8 %all-to-all-start.2 = ((bf16[4,128,1280]{2,1,0:T(8,128)(2,1)}), bf16[4,128,1280]{2,1,0:T(8,128)(2,1)S(1)}, u32[]{:S(2)}, u32[]{:S(2)}) async-start(bf16[4,128,1280]{2,1,0:T(8,128)(2,1)} %pad_maximum_fusion), calls=%async_computation.2 | async-start | bytes 2621440 | tf_op jit(solution)/shard_map/sum_y/all_to_all | solution.py:133
  151.0 2.0 copy.68
  153.0 2.1 reshape.413
  155.1 11.3 %all-to-all-done.2 = bf16[4,128,1280]{2,1,0:T(8,128)(2,1)S(1)} async-done(((bf16[4,128,1280]{2,1,0:T(8,128)(2,1)}), bf16[4,128,1280]{2,1,0:T(8,128)(2,1)S(1)}, u32[]{:S(2)}, u32[]{:S(2)}) %all-to-all-start.2) | async-done | bytes 1310752 | tf_op jit(solution)/shard_map/sum_y/all_to_all | solution.py:133
  167.4 12.2 %all_gather.14 = bf16[4,96,1280]{2,1,0:T(8,128)(2,1)S(1)} all-gather(bf16[1,96,1280]{2,1,0:T(8,128)(2,1)S(1)} %fusion.29), channel_id=1, replica_groups=mesh['x'=4,'z'=16,'y'=4,'core'=2] {'y'}, dimensions={0}, use_global_device_ids=true | all-gather | bytes 1228800 | tf_op jit(solution)/shard_map/gather_vit/all_gather | solution.py:141
  179.7 7.0 %collective-permute-start.5 = (bf16[5,96,1280]{2,1,0:T(8,128)(2,1)S(1)}, bf16[5,96,1280]{2,1,0:T(8,128)(2,1)}, u32[]{:S(2)}, u32[]{:S(2)}) collective-permute-start(bf16[5,96,1280]{2,1,0:T(8,128)(2,1)S(1)} %constant_dynamic-update-slice_fusion), channel_id=1, source_target_pairs={{0,1},{1,0},{2,3},{3,2},{4,5},{5,4},{6,7},{7,6},{8,9},{9,8},{10,11... | collective-permute-start | bytes 3686408 | tf_op jit(solution)/shard_map/gather_vit/ppermute | solution.py:94
  194.3 5.3 %slice.93 = bf16[16,320,448]{2,1,0:T(8,128)(2,1)} slice(bf16[16,400,448]{2,1,0:T(8,128)(2,1)} %bitcast.56), slice={[0:16], [0:320], [0:448]} | slice | bytes 9175040 | tf_op jit(solution)/shard_map/project/slice | solution.py:150
  201.4 5.7 %gather_fusion.3 = bf16[4,16,80,448]{3,2,1,0:T(8,128)(2,1)} fusion(bf16[16,4,80,448]{3,2,1,0:T(8,128)(2,1)} %bitcast.54, s32[1024]{0:T(1024)S(1)} %pad_clamp_fusion), kind=kCustom, calls=%fused_computation.3 | custom fusion | bytes 9175056 | tf_op jit(solution)/shard_map/project/gather | solution.py:154
  207.1 3.0 %gather_fusion.4 = bf16[4,16,20,448]{3,1,2,0:T(8,128)(2,1)} fusion(bf16[16,4,20,448]{3,0,2,1:T(8,128)(2,1)} %bitcast.57, s32[1024]{0:T(1024)S(1)} %pad_clamp_fusion), kind=kCustom, calls=%fused_computation.4 | custom fusion | bytes 2293776 | tf_op jit(solution)/shard_map/project/gather | solution.py:155
  210.1 3.2 %copy.76 = bf16[4,16,20,448]{3,2,1,0:T(8,128)(2,1)} copy(bf16[4,16,20,448]{3,1,2,0:T(8,128)(2,1)} %gather_fusion.4) | data formatting | bytes 2293760 | tf_op jit(solution)/shard_map/project/gather | solution.py:155
  213.3 3.5 %reshape.424 = bf16[1280,448]{1,0:T(8,128)(2,1)} reshape(bf16[4,16,20,448]{3,2,1,0:T(8,128)(2,1)} %copy.76) | data formatting | bytes 2293760 | tf_op jit(solution)/shard_map/project/reshape | solution.py:155
  218.8 3.7 %convolution_convert_fusion.1 = bf16[192,448]{1,0:T(8,128)(2,1)S(1)} fusion(bf16[192,5120]{1,0:T(8,128)(2,1)S(1)} %bitcast.61, bf16[5120,448]{1,0:T(8,128)(2,1)} %bitcast.58), kind=kOutput, calls=%fused_computation.22 | convolution fusion | flops 880889856 | bytes 6725632 | tf_op jit(solution)/shard_map/project/dot_general | solution.py:34
  222.5 2.2 scatter_custom_fusion
  (120 shorter events, 32.8 us)
Async XLA Ops:
  6.5 22.9 %copy-start = (bf16[384,160]{0,1:T(8,128)(2,1)S(1)}, bf16[384,160]{0,1:T(8,128)(2,1)}, u32[]{:S(2)}) copy-start(bf16[384,160]{0,1:T(8,128)(2,1)} %param.14) | copy-start | bytes 368644
  6.5 23.2 %copy-start.6 = (bf16[80,448]{1,0:T(8,128)(2,1)S(1)}, bf16[80,448]{1,0:T(8,128)(2,1)}, u32[]{:S(2)}) copy-start(bf16[80,448]{1,0:T(8,128)(2,1)} %param.19) | copy-start | bytes 215044
  6.5 23.2 %copy-start.8 = (bf16[20,448]{1,0:T(8,128)(2,1)S(1)}, bf16[20,448]{1,0:T(8,128)(2,1)}, u32[]{:S(2)}) copy-start(bf16[20,448]{1,0:T(8,128)(2,1)} %param.18) | copy-start | bytes 53764
  6.5 186.4 %all-gather.3.cloned.1.call-start = ((), (), s32[]{:S(2)}) async-start(), calls=%async_computation.3 | async-start | bytes 6963200 | tf_op jit(solution)/shard_map/weights_z/all_gather | solution.py:66
  8.2 21.4 %collective-permute-start.8 = (bf16[100,448]{1,0:T(8,128)(2,1)S(1)}, bf16[100,448]{1,0:T(8,128)(2,1)S(1)}, u32[]{:S(2)}, u32[]{:S(2)}) collective-permute-start(bf16[100,448]{1,0:T(8,128)(2,1)S(1)} %constant_dynamic-update-slice_fusion.2), channel_id=1, source_target_pairs={{0,256},{128,384},{256,0},{384,128},{1,257},{129,385},{257,1},{385... | collective-permute-start | bytes 268808 | tf_op jit(solution)/shard_map/weights_x/ppermute | solution.py:22
  13.7 15.9 %collective-permute-start.7 = (bf16[100,448]{1,0:T(8,128)(2,1)S(1)}, bf16[100,448]{1,0:T(8,128)(2,1)S(1)}, u32[]{:S(2)}, u32[]{:S(2)}) collective-permute-start(bf16[100,448]{1,0:T(8,128)(2,1)S(1)} %constant_dynamic-update-slice_fusion.2), channel_id=1, source_target_pairs={{0,384},{128,0},{256,128},{384,256},{1,385},{129,1},{257,129},{385... | collective-permute-start | bytes 268808 | tf_op jit(solution)/shard_map/weights_x/ppermute | solution.py:22
  16.5 13.2 %collective-permute-start.6 = (bf16[100,448]{1,0:T(8,128)(2,1)S(1)}, bf16[100,448]{1,0:T(8,128)(2,1)S(1)}, u32[]{:S(2)}, u32[]{:S(2)}) collective-permute-start(bf16[100,448]{1,0:T(8,128)(2,1)S(1)} %constant_dynamic-update-slice_fusion.2), channel_id=1, source_target_pairs={{0,128},{128,256},{256,384},{384,0},{1,129},{129,257},{257,385},{3... | collective-permute-start | bytes 268808 | tf_op jit(solution)/shard_map/weights_x/ppermute | solution.py:22
  19.7 16.7 %collective-permute-start.3 = (bf16[1,128]{1,0:T(2,128)(2,1)S(1)}, bf16[1,128]{1,0:T(2,128)(2,1)S(1)}, u32[]{:S(2)}, u32[]{:S(2)}) collective-permute-start(bf16[1,128]{1,0:T(2,128)(2,1)S(1)} %slice.54), channel_id=1, source_target_pairs={{0,8},{8,16},{16,24},{24,32},{32,40},{40,48},{48,56},{56,64},{64,7... | collective-permute-start | bytes 776 | tf_op jit(solution)/shard_map/audio_conv/ppermute | solution.py:82
  36.4 19.3 %copy-start.7 = (bf16[768,160]{0,1:T(8,128)(2,1)S(1)}, bf16[768,160]{0,1:T(8,128)(2,1)}, u32[]{:S(2)}) copy-start(bf16[768,160]{0,1:T(8,128)(2,1)} %param.15) | copy-start | bytes 737284
  39.0 30.2 %all-to-all-start.1 = ((bf16[64,2,240]{2,1,0:T(2,128)(2,1)}), bf16[64,2,240]{2,1,0:T(2,128)(2,1)S(1)}, u32[]{:S(2)}, u32[]{:S(2)}) async-start(bf16[64,2,240]{2,1,0:T(2,128)(2,1)} %reshape.478), calls=%async_computation.1 | async-start | bytes 131072 | tf_op jit(solution)/shard_map/audio_conv/all_to_all | solution.py:91
  69.2 29.1 %all-to-all-start = ((bf16[64,3,640]{2,1,0:T(4,128)(2,1)}), bf16[64,3,640]{2,1,0:T(4,128)(2,1)S(1)}, u32[]{:S(2)}, u32[]{:S(2)}) async-start(bf16[64,3,640]{2,1,0:T(4,128)(2,1)} %reshape.409), calls=%async_computation | async-start | bytes 655360 | tf_op jit(solution)/shard_map/route/all_to_all | solution.py:78
  73.9 63.6 %collective-permute-start.1 = (bf16[1280,640]{1,0:T(8,128)(2,1)}, bf16[1280,640]{1,0:T(8,128)(2,1)}, u32[]{:S(2)}, u32[]{:S(2)}) collective-permute-start(bf16[1280,640]{1,0:T(8,128)(2,1)} %param.16), channel_id=1, source_target_pairs={{0,1},{1,0},{2,3},{3,2},{4,5},{5,4},{6,7},{7,6},{8,9},{9,8},{10,11... | collective-permute-start | bytes 4915208 | tf_op jit(solution)/shard_map/core_swap/ppermute | solution.py:94
  79.2 58.3 %collective-permute-start.2 = (bf16[640,1280]{1,0:T(8,128)(2,1)}, bf16[640,1280]{1,0:T(8,128)(2,1)}, u32[]{:S(2)}, u32[]{:S(2)}) collective-permute-start(bf16[640,1280]{1,0:T(8,128)(2,1)} %param.17), channel_id=1, source_target_pairs={{0,1},{1,0},{2,3},{3,2},{4,5},{5,4},{6,7},{7,6},{8,9},{9,8},{10,11... | collective-permute-start | bytes 4915208 | tf_op jit(solution)/shard_map/core_swap/ppermute | solution.py:94
  81.4 24.6 %collective-permute-start.4 = (bf16[96,160]{1,0:T(8,128)(2,1)S(1)}, bf16[96,160]{1,0:T(8,128)(2,1)S(1)}, u32[]{:S(2)}, u32[]{:S(2)}) collective-permute-start(bf16[96,160]{1,0:T(8,128)(2,1)S(1)} %constant_dynamic-slice_fusion), channel_id=1, source_target_pairs={{0,1},{1,0},{2,3},{3,2},{4,5},{5,4},{6,7},{7,6},{8,9},{9,8},{10,11... | collective-permute-start | bytes 92168 | tf_op jit(solution)/shard_map/core_swap/ppermute | solution.py:94
  98.6 8.3 %collective-permute-start = (bf16[96,640]{1,0:T(8,128)(2,1)S(1)}, bf16[96,640]{1,0:T(8,128)(2,1)S(1)}, u32[]{:S(2)}, u32[]{:S(2)}) collective-permute-start(bf16[96,640]{1,0:T(8,128)(2,1)S(1)} %constant_dynamic-slice_fusion.1), channel_id=1, source_target_pairs={{0,1},{1,0},{2,3},{3,2},{4,5},{5,4},{6,7},{7,6},{8,9},{9,8},{10,11... | collective-permute-start | bytes 368648 | tf_op jit(solution)/shard_map/core_swap/ppermute | solution.py:94
  147.2 19.2 %all-to-all-start.2 = ((bf16[4,128,1280]{2,1,0:T(8,128)(2,1)}), bf16[4,128,1280]{2,1,0:T(8,128)(2,1)S(1)}, u32[]{:S(2)}, u32[]{:S(2)}) async-start(bf16[4,128,1280]{2,1,0:T(8,128)(2,1)} %pad_maximum_fusion), calls=%async_computation.2 | async-start | bytes 2621440 | tf_op jit(solution)/shard_map/sum_y/all_to_all | solution.py:133
  167.4 19.3 %copy-start.5 = (bf16[512,1,448]{0,2,1:T(8,128)(2,1)S(1)}, bf16[512,1,448]{0,2,1:T(8,128)(2,1)}, u32[]{:S(2)}) copy-start(bf16[512,1,448]{0,2,1:T(8,128)(2,1)} %param.20) | copy-start | bytes 1376260
  179.6 7.3 %copy-start.2 = (s32[4]{0:T(128)S(1)}, s32[4]{0:T(128)}, u32[]{:S(2)}) copy-start(s32[4]{0:T(128)} %constant.214.clone) | copy-start | bytes 52
  179.6 8.0 %copy-start.9 = (s32[192]{0:T(256)S(1)}, s32[192]{0:T(256)}, u32[]{:S(2)}) copy-start(s32[192]{0:T(256)} %param.24) | copy-start | bytes 2308
  179.6 8.0 %copy-start.10 = (s32[192]{0:T(256)S(1)}, s32[192]{0:T(256)}, u32[]{:S(2)}) copy-start(s32[192]{0:T(256)} %param.23) | copy-start | bytes 2308
  179.7 8.0 %copy-start.3 = (bf16[5,96,1280]{2,1,0:T(8,128)(2,1)}, bf16[5,96,1280]{2,1,0:T(8,128)(2,1)S(1)}, u32[]{:S(2)}) copy-start(bf16[5,96,1280]{2,1,0:T(8,128)(2,1)S(1)} %constant_dynamic-update-slice_fusion) | copy-start | bytes 3686404
  179.7 9.6 %collective-permute-start.5 = (bf16[5,96,1280]{2,1,0:T(8,128)(2,1)S(1)}, bf16[5,96,1280]{2,1,0:T(8,128)(2,1)}, u32[]{:S(2)}, u32[]{:S(2)}) collective-permute-start(bf16[5,96,1280]{2,1,0:T(8,128)(2,1)S(1)} %constant_dynamic-update-slice_fusion), channel_id=1, source_target_pairs={{0,1},{1,0},{2,3},{3,2},{4,5},{5,4},{6,7},{7,6},{8,9},{9,8},{10,11... | collective-permute-start | bytes 3686408 | tf_op jit(solution)/shard_map/gather_vit/ppermute | solution.py:94
  216.8 1.9 copy-start.4
  218.8 6.9 %copy-start.1 = (bf16[384,160]{0,1:T(8,128)(2,1)S(1)}, bf16[384,160]{0,1:T(8,128)(2,1)}, u32[]{:S(2)}) copy-start(bf16[384,160]{0,1:T(8,128)(2,1)} %param.14) | copy-start | bytes 368644
Sparse Core Ops, SparseCore 0:
  36.5 106.7 all-gather.2

commit v2 on v0

v2 whole, which is shorter than its diff:
```python
import jax
import jax.numpy as jnp
from jax import lax
from jax.experimental import pallas as pl
from jax.experimental.pallas import tpu as pltpu
from jax.sharding import Mesh, PartitionSpec as P

AT = 50
VT = 64
BF = jnp.bfloat16
F32 = jnp.float32
I32 = jnp.int32
TM = ("x", "z")
MP = ("y", "core")
PAD_A = 32
VMEM = pl.BlockSpec(memory_space=pltpu.VMEM)
SMEM = pl.BlockSpec(memory_space=pltpu.SMEM)
ANY = pl.BlockSpec(memory_space=pl.ANY)
ROOT_HALF = 0.7071067811865476


def span_starts(span_order, offsets):
    listed = jnp.arange(span_order.shape[0], dtype=I32)
    matches = (span_order[:, None] == listed[None, :]).astype(I32)
    return jnp.sum(matches * offsets[:, None], axis=0)


def ring(value, axis, step):
    count = lax.axis_size(axis)
    return lax.ppermute(value, axis, [(i, (i + step) % count) for i in range(count)])


def swap(value):
    return lax.ppermute(value, "core", [(0, 1), (1, 0)])


def gelu(value):
    return 0.5 * value * (1.0 + lax.erf(value * ROOT_HALF))


def dot(a, b):
    return jnp.dot(a, b, preferred_element_type=F32)


def dot_nt(a, b):
    return lax.dot_general(a, b, (((1,), (1,)), ((), ())), preferred_element_type=F32)


def iota(shape, axis):
    return lax.broadcasted_iota(I32, shape, axis)


def params(mib=48):
    return pltpu.CompilerParams(vmem_limit_bytes=mib * 1024 * 1024)


def one_hot(condition):
    return jnp.where(condition, 1.0, 0.0).astype(BF)


def prep_kernel(first_ref, audio_ref, patch_ref, mel_ref, rim_ref, conv_ref, out_ref):
    rows, width = out_ref.shape
    spans, count = 3, patch_ref.shape[1]
    block = patch_ref.shape[0]
    patch = patch_ref[...]
    row = iota((rows, 1), 0)
    owner, kind = row >> 2, row & 3
    start = jnp.where(kind == 0, first_ref[0], jnp.where(kind == 1, first_ref[1], first_ref[2]))
    token = (kind << 6) + ((owner - start) & (VT - 1))
    target = jnp.where(kind < spans, token * 4, -8)
    column = iota((rows, count), 1)
    source = iota((block, width), 0)
    place = iota((block, width), 1)
    total = jnp.zeros((rows, width), F32)
    for s in range(4):
        picked = dot_nt(one_hot(column == target + s), patch).astype(BF)
        total += dot(picked, one_hot(place == source + s * block))

    frames = mel_ref.shape[0]
    f0, f1, f2, f3 = (mel_ref[:, k * 128 : (k + 1) * 128] for k in range(4))
    behind = one_hot(iota((frames, frames), 1) == iota((frames, frames), 0) - 1)
    first_row = iota((frames, 1), 0) == 0
    before = dot(behind, f3) + jnp.where(first_row, rim_ref[...].astype(F32), 0.0)
    before = before.astype(BF)
    c0, c1, c2 = (conv_ref[k * 128 : (k + 1) * 128, :] for k in range(3))
    even = dot(before, c0) + dot(f0, c1) + dot(f1, c2)
    odd = dot(f1, c0) + dot(f2, c1) + dot(f3, c2)
    pooled = (0.5 * (gelu(even) + gelu(odd))).astype(BF)
    column = iota((rows, frames), 1)
    for i in range(spans):
        index = jnp.minimum((owner - audio_ref[i]) & (VT - 1), AT - 1) + i * AT
        index = jnp.where(kind == spans, index, -8)
        picked = dot(one_hot(column == index), pooled).astype(BF)
        total += dot(picked, one_hot(place == source + i * block))
    out_ref[...] = total.astype(BF)


def vision_kernel(
    index_ref, video_ref, up0, down0, up1, down1, send_ref, rest_ref, xs, wu, wd, sems
):
    copies = []
    for i, (u, d) in enumerate(((up0, down0), (up1, down1))):
        copies.append(pltpu.make_async_copy(u, wu.at[i], sems.at[2 * i]))
        copies.append(pltpu.make_async_copy(d, wd.at[i], sems.at[2 * i + 1]))
    for copy in copies:
        copy.start()
    my_y = index_ref[0]
    ny, cores, half, width = video_ref.shape
    block = width // 4
    for y in range(ny):
        for c in range(cores):
            for s in range(4):
                a, b = (y * cores + c) * block, s * block
                xs[s * half : (s + 1) * half, a : a + block] = video_ref[y, c, :, b : b + block]
    wide = xs[...].astype(F32)
    centred = wide - jnp.mean(wide, axis=1, keepdims=True)
    spread = jnp.mean(centred * centred, axis=1, keepdims=True)
    normed = (centred * lax.rsqrt(spread + 1e-06)).astype(BF)
    total = None
    for i in range(2):
        copies[2 * i].wait()
        hidden = gelu(dot(normed, wu[i])).astype(BF)
        copies[2 * i + 1].wait()
        term = dot(hidden, wd[i])
        total = term if total is None else total + term
    total = total.astype(BF)
    for s in range(4):
        send_ref[s] = total[s * half : (s + 1) * half]
    begin = pl.multiple_of(my_y * half, half)
    rest_ref[...] = xs[pl.ds(begin, half), :]


def audio_kernel(index_ref, a_ref, b_ref, c_ref, d_ref, out_ref):
    my_y = index_ref[0]
    owners = a_ref.shape[0] // 2
    block = a_ref.shape[1] // 3
    source, place = iota((block, 256), 0), iota((block, 256), 1)
    group = place // PAD_A
    lane = place - group * PAD_A
    spread = one_hot((lane < 20) & (source == group * 20 + lane))
    for ref, far in ((a_ref, 0), (b_ref, 1), (c_ref, 3), (d_ref, 2)):
        y = (my_y - far) & 3
        for k in range(3):
            piece = dot(ref[:, k * block : (k + 1) * block], spread).astype(BF)
            for c in range(2):
                out_ref[y, k * owners : (k + 1) * owners, c * 256 : (c + 1) * 256] = piece[
                    c * owners : (c + 1) * owners
                ]


def tail_kernel(
    own_ref, other_ref, audio_ref, weight_ref, place_ref, text_ref, out_ref, video, audio
):
    step = pl.program_id(0)

    @pl.when(step == 0)
    def _():
        video[...] = jnp.zeros_like(video)
        audio[...] = jnp.zeros_like(audio)

    nz, _, rows, columns = weight_ref.shape
    rows_m = rows - PAD_A
    merge_w = weight_ref[:, 0, :rows_m, :].reshape(nz * rows_m, columns)
    audio_w = weight_ref[:, 0, rows_m:, :].reshape(nz * PAD_A, columns)
    both = jnp.concatenate([own_ref[0], other_ref[0]], axis=0)
    video[...] += dot(both, merge_w)
    audio[...] += dot(audio_ref[0], audio_w)

    @pl.when(step == 3)
    def _():
        media = jnp.concatenate([video[...], audio[...]], axis=0).astype(BF)
        count, length = media.shape[0], out_ref.shape[1]
        marks = one_hot(place_ref[...] == iota((length, count), 0))
        placed = lax.dot_general(
            media, marks, (((0,), (1,)), ((), ())), preferred_element_type=F32
        )
        taken = dot_nt(jnp.ones((8, count), BF), marks)[0:1, :]
        out_ref[...] = jnp.where(taken > 0.5, placed, text_ref[...].astype(F32)).astype(BF)


def local(
    mel_frames,
    conv_weight,
    patches,
    vit_up,
    vit_down,
    audio_proj,
    merger,
    text_rows,
    span_order,
    offsets,
    audio_count,
    video_count,
):
    nx, nz, ny = (lax.axis_size(a) for a in ("x", "z", "y"))
    owners = nx * nz
    position = lax.axis_index(TM)
    my_y, my_core = lax.axis_index("y"), lax.axis_index("core")
    spans = mel_frames.shape[0] // (4 * AT)
    tokens = spans * owners
    half, near = tokens // 2, owners // 2
    columns, rows_m, rows_a = merger.shape[1], merger.shape[0], audio_proj.shape[0]
    rows_w = rows_m + PAD_A
    width = 4 * patches.shape[1]
    full = vit_down.shape[1]

    rim = lax.ppermute(mel_frames[-1:], TM, [(i, i + 1) for i in range(owners - 1)])

    own = jnp.concatenate([merger, audio_proj, jnp.zeros((PAD_A - rows_a, columns), BF)], axis=0)
    block = lax.all_gather(own, "x", axis=0, tiled=False)
    weights = lax.all_gather(block, "z", axis=0, tiled=False)

    starts = span_starts(span_order, offsets)
    local_start = lax.dynamic_slice_in_dim(starts, position * spans, spans)
    local_video = lax.dynamic_slice_in_dim(video_count, position * spans, spans)
    outgoing = pl.pallas_call(
        prep_kernel,
        name="prep",
        out_shape=jax.ShapeDtypeStruct((owners * (spans + 1), width), BF),
        in_specs=[SMEM, SMEM, VMEM, VMEM, VMEM, VMEM],
        out_specs=VMEM,
        compiler_params=params(),
    )(
        local_start,
        local_start + local_video,
        patches.T,
        mel_frames.reshape(spans * AT, -1),
        rim,
        conv_weight,
    )
    arrived = lax.all_to_all(
        outgoing.reshape(owners, spans + 1, width), TM, 0, 0, tiled=True
    )

    up_other, down_other = swap(vit_up), swap(vit_down)
    cores = lax.all_gather(arrived, "core", axis=0, tiled=False)
    pair = lax.dynamic_slice_in_dim(cores, my_core * near, near, axis=1)[:, :, :spans]
    video_pair = jnp.transpose(pair, (0, 2, 1, 3)).reshape(2, half, width)
    video_y = lax.all_gather(video_pair, "y", axis=0, tiled=False)

    where_am_i = jnp.stack([my_y]).astype(I32)
    flops = 2 * 4 * half * full * 4 * vit_up.shape[1]
    partial_sum, residual = pl.pallas_call(
        vision_kernel,
        name="vision",
        out_shape=(
            jax.ShapeDtypeStruct((4, half, full), BF),
            jax.ShapeDtypeStruct((half, full), BF),
        ),
        in_specs=[SMEM, VMEM, ANY, ANY, ANY, ANY],
        out_specs=(VMEM, VMEM),
        scratch_shapes=[
            pltpu.VMEM((4 * half, full), BF),
            pltpu.VMEM((2,) + vit_up.shape, BF),
            pltpu.VMEM((2,) + vit_down.shape, BF),
            pltpu.SemaphoreType.DMA((4,)),
        ],
        compiler_params=params(),
        cost_estimate=pl.CostEstimate(flops=flops, bytes_accessed=9000000, transcendentals=500000),
    )(where_am_i, video_y, vit_up, vit_down, up_other, down_other)

    audio_own = cores[:, :, spans, : spans * patches.shape[1]].reshape(2 * owners, -1)
    audio_own, partial_sum = lax.optimization_barrier((audio_own, partial_sum))
    incoming = lax.all_to_all(partial_sum, "y", 0, 0, tiled=True)
    audio_y = [audio_own] + [ring(audio_own, "y", k) for k in (1, 3, 2)]
    audio_tokens = pl.pallas_call(
        audio_kernel,
        name="audio_spread",
        out_shape=jax.ShapeDtypeStruct((ny, tokens, nz * PAD_A), BF),
        in_specs=[SMEM] + [VMEM] * 4,
        out_specs=VMEM,
        compiler_params=params(),
    )(where_am_i, *audio_y)
    summed = jnp.sum(incoming.astype(F32), axis=0)
    vit_out = (residual.astype(F32) + summed).astype(BF)
    vit_out, audio_tokens = lax.optimization_barrier((vit_out, audio_tokens))
    vit_mine = lax.all_gather(vit_out, "y", axis=0, tiled=False)
    vit_theirs = swap(vit_mine)

    seq_count = text_rows.shape[0]
    video_where = jnp.mod(position - starts, owners)
    video_place = jnp.where(video_where < video_count, (starts + video_where) // owners, seq_count)
    audio_where = jnp.mod(position - starts - video_count, owners)
    audio_place = jnp.where(
        audio_where < audio_count, (starts + video_count + audio_where) // owners, seq_count
    )

    video_place = video_place.reshape(2, near, spans)
    video_place = jnp.where(my_core == 0, video_place, video_place[::-1])
    video_place = jnp.transpose(video_place, (0, 2, 1)).reshape(-1)
    audio_place = audio_place.reshape(owners, spans).T.reshape(-1)
    places = jnp.concatenate([video_place, audio_place])
    result = pl.pallas_call(
        tail_kernel,
        name="project_place",
        out_shape=jax.ShapeDtypeStruct((columns, seq_count), BF),
        grid_spec=pl.GridSpec(
            grid=(4,),
            in_specs=[
                pl.BlockSpec((1, half, full), lambda s: (s, 0, 0)),
                pl.BlockSpec((1, half, full), lambda s: (s, 0, 0)),
                pl.BlockSpec((1, tokens, nz * PAD_A), lambda s: (s, 0, 0)),
                pl.BlockSpec((nz, 1, rows_w, columns), lambda s: (0, s, 0, 0)),
                pl.BlockSpec((1, 2 * tokens), lambda s: (0, 0)),
                pl.BlockSpec((columns, seq_count), lambda s: (0, 0)),
            ],
            out_specs=pl.BlockSpec((columns, seq_count), lambda s: (0, 0)),
            scratch_shapes=[pltpu.VMEM((tokens, columns), F32), pltpu.VMEM((tokens, columns), F32)],
        ),
        compiler_params=params(),
        cost_estimate=pl.CostEstimate(flops=1100000000, bytes_accessed=9000000, transcendentals=0),
    )(
        vit_mine,
        vit_theirs,
        audio_tokens,
        weights.reshape(nz, nx, rows_w, columns),
        places.reshape(1, -1),
        text_rows[:, 0, :].T,
    )
    return result.T[:, None, :]


def solution(mesh):
    grid = Mesh(mesh.devices.reshape(4, 16, 4, 2), ("x", "z", "y", "core"))
    placed = (
        P(TM, None),
        P(None, MP),
        P(TM, MP),
        P(None, MP),
        P(MP, None),
        P(TM, MP),
        P(TM, MP),
        P(None, TM, MP),
        P(),
        P(),
        P(),
        P(),
    )
    return jax.shard_map(
        local, mesh=grid, in_specs=placed, out_specs=P(None, TM, MP), check_vma=False
    )
```

time: 474 us -> 157 us (0.33); the launches traced: 465 us -> 156 us
  waiting for transfers between devices: 373 us -> 22.6 us
  starting transfers between devices: 12.5 us -> 49.3 us
  blocking collectives: 13.8 us -> 47.5 us
  local copies, waits for them, and re-layouts: 28.1 us -> 3.94 us
  Pallas kernels: 0 us -> 16.3 us
  matrix products: 15.6 us -> 0 us
  other arithmetic: 8.25 us -> 2.95 us
    all_gather x3 -> x1, waiting for transfers between devices: 266 us -> 0.01 us  [local(): weights = lax.all_gather(block, 'z', axis=0, tiled=False)]
    psum x1 -> x0, waiting for transfers between devices: 88.6 us -> none  [local(): summed = lax.psum(partial_value, 'mp')]
    all_gather x1 -> x4, blocking collectives: 13.8 us -> 47.5 us  [the longest x1 13.5 us: local(): video_y = lax.all_gather(video_pair, 'y', axis=0, tiled=False)]
    ppermute x1 -> x7, starting transfers between devices: 3.15 us -> 29.8 us  [the longest x3 15.3 us: swap(): return lax.ppermute(value, 'core', [(0, 1), (1, 0)])]
    pallas_call x0 -> x4, Pallas kernels: none -> 16.3 us  [the longest x1 6.54 us: local(): pl.pallas_call(vision_kernel, name='vision', out_shape=(jax.ShapeDtypeStr...]
    dot_general x4 -> x0, matrix products: 15.6 us -> none  [the longest x1 10.2 us: local(): jnp.dot(hidden, vit_down, preferred_element_type=jnp.float32)]
    all_to_all x1 -> x2, starting transfers between devices: 9.27 us -> 19.5 us  [the longest x1 16 us: local(): lax.all_to_all(outgoing.reshape(owners, spans + 1, width), TM, 0, 0, tile...]
    ppermute x1 -> x7, waiting for transfers between devices: 0.01 us -> 8.69 us  [the longest x3 7.27 us: ring(): lax.ppermute(value, axis, [(i, (i + step) % count) for i in range(count)])]
  transfers between devices with their start and end apart: 6 -> 10, of which waited for: 5 -> 5; matrix products, arithmetic and copies ran while one was open for 9% -> 4% of each run, Pallas kernels for 0% -> 6%
where the time goes in v2:
time: 157 us; the launch traced here: 156 us
  starting transfers between devices  49.3 us (31%)
  blocking collectives  47.5 us (30%)
  waiting for transfers between devices  22.6 us (14%)
  Pallas kernels  16.3 us (10%)
  between operations  13.7 us (9%)
  local copies, waits for them, and re-layouts  3.94 us (3%)
  other arithmetic  2.95 us (2%)
    all_to_all x1, starting transfers between devices, local(): lax.all_to_all(outgoing.reshape(owners, spans + 1, width), TM, 0, 0, tile...  16 us
    ppermute x3, starting transfers between devices, swap(): return lax.ppermute(value, 'core', [(0, 1), (1, 0)])  15.3 us
    all_to_all x1, waiting for transfers between devices, local(): lax.all_to_all(outgoing.reshape(owners, spans + 1, width), TM, 0, 0, tile...  13.9 us
    all_gather x1, blocking collectives, local(): video_y = lax.all_gather(video_pair, 'y', axis=0, tiled=False)  13.5 us
    all_gather x1, blocking collectives, local(): vit_mine = lax.all_gather(vit_out, 'y', axis=0, tiled=False)  13.2 us
    all_gather x1, blocking collectives, local(): block = lax.all_gather(own, 'x', axis=0, tiled=False)  11.7 us
    ppermute x3, starting transfers between devices, ring(): lax.ppermute(value, axis, [(i, (i + step) % count) for i in range(count)])  10.1 us
    all_gather x1, blocking collectives, local(): cores = lax.all_gather(arrived, 'core', axis=0, tiled=False)  9.13 us
  transfers between devices with their start and end apart: 10, of which 5 were waited for; matrix products, arithmetic and copies ran while one was open for 4% of the time, Pallas kernels for 6%

profile of v2, /device:TPU:1, one launch (start us, length us, event | category | flops | bytes accessed | tf_op | source)
XLA Modules:
  0.0 156.3 jit_solution(9729653260304023581)
XLA Ops:
  6.6 1.1 maximum_maximum_fusion
  7.7 11.7 %all-gather.2 = bf16[448,448]{1,0:T(8,128)(2,1)} all-gather(bf16[112,448]{1,0:T(8,128)(2,1)S(1)} %maximum_maximum_fusion), channel_id=4, replica_groups=mesh['x'=4,'z'=16,'y'=4,'core'=2] {'x'}, dimensions={0}, use_global_device_ids=true | all-gather | bytes 501760 | tf_op jit(solution)/shard_map/all_gather | solution.py:210
  19.4 0.8 slice.9
  20.2 4.4 %collective-permute-start = (bf16[1,128]{1,0:T(2,128)(2,1)S(1)}, bf16[1,128]{1,0:T(2,128)(2,1)S(1)}, u32[]{:S(2)}, u32[]{:S(2)}) collective-permute-start(bf16[1,128]{1,0:T(2,128)(2,1)S(1)} %slice.9), channel_id=1, source_target_pairs={{0,8},{8,16},{16,24},{24,32},{32,40},{40,48},{48,56},{56,64},{64,7... | collective-permute-start | bytes 776 | tf_op jit(solution)/shard_map/ppermute | solution.py:207
  24.6 0.8 select_reduce_fusion
  25.5 0.8 dynamic-slice_add_fusion
  26.2 1.0 reshape.23.mel_ref
  27.2 0.1 copy.26.conv_ref
  27.4 3.1 %prep.1 = bf16[256,640]{1,0:T(8,128)(2,1)S(1)} custom-call(s32[3]{0:T(128)S(1)} %get-tuple-element.18.first_ref, s32[3]{0:T(128)S(1)} %get-tuple-element.17.audio_ref, bf16[160,768]{1,0:T(8,128)(2,1)S(1)} %bitcast.26, bf16[150,512]{1,0:T(8,128)(2,1)S(1)} %reshape.23.mel_ref, bf16[1,128]{1,0:T(2,128)(2,1)S(1)} %collective-permute-done.rim_ref, ...), custom_call_target="tpu_custom_call" | custom-call | tf_op jit(solution)/shard_map/prep/pallas_call | solution.py:216
  30.5 0.8 reshape.24
  31.3 16.0 %all-to-all-start = ((bf16[64,4,640]{2,1,0:T(4,128)(2,1)}), bf16[64,4,640]{2,1,0:T(4,128)(2,1)S(1)}, u32[]{:S(2)}, u32[]{:S(2)}) async-start(bf16[64,4,640]{2,1,0:T(4,128)(2,1)} %reshape.24), calls=%async_computation | async-start | bytes 655360 | tf_op jit(solution)/shard_map/all_to_all | solution.py:231
  47.3 7.5 %collective-permute-start.1 = (bf16[1280,640]{1,0:T(8,128)(2,1)S(1)}, bf16[1280,640]{1,0:T(8,128)(2,1)}, u32[]{:S(2)}, u32[]{:S(2)}) collective-permute-start(bf16[1280,640]{1,0:T(8,128)(2,1)S(1)} %copy-done.2), channel_id=1, source_target_pairs={{0,1},{1,0},{2,3},{3,2},{4,5},{5,4},{6,7},{7,6},{8,9},{9,8},{10,11... | collective-permute-start | bytes 4915208 | tf_op jit(solution)/shard_map/ppermute | solution.py:34
  54.8 1.9 %collective-permute-start.2 = (bf16[640,1280]{1,0:T(8,128)(2,1)}, bf16[640,1280]{1,0:T(8,128)(2,1)}, u32[]{:S(2)}, u32[]{:S(2)}) collective-permute-start(bf16[640,1280]{1,0:T(8,128)(2,1)} %down0.1), channel_id=1, source_target_pairs={{0,1},{1,0},{2,3},{3,2},{4,5},{5,4},{6,7},{7,6},{8,9},{9,8},{10,11... | collective-permute-start | bytes 4915208 | tf_op jit(solution)/shard_map/ppermute | solution.py:34
  56.8 13.9 %all-to-all-done = bf16[64,4,640]{2,1,0:T(4,128)(2,1)S(1)} async-done(((bf16[64,4,640]{2,1,0:T(4,128)(2,1)}), bf16[64,4,640]{2,1,0:T(4,128)(2,1)S(1)}, u32[]{:S(2)}, u32[]{:S(2)}) %all-to-all-start) | async-done | bytes 327712 | tf_op jit(solution)/shard_map/all_to_all | solution.py:231
  70.6 9.1 %all-gather = bf16[128,4,640]{2,1,0:T(4,128)(2,1)S(1)} all-gather(bf16[64,4,640]{2,1,0:T(4,128)(2,1)S(1)} %all-to-all-done), channel_id=2, replica_groups=mesh['x'=4,'z'=16,'y'=4,'core'=2] {'core'}, dimensions={0}, use_global_device_ids=true | all-gather | bytes 983040 | tf_op jit(solution)/shard_map/all_gather | solution.py:236
  79.7 0.3 slice.12
  80.2 13.5 %all_gather.29.video_ref = bf16[4,2,96,640]{3,2,1,0:T(8,128)(2,1)S(1)} all-gather(bf16[1,2,96,640]{3,2,1,0:T(8,128)(2,1)S(1)} %bitcast.31), channel_id=1, replica_groups=mesh['x'=4,'z'=16,'y'=4,'core'=2] {'y'}, dimensions={0}, use_global_device_ids=true | all-gather | bytes 1228800 | tf_op jit(solution)/shard_map/all_gather | solution.py:239
  93.8 6.5 %vision.1 = (bf16[4,96,1280]{2,1,0:T(8,128)(2,1)}, bf16[96,1280]{1,0:T(8,128)(2,1)S(1)}) custom-call(s32[1]{0:T(128)} %bitcast.index_ref, bf16[4,2,96,640]{3,2,1,0:T(8,128)(2,1)S(1)} %all_gather.29.video_ref, bf16[1280,640]{1,0:T(8,128)(2,1)S(1)} %copy-done.2, bf16[640,1280]{1,0:T(8,128)(2,1)S(1)} %copy-done.3, ...), custom_call_target="tpu_custom_call" | custom-call | flops 2516582400 | bytes 9000000 | tf_op jit(solution)/shard_map/vision/pallas_call | solution.py:243
  100.3 3.5 %all-to-all-start.1 = ((bf16[4,96,1280]{2,1,0:T(8,128)(2,1)}), bf16[4,96,1280]{2,1,0:T(8,128)(2,1)S(1)}, u32[]{:S(2)}, u32[]{:S(2)}) async-start(bf16[4,96,1280]{2,1,0:T(8,128)(2,1)} %get-tuple-element.13), calls=%async_computation.1 | async-start | bytes 1966080 | tf_op jit(solution)/shard_map/all_to_all | solution.py:264
  103.8 3.3 %collective-permute-start.3 = (bf16[128,480]{1,0:T(8,128)(2,1)S(1)}, bf16[128,480]{1,0:T(8,128)(2,1)S(1)}, u32[]{:S(2)}, u32[]{:S(2)}) collective-permute-start(bf16[128,480]{1,0:T(8,128)(2,1)S(1)} %bitcast.21), channel_id=1, source_target_pairs={{0,2},{2,4},{4,6},{6,0},{1,3},{3,5},{5,7},{7,1},{8,10},{10,12},{12... | collective-permute-start | bytes 368648 | tf_op jit(solution)/shard_map/ppermute | solution.py:30
  107.2 3.2 %collective-permute-start.4 = (bf16[128,480]{1,0:T(8,128)(2,1)S(1)}, bf16[128,480]{1,0:T(8,128)(2,1)S(1)}, u32[]{:S(2)}, u32[]{:S(2)}) collective-permute-start(bf16[128,480]{1,0:T(8,128)(2,1)S(1)} %bitcast.22), channel_id=1, source_target_pairs={{0,6},{2,0},{4,2},{6,4},{1,7},{3,1},{5,3},{7,5},{8,14},{10,8},{12,... | collective-permute-start | bytes 368648 | tf_op jit(solution)/shard_map/ppermute | solution.py:30
  110.4 3.6 %collective-permute-start.5 = (bf16[128,480]{1,0:T(8,128)(2,1)S(1)}, bf16[128,480]{1,0:T(8,128)(2,1)S(1)}, u32[]{:S(2)}, u32[]{:S(2)}) collective-permute-start(bf16[128,480]{1,0:T(8,128)(2,1)S(1)} %bitcast.23), channel_id=1, source_target_pairs={{0,4},{2,6},{4,0},{6,2},{1,5},{3,7},{5,1},{7,3},{8,12},{10,14},{12... | collective-permute-start | bytes 368648 | tf_op jit(solution)/shard_map/ppermute | solution.py:30
  114.0 1.6 %collective-permute-done.3.b_ref = bf16[128,480]{1,0:T(8,128)(2,1)S(1)} collective-permute-done((bf16[128,480]{1,0:T(8,128)(2,1)S(1)}, bf16[128,480]{1,0:T(8,128)(2,1)S(1)}, u32[]{:S(2)}, u32[]{:S(2)}) %collective-permute-start.3) | collective-permute-done | bytes 122912 | tf_op jit(solution)/shard_map/ppermute | solution.py:30
  115.6 1.5 collective-permute-done.4.c_ref
  117.0 4.2 %collective-permute-done.5.d_ref = bf16[128,480]{1,0:T(8,128)(2,1)S(1)} collective-permute-done((bf16[128,480]{1,0:T(8,128)(2,1)S(1)}, bf16[128,480]{1,0:T(8,128)(2,1)S(1)}, u32[]{:S(2)}, u32[]{:S(2)}) %collective-permute-start.5) | collective-permute-done | bytes 122912 | tf_op jit(solution)/shard_map/ppermute | solution.py:30
  121.3 0.4 audio_spread.1.audio_ref
  121.7 0.1 convert_reduce_fusion
  121.9 13.2 %all-gather.1 = bf16[384,1280]{1,0:T(8,128)(2,1)S(1)} all-gather(bf16[96,1280]{1,0:T(8,128)(2,1)S(1)} %add_convert_fusion), channel_id=3, replica_groups=mesh['x'=4,'z'=16,'y'=4,'core'=2] {'y'}, dimensions={0}, use_global_device_ids=true | all-gather | bytes 1228800 | tf_op jit(solution)/shard_map/all_gather | solution.py:277
  135.1 5.9 %collective-permute-start.6 = (bf16[4,96,1280]{2,1,0:T(8,128)(2,1)S(1)}, bf16[4,96,1280]{2,1,0:T(8,128)(2,1)S(1)}, u32[]{:S(2)}, u32[]{:S(2)}) collective-permute-start(bf16[4,96,1280]{2,1,0:T(8,128)(2,1)S(1)} %bitcast.19), channel_id=1, source_target_pairs={{0,1},{1,0},{2,3},{3,2},{4,5},{5,4},{6,7},{7,6},{8,9},{9,8},{10,11... | collective-permute-start | bytes 2949128 | tf_op jit(solution)/shard_map/ppermute | solution.py:34
  141.4 0.1 reshape.27
  141.8 1.4 collective-permute-done.6.other_ref
  143.2 6.2 %project_place.1 = bf16[448,512]{1,0:T(8,128)(2,1)} custom-call(bf16[4,96,1280]{2,1,0:T(8,128)(2,1)S(1)} %bitcast.20, bf16[4,96,1280]{2,1,0:T(8,128)(2,1)S(1)} %collective-permute-done.6.other_ref, bf16[4,192,512]{2,1,0:T(8,128)(2,1)S(1)} %audio_spread.1.audio_ref, bf16[16,4,112,448]{3,2,1,0:T(8,128)(2,1)} %bitcast.27, s32[1,384]{1,0:T(1,128)S(1)} %reshape.29.place_ref, ...), custom_call_target="tpu_custom_call" | custom-call | flops 1100000000 | bytes 9000000 | tf_op jit(solution)/shard_map/project_place/pallas_call | solution.py:293
  (36 shorter events, 0.9 us)
Async XLA Ops:
  6.5 20.7 %copy-start.4 = (bf16[384,160]{0,1:T(8,128)(2,1)S(1)}, bf16[384,160]{0,1:T(8,128)(2,1)}, u32[]{:S(2)}) copy-start(bf16[384,160]{0,1:T(8,128)(2,1)} %param.13) | copy-start | bytes 368644
  6.5 20.9 %copy-start.1 = (bf16[768,160]{0,1:T(8,128)(2,1)S(1)}, bf16[768,160]{0,1:T(8,128)(2,1)}, u32[]{:S(2)}) copy-start(bf16[768,160]{0,1:T(8,128)(2,1)} %param.14) | copy-start | bytes 737284
  6.5 136.7 %all-gather.6.cloned.1.call-start = ((), (), s32[]{:S(2)}) async-start(), calls=%async_computation.2 | async-start | bytes 7798784 | tf_op jit(solution)/shard_map/all_gather | solution.py:211
  19.4 27.9 %copy-start.2 = (bf16[1280,640]{1,0:T(8,128)(2,1)S(1)}, bf16[1280,640]{1,0:T(8,128)(2,1)}, u32[]{:S(2)}) copy-start(bf16[1280,640]{1,0:T(8,128)(2,1)} %up0.1) | copy-start | bytes 4915204
  20.2 7.2 %collective-permute-start = (bf16[1,128]{1,0:T(2,128)(2,1)S(1)}, bf16[1,128]{1,0:T(2,128)(2,1)S(1)}, u32[]{:S(2)}, u32[]{:S(2)}) collective-permute-start(bf16[1,128]{1,0:T(2,128)(2,1)S(1)} %slice.9), channel_id=1, source_target_pairs={{0,8},{8,16},{16,24},{24,32},{32,40},{40,48},{48,56},{56,64},{64,7... | collective-permute-start | bytes 776 | tf_op jit(solution)/shard_map/ppermute | solution.py:207
  31.3 39.3 %all-to-all-start = ((bf16[64,4,640]{2,1,0:T(4,128)(2,1)}), bf16[64,4,640]{2,1,0:T(4,128)(2,1)S(1)}, u32[]{:S(2)}, u32[]{:S(2)}) async-start(bf16[64,4,640]{2,1,0:T(4,128)(2,1)} %reshape.24), calls=%async_computation | async-start | bytes 655360 | tf_op jit(solution)/shard_map/all_to_all | solution.py:231
  47.3 46.4 %collective-permute-start.1 = (bf16[1280,640]{1,0:T(8,128)(2,1)S(1)}, bf16[1280,640]{1,0:T(8,128)(2,1)}, u32[]{:S(2)}, u32[]{:S(2)}) collective-permute-start(bf16[1280,640]{1,0:T(8,128)(2,1)S(1)} %copy-done.2), channel_id=1, source_target_pairs={{0,1},{1,0},{2,3},{3,2},{4,5},{5,4},{6,7},{7,6},{8,9},{9,8},{10,11... | collective-permute-start | bytes 4915208 | tf_op jit(solution)/shard_map/ppermute | solution.py:34
  54.8 38.9 %collective-permute-start.2 = (bf16[640,1280]{1,0:T(8,128)(2,1)}, bf16[640,1280]{1,0:T(8,128)(2,1)}, u32[]{:S(2)}, u32[]{:S(2)}) collective-permute-start(bf16[640,1280]{1,0:T(8,128)(2,1)} %down0.1), channel_id=1, source_target_pairs={{0,1},{1,0},{2,3},{3,2},{4,5},{5,4},{6,7},{7,6},{8,9},{9,8},{10,11... | collective-permute-start | bytes 4915208 | tf_op jit(solution)/shard_map/ppermute | solution.py:34
  79.7 14.0 %copy-start.3 = (bf16[640,1280]{1,0:T(8,128)(2,1)S(1)}, bf16[640,1280]{1,0:T(8,128)(2,1)}, u32[]{:S(2)}) copy-start(bf16[640,1280]{1,0:T(8,128)(2,1)} %down0.1) | copy-start | bytes 4915204
  100.3 21.4 %all-to-all-start.1 = ((bf16[4,96,1280]{2,1,0:T(8,128)(2,1)}), bf16[4,96,1280]{2,1,0:T(8,128)(2,1)S(1)}, u32[]{:S(2)}, u32[]{:S(2)}) async-start(bf16[4,96,1280]{2,1,0:T(8,128)(2,1)} %get-tuple-element.13), calls=%async_computation.1 | async-start | bytes 1966080 | tf_op jit(solution)/shard_map/all_to_all | solution.py:264
  103.8 11.7 %collective-permute-start.3 = (bf16[128,480]{1,0:T(8,128)(2,1)S(1)}, bf16[128,480]{1,0:T(8,128)(2,1)S(1)}, u32[]{:S(2)}, u32[]{:S(2)}) collective-permute-start(bf16[128,480]{1,0:T(8,128)(2,1)S(1)} %bitcast.21), channel_id=1, source_target_pairs={{0,2},{2,4},{4,6},{6,0},{1,3},{3,5},{5,7},{7,1},{8,10},{10,12},{12... | collective-permute-start | bytes 368648 | tf_op jit(solution)/shard_map/ppermute | solution.py:30
  107.2 9.9 %collective-permute-start.4 = (bf16[128,480]{1,0:T(8,128)(2,1)S(1)}, bf16[128,480]{1,0:T(8,128)(2,1)S(1)}, u32[]{:S(2)}, u32[]{:S(2)}) collective-permute-start(bf16[128,480]{1,0:T(8,128)(2,1)S(1)} %bitcast.22), channel_id=1, source_target_pairs={{0,6},{2,0},{4,2},{6,4},{1,7},{3,1},{5,3},{7,5},{8,14},{10,8},{12,... | collective-permute-start | bytes 368648 | tf_op jit(solution)/shard_map/ppermute | solution.py:30
  110.4 10.9 %collective-permute-start.5 = (bf16[128,480]{1,0:T(8,128)(2,1)S(1)}, bf16[128,480]{1,0:T(8,128)(2,1)S(1)}, u32[]{:S(2)}, u32[]{:S(2)}) collective-permute-start(bf16[128,480]{1,0:T(8,128)(2,1)S(1)} %bitcast.23), channel_id=1, source_target_pairs={{0,4},{2,6},{4,0},{6,2},{1,5},{3,7},{5,1},{7,3},{8,12},{10,14},{12... | collective-permute-start | bytes 368648 | tf_op jit(solution)/shard_map/ppermute | solution.py:30
  121.7 19.4 %copy-start.5 = (s32[192]{0:T(256)S(1)}, s32[192]{0:T(256)}, u32[]{:S(2)}) copy-start(s32[192]{0:T(256)} %param.23) | copy-start | bytes 2308
  121.7 19.4 %copy-start.6 = (s32[192]{0:T(256)S(1)}, s32[192]{0:T(256)}, u32[]{:S(2)}) copy-start(s32[192]{0:T(256)} %param.22) | copy-start | bytes 2308
  121.7 21.5 %copy-start = (bf16[512,1,448]{0,2,1:T(8,128)(2,1)S(1)}, bf16[512,1,448]{0,2,1:T(8,128)(2,1)}, u32[]{:S(2)}) copy-start(bf16[512,1,448]{0,2,1:T(8,128)(2,1)} %param.19) | copy-start | bytes 1376260
  135.1 8.1 %collective-permute-start.6 = (bf16[4,96,1280]{2,1,0:T(8,128)(2,1)S(1)}, bf16[4,96,1280]{2,1,0:T(8,128)(2,1)S(1)}, u32[]{:S(2)}, u32[]{:S(2)}) collective-permute-start(bf16[4,96,1280]{2,1,0:T(8,128)(2,1)S(1)} %bitcast.19), channel_id=1, source_target_pairs={{0,1},{1,0},{2,3},{3,2},{4,5},{5,4},{6,7},{7,6},{8,9},{9,8},{10,11... | collective-permute-start | bytes 2949128 | tf_op jit(solution)/shard_map/ppermute | solution.py:34
Sparse Core Ops, SparseCore 0:
  19.5 116.7 all-gather.5

commit v3 on v2

v3 whole, which is shorter than its diff:
```python
import jax
import jax.numpy as jnp
from jax import lax
from jax.experimental import pallas as pl
from jax.experimental.pallas import tpu as pltpu
from jax.sharding import Mesh, PartitionSpec as P

AT = 50
VT = 64
BF = jnp.bfloat16
F32 = jnp.float32
I32 = jnp.int32
TM = ("x", "z")
MP = ("y", "core")
PAD_A = 32
VMEM = pl.BlockSpec(memory_space=pltpu.VMEM)
SMEM = pl.BlockSpec(memory_space=pltpu.SMEM)
ANY = pl.BlockSpec(memory_space=pl.ANY)
ROOT_HALF = 0.7071067811865476


def span_starts(span_order, offsets):
    listed = jnp.arange(span_order.shape[0], dtype=I32)
    matches = (span_order[:, None] == listed[None, :]).astype(I32)
    return jnp.sum(matches * offsets[:, None], axis=0)


def ring(value, axis, step):
    count = lax.axis_size(axis)
    return lax.ppermute(value, axis, [(i, (i + step) % count) for i in range(count)])


def swap(value):
    return lax.ppermute(value, "core", [(0, 1), (1, 0)])


def gelu(value):
    return 0.5 * value * (1.0 + lax.erf(value * ROOT_HALF))


def dot(a, b):
    return jnp.dot(a, b, preferred_element_type=F32)


def dot_nt(a, b):
    return lax.dot_general(a, b, (((1,), (1,)), ((), ())), preferred_element_type=F32)


def iota(shape, axis):
    return lax.broadcasted_iota(I32, shape, axis)


def params(mib=48):
    return pltpu.CompilerParams(vmem_limit_bytes=mib * 1024 * 1024)


def one_hot(condition):
    return jnp.where(condition, 1.0, 0.0).astype(BF)


def prep_kernel(
    order_ref, offset_ref, video_ref, patch_ref, mel_ref, rim_ref, conv_ref, out_ref
):
    rows, width = out_ref.shape
    spans, count = 3, patch_ref.shape[1]
    block = patch_ref.shape[0]
    nx, nz = lax.axis_size("x"), lax.axis_size("z")
    videos = nx * spans
    position = lax.axis_index("x") * lax.axis_size("z") + lax.axis_index("z")
    listed = iota(order_ref.shape, 1)

    def pick(condition, values):
        return jnp.sum(jnp.where(condition, values, 0), axis=1, keepdims=True)

    first = [pick(order_ref[...] == position * spans + k, offset_ref[...]) for k in range(spans)]
    kept = [pick(listed == position * spans + k, video_ref[...]) for k in range(spans)]
    patch = patch_ref[...]
    row = iota((rows, 1), 0)
    far, slot = row >> 4, row & 15
    to_x = sum((slot >= spans * i).astype(I32) for i in range(1, nx))
    is_video = slot < videos
    kind = jnp.where(is_video, slot - spans * to_x, slot - videos)

    def of_kind(values):
        return jnp.where(kind == 0, values[0], jnp.where(kind == 1, values[1], values[2]))

    start = of_kind(first)
    token = (kind << 6) + ((to_x * nz + far - start) & (VT - 1))
    target = jnp.where(is_video, token * 4, -8)
    column = iota((rows, count), 1)
    source = iota((block, width), 0)
    place = iota((block, width), 1)
    total = jnp.zeros((rows, width), F32)
    for s in range(4):
        picked = dot_nt(one_hot(column == target + s), patch).astype(BF)
        total += dot(picked, one_hot(place == source + s * block))

    total_frames = mel_ref.shape[0]
    frames = total_frames // 4
    frame, at = iota((frames, total_frames), 1), 4 * iota((frames, total_frames), 0)
    mel = mel_ref[...]
    before, f0, f1, f2, f3 = (dot(one_hot(frame == at + k), mel).astype(BF) for k in range(-1, 4))
    first_row = iota((frames, 1), 0) == 0
    before = jnp.where(first_row, rim_ref[...].astype(F32), before.astype(F32)).astype(BF)
    c0, c1, c2 = (conv_ref[k * 128 : (k + 1) * 128, :] for k in range(3))
    even = dot(before, c0) + dot(f0, c1) + dot(f1, c2)
    odd = dot(f1, c0) + dot(f2, c1) + dot(f3, c2)
    pooled = (0.5 * (gelu(even) + gelu(odd))).astype(BF)
    column = iota((rows, frames), 1)
    start = start + of_kind(kept)
    for i in range(nx):
        index = jnp.minimum((i * nz + far - start) & (VT - 1), AT - 1) + kind * AT
        index = jnp.where(is_video | (kind >= spans), -8, index)
        picked = dot(one_hot(column == index), pooled).astype(BF)
        total += dot(picked, one_hot(place == source + i * block))
    out_ref[...] = total.astype(BF)


def vision_kernel(
    video_ref, audio_ref, up0, down0, up1, down1, send_ref, xs, wu, wd, sems
):
    copies = []
    for i, (u, d) in enumerate(((up0, down0), (up1, down1))):
        copies.append(pltpu.make_async_copy(u, wu.at[i], sems.at[2 * i]))
        copies.append(pltpu.make_async_copy(d, wd.at[i], sems.at[2 * i + 1]))
    for copy in copies:
        copy.start()
    ny, cores, half, width = video_ref.shape
    block = width // 4
    for y in range(ny):
        for c in range(cores):
            for s in range(4):
                a, b = (y * cores + c) * block, s * block
                xs[s * half : (s + 1) * half, a : a + block] = video_ref[y, c, :, b : b + block]
    wide = xs[...].astype(F32)
    centred = wide - jnp.mean(wide, axis=1, keepdims=True)
    spread = jnp.mean(centred * centred, axis=1, keepdims=True)
    normed = (centred * lax.rsqrt(spread + 1e-06)).astype(BF)
    total = None
    for i in range(2):
        copies[2 * i].wait()
        hidden = gelu(dot(normed, wu[i])).astype(BF)
        copies[2 * i + 1].wait()
        term = dot(hidden, wd[i])
        total = term if total is None else total + term
    total += wide * (1.0 / ny)
    parts = send_ref.shape[0] // 4
    some = half // parts
    send_ref[...] = jnp.zeros_like(send_ref)
    for s in range(4):
        for x in range(parts):
            a = s * half + x * some
            send_ref[x * ny + s, :some] = total[a : a + some].astype(BF)
            for c in range(cores):
                for k in range(3):
                    a, b = (c * 3 + k) * block, x * block
                    send_ref[x * ny + s, some:, a : a + block] = audio_ref[c, k, :, b : b + block]


def audio_kernel(in_ref, out_ref):
    ny, tokens, _ = out_ref.shape
    block, parts = in_ref.shape[2] // 8, in_ref.shape[0] // ny
    owners = tokens // 3
    near = owners // parts
    some = in_ref.shape[1] - near
    source, place = iota((block, 256), 0), iota((block, 256), 1)
    group = place // PAD_A
    lane = place - group * PAD_A
    spread = one_hot((lane < 20) & (source == group * 20 + lane))
    for y in range(ny):
        for c in range(2):
            for k in range(3):
                a = (c * 3 + k) * block
                rows = [in_ref[x * ny + y, some:, a : a + block] for x in range(parts)]
                piece = dot(jnp.concatenate(rows, axis=0), spread).astype(BF)
                out_ref[y, k * owners : (k + 1) * owners, c * 256 : (c + 1) * 256] = piece


def tail_kernel(
    own_ref, other_ref, audio_ref, weight_ref, place_ref, text_ref, out_ref, video, audio, spread
):
    step = pl.program_id(0)

    @pl.when(step == 0)
    def _():
        video[...] = jnp.zeros_like(video)
        audio[...] = jnp.zeros_like(audio)
        spread[...] = jnp.zeros_like(spread)

    nz, _, rows, columns = weight_ref.shape
    rows_a = rows // 5
    rows_m = rows - rows_a
    merge_w = weight_ref[:, 0, :rows_m, :].reshape(nz * rows_m, columns)
    for z in range(nz):
        spread[z * PAD_A : z * PAD_A + rows_a, :] = weight_ref[z, 0, rows_m:, :]
    both = jnp.concatenate([own_ref[0], other_ref[0]], axis=0)
    video[...] += dot(both, merge_w)
    audio[...] += dot(audio_ref[0], spread[...])

    @pl.when(step == 3)
    def _():
        media = jnp.concatenate([video[...], audio[...]], axis=0).astype(BF)
        count, length = media.shape[0], out_ref.shape[1]
        marks = one_hot(place_ref[...] == iota((length, count), 0))
        placed = lax.dot_general(
            media, marks, (((0,), (1,)), ((), ())), preferred_element_type=F32
        )
        taken = dot_nt(jnp.ones((8, count), BF), marks)[0:1, :]
        out_ref[...] = jnp.where(taken > 0.5, placed, text_ref[...].astype(F32)).astype(BF)


def local(
    mel_frames,
    conv_weight,
    patches,
    vit_up,
    vit_down,
    audio_proj,
    merger,
    text_rows,
    span_order,
    offsets,
    audio_count,
    video_count,
):
    nx, nz, ny = (lax.axis_size(a) for a in ("x", "z", "y"))
    owners = nx * nz
    position = lax.axis_index(TM)
    my_core = lax.axis_index("core")
    spans = mel_frames.shape[0] // (4 * AT)
    tokens = spans * owners
    half = tokens // 2
    columns, rows_m, rows_a = merger.shape[1], merger.shape[0], audio_proj.shape[0]
    rows_w = rows_m + rows_a
    width = 4 * patches.shape[1]
    full = vit_down.shape[1]

    rim = lax.ppermute(mel_frames[-1:], TM, [(i, i + 1) for i in range(owners - 1)])

    own = jnp.concatenate([merger, audio_proj], axis=0)
    rim, own = lax.optimization_barrier((rim, own))
    everywhere = jnp.broadcast_to(own[None], (nx,) + own.shape)
    block = lax.all_to_all(everywhere, "x", 0, 0, tiled=True)

    starts = span_starts(span_order, offsets)
    outgoing = pl.pallas_call(
        prep_kernel,
        name="prep",
        out_shape=jax.ShapeDtypeStruct((nz * 16, width), BF),
        in_specs=[VMEM] * 7,
        out_specs=VMEM,
        compiler_params=params(),
        cost_estimate=pl.CostEstimate(
            flops=2000000000, bytes_accessed=8000000, transcendentals=500000
        ),
    )(
        span_order.reshape(1, -1),
        offsets.reshape(1, -1),
        video_count.reshape(1, -1),
        patches.T,
        mel_frames,
        rim,
        conv_weight,
    )
    block, outgoing = lax.optimization_barrier((block, outgoing))
    weights = lax.all_gather(block, "z", axis=0, tiled=False)
    arrived = lax.all_to_all(outgoing.reshape(nz, 16, width), "z", 0, 0, tiled=True)

    up_other, down_other = swap(vit_up), swap(vit_down)
    cores = lax.all_gather(arrived, "core", axis=0, tiled=False)
    videos, half_z = nx * spans, nz // 2
    pair = lax.dynamic_slice_in_dim(cores, my_core * half_z, half_z, axis=1)[:, :, :videos]
    pair = pair.reshape(2, half_z, nx, spans, width)
    video_pair = jnp.transpose(pair, (0, 2, 1, 3, 4)).reshape(2, half, width)
    video_y = lax.all_gather(video_pair, "y", axis=0, tiled=False)
    audio_own = jnp.transpose(cores[:, :, videos : videos + spans], (0, 2, 1, 3))

    some = half // nx
    rows_sent = some + nz
    flops = 2 * 4 * half * full * 4 * vit_up.shape[1]
    partial_sum = pl.pallas_call(
        vision_kernel,
        name="vision",
        out_shape=jax.ShapeDtypeStruct((nx * ny, rows_sent, full), BF),
        in_specs=[VMEM, VMEM, ANY, ANY, ANY, ANY],
        out_specs=VMEM,
        scratch_shapes=[
            pltpu.VMEM((4 * half, full), BF),
            pltpu.VMEM((2,) + vit_up.shape, BF),
            pltpu.VMEM((2,) + vit_down.shape, BF),
            pltpu.SemaphoreType.DMA((4,)),
        ],
        compiler_params=params(),
        cost_estimate=pl.CostEstimate(flops=flops, bytes_accessed=9000000, transcendentals=500000),
    )(video_y, audio_own, vit_up, vit_down, up_other, down_other)

    incoming = lax.all_to_all(partial_sum, ("x", "y"), 0, 0, tiled=True)
    audio_tokens = pl.pallas_call(
        audio_kernel,
        name="audio_spread",
        out_shape=jax.ShapeDtypeStruct((ny, tokens, nz * PAD_A), BF),
        in_specs=[VMEM],
        out_specs=VMEM,
        compiler_params=params(),
    )(incoming)
    summed = jnp.sum(incoming.reshape(nx, ny, rows_sent, full)[:, :, :some].astype(F32), axis=1)
    vit_out = summed.astype(BF).reshape(half, full)
    vit_mine = lax.all_gather(vit_out, "y", axis=0, tiled=False)
    vit_theirs = swap(vit_mine)

    seq_count = text_rows.shape[0]
    video_where = jnp.mod(position - starts, owners)
    video_place = jnp.where(video_where < video_count, (starts + video_where) // owners, seq_count)
    audio_where = jnp.mod(position - starts - video_count, owners)
    audio_place = jnp.where(
        audio_where < audio_count, (starts + video_count + audio_where) // owners, seq_count
    )

    video_place = video_place.reshape(nx, 2, half_z, spans)
    video_place = jnp.where(my_core == 0, video_place, video_place[:, ::-1])
    video_place = jnp.transpose(video_place, (1, 0, 2, 3)).reshape(-1)
    audio_place = audio_place.reshape(owners, spans).T.reshape(-1)
    places = jnp.concatenate([video_place, audio_place])
    result = pl.pallas_call(
        tail_kernel,
        name="project_place",
        out_shape=jax.ShapeDtypeStruct((columns, seq_count), BF),
        grid_spec=pl.GridSpec(
            grid=(4,),
            in_specs=[
                pl.BlockSpec((1, half, full), lambda s: (s, 0, 0)),
                pl.BlockSpec((1, half, full), lambda s: (s, 0, 0)),
                pl.BlockSpec((1, tokens, nz * PAD_A), lambda s: (s, 0, 0)),
                pl.BlockSpec((nz, 1, rows_w, columns), lambda s: (0, s, 0, 0)),
                pl.BlockSpec((1, 2 * tokens), lambda s: (0, 0)),
                pl.BlockSpec((columns, seq_count), lambda s: (0, 0)),
            ],
            out_specs=pl.BlockSpec((columns, seq_count), lambda s: (0, 0)),
            scratch_shapes=[
                pltpu.VMEM((tokens, columns), F32),
                pltpu.VMEM((tokens, columns), F32),
                pltpu.VMEM((nz * PAD_A, columns), BF),
            ],
        ),
        compiler_params=params(),
        cost_estimate=pl.CostEstimate(flops=1100000000, bytes_accessed=9000000, transcendentals=0),
    )(
        vit_mine,
        vit_theirs,
        audio_tokens,
        weights.reshape(nz, nx, rows_w, columns),
        places.reshape(1, -1),
        text_rows[:, 0, :].T,
    )
    return result.T[:, None, :]


def solution(mesh):
    grid = Mesh(mesh.devices.reshape(4, 16, 4, 2), ("x", "z", "y", "core"))
    placed = (
        P(TM, None),
        P(None, MP),
        P(TM, MP),
        P(None, MP),
        P(MP, None),
        P(TM, MP),
        P(TM, MP),
        P(None, TM, MP),
        P(),
        P(),
        P(),
        P(),
    )
    return jax.shard_map(
        local, mesh=grid, in_specs=placed, out_specs=P(None, TM, MP), check_vma=False
    )
```

time: 157 us -> 148 us (0.943)
  blocking collectives: 47.5 us -> 63.4 us
  waiting for transfers between devices: 22.6 us -> 7.68 us
  starting transfers between devices: 49.3 us -> 39.2 us
  other arithmetic: 2.95 us -> 1.29 us
  local copies, waits for them, and re-layouts: 3.94 us -> 5.52 us
    all_to_all x0 -> x1, blocking collectives: none -> 25.5 us  [local(): incoming = lax.all_to_all(partial_sum, ('x', 'y'), 0, 0, tiled=True)]
    all_gather x1 -> x0, blocking collectives: 11.7 us -> none  [local(): block = lax.all_gather(own, 'x', axis=0, tiled=False)]
    ppermute x3 -> x0, starting transfers between devices: 10.1 us -> none  [ring(): lax.ppermute(value, axis, [(i, (i + step) % count) for i in range(count)])]
    ppermute x3 -> x0, waiting for transfers between devices: 7.27 us -> none  [ring(): lax.ppermute(value, axis, [(i, (i + step) % count) for i in range(count)])]
    all_to_all x2, waiting for transfers between devices: 13.9 us -> 6.69 us  [the longest x1 6.24 us: local(): lax.all_to_all(outgoing.reshape(nz, 16, width), 'z', 0, 0, tiled=True)]
    unnamed x16 -> x22, local copies, waits for them, and re-layouts: 0.2 us -> 3.05 us
    all_gather x1, blocking collectives: 9.13 us -> 11.9 us  [local(): cores = lax.all_gather(arrived, 'core', axis=0, tiled=False)]
    reshape x4 -> x2, local copies, waits for them, and re-layouts: 2.04 us -> 0.26 us  [the longest x1 0.13 us: local(): video_place = jnp.transpose(video_place, (1, 0, 2, 3)).reshape(-1)]
  transfers between devices with their start and end apart: 10 -> 7, of which waited for: 5 -> 3; matrix products, arithmetic and copies ran while one was open for 4% -> 2% of each run, Pallas kernels for 6% -> 7%
where the time goes in v3:
time: 148 us; the launch traced here: 147 us
  blocking collectives  63.4 us (43%)
  starting transfers between devices  39.2 us (26%)
  Pallas kernels  16.6 us (11%)
  between operations  13.6 us (9%)
  waiting for transfers between devices  7.68 us (5%)
  local copies, waits for them, and re-layouts  5.52 us (4%)
    all_to_all x1, blocking collectives, local(): incoming = lax.all_to_all(partial_sum, ('x', 'y'), 0, 0, tiled=True)  25.5 us
    ppermute x3, starting transfers between devices, swap(): return lax.ppermute(value, 'core', [(0, 1), (1, 0)])  14.8 us
    all_gather x1, blocking collectives, local(): video_y = lax.all_gather(video_pair, 'y', axis=0, tiled=False)  13.8 us
    all_gather x1, blocking collectives, local(): vit_mine = lax.all_gather(vit_out, 'y', axis=0, tiled=False)  12.2 us
    all_gather x1, blocking collectives, local(): cores = lax.all_gather(arrived, 'core', axis=0, tiled=False)  11.9 us
    all_to_all x1, starting transfers between devices, local(): block = lax.all_to_all(everywhere, 'x', 0, 0, tiled=True)  11.6 us
    all_to_all x1, starting transfers between devices, local(): lax.all_to_all(outgoing.reshape(nz, 16, width), 'z', 0, 0, tiled=True)  8.48 us
    pallas_call x1, Pallas kernels, local(): pl.pallas_call(tail_kernel, name='project_place', out_shape=jax.ShapeDtyp...  6.49 us
  transfers between devices with their start and end apart: 7, of which 3 were waited for; matrix products, arithmetic and copies ran while one was open for 2% of the time, Pallas kernels for 7%

profile of v3, /device:TPU:1, one launch (start us, length us, event | category | flops | bytes accessed | tf_op | source)
XLA Modules:
  0.0 147.3 jit_solution(289130432920829500)
XLA Ops:
  6.5 0.7 slice.12
  7.3 4.4 %collective-permute-start = (bf16[1,128]{1,0:T(2,128)(2,1)S(1)}, bf16[1,128]{1,0:T(2,128)(2,1)S(1)}, u32[]{:S(2)}, u32[]{:S(2)}) collective-permute-start(bf16[1,128]{1,0:T(2,128)(2,1)S(1)} %slice.12), channel_id=1, source_target_pairs={{0,8},{8,16},{16,24},{24,32},{32,40},{40,48},{48,56},{56,64},{64,7... | collective-permute-start | bytes 776 | tf_op jit(solution)/shard_map/ppermute | solution.py:238
  11.6 0.9 pad_maximum_fusion
  12.6 0.8 broadcast_in_dim.9
  13.4 11.6 %all-to-all-start = ((bf16[4,100,448]{2,1,0:T(8,128)(2,1)}), bf16[4,100,448]{2,1,0:T(8,128)(2,1)}, u32[]{:S(2)}, u32[]{:S(2)}) async-start(bf16[4,100,448]{2,1,0:T(8,128)(2,1)} %broadcast_in_dim.9), calls=%async_computation | async-start | bytes 851968 | tf_op jit(solution)/shard_map/all_to_all | solution.py:243
  24.9 0.1 copy.35.conv_ref
  25.1 0.9 copy-done.6
  26.1 0.9 copy-done.7
  27.0 4.0 %prep.1 = bf16[256,640]{1,0:T(8,128)(2,1)} custom-call(s32[1,192]{1,0:T(1,128)S(1)} %bitcast.30, s32[1,192]{1,0:T(1,128)S(1)} %bitcast.31, s32[1,192]{1,0:T(1,128)S(1)} %bitcast.32, bf16[160,768]{1,0:T(8,128)(2,1)S(1)} %bitcast.33, bf16[600,128]{1,0:T(8,128)(2,1)S(1)} %copy-done.7, bf16[1,128]{1,0:T(2,128)(2,1)S(1)} %collective-permute-done.rim_ref, ...), custom_call_target="tpu_custom_call" | custom-call | flops 2000000000 | bytes 8000000 | tf_op jit(solution)/shard_map/prep/pallas_call | solution.py:246
  31.0 0.4 all-to-all-done
  31.5 8.5 %all-to-all-start.1 = ((bf16[16,16,640]{2,1,0:T(8,128)(2,1)}), bf16[16,16,640]{2,1,0:T(8,128)(2,1)}, u32[]{:S(2)}, u32[]{:S(2)}) async-start(bf16[16,16,640]{2,1,0:T(8,128)(2,1)} %bitcast.4), calls=%async_computation.1 | async-start | bytes 655360 | tf_op jit(solution)/shard_map/all_to_all | solution.py:267
  40.0 5.4 %collective-permute-start.1 = (bf16[1280,640]{1,0:T(8,128)(2,1)S(1)}, bf16[1280,640]{1,0:T(8,128)(2,1)}, u32[]{:S(2)}, u32[]{:S(2)}) collective-permute-start(bf16[1280,640]{1,0:T(8,128)(2,1)S(1)} %copy-done.4), channel_id=1, source_target_pairs={{0,1},{1,0},{2,3},{3,2},{4,5},{5,4},{6,7},{7,6},{8,9},{9,8},{10,11... | collective-permute-start | bytes 4915208 | tf_op jit(solution)/shard_map/ppermute | solution.py:34
  45.4 1.9 %collective-permute-start.2 = (bf16[640,1280]{1,0:T(8,128)(2,1)S(1)}, bf16[640,1280]{1,0:T(8,128)(2,1)}, u32[]{:S(2)}, u32[]{:S(2)}) collective-permute-start(bf16[640,1280]{1,0:T(8,128)(2,1)S(1)} %copy-done.5), channel_id=1, source_target_pairs={{0,1},{1,0},{2,3},{3,2},{4,5},{5,4},{6,7},{7,6},{8,9},{9,8},{10,11... | collective-permute-start | bytes 4915208 | tf_op jit(solution)/shard_map/ppermute | solution.py:34
  47.3 6.2 %all-to-all-done.1 = bf16[16,16,640]{2,1,0:T(8,128)(2,1)} async-done(((bf16[16,16,640]{2,1,0:T(8,128)(2,1)}), bf16[16,16,640]{2,1,0:T(8,128)(2,1)}, u32[]{:S(2)}, u32[]{:S(2)}) %all-to-all-start.1) | async-done | bytes 327712 | tf_op jit(solution)/shard_map/all_to_all | solution.py:267
  53.5 11.9 %all-gather = bf16[32,16,640]{2,1,0:T(8,128)(2,1)S(1)} all-gather(bf16[16,16,640]{2,1,0:T(8,128)(2,1)} %all-to-all-done.1), channel_id=2, replica_groups=mesh['x'=4,'z'=16,'y'=4,'core'=2] {'core'}, dimensions={0}, use_global_device_ids=true | all-gather | bytes 983040 | tf_op jit(solution)/shard_map/all_gather | solution.py:270
  65.4 0.1 slice.16
  65.6 0.2 copy.37
  65.9 13.8 %all_gather.20.video_ref = bf16[4,2,96,640]{3,2,1,0:T(8,128)(2,1)S(1)} all-gather(bf16[1,2,96,640]{3,2,1,0:T(8,128)(2,1)S(1)} %copy.38), channel_id=1, replica_groups=mesh['x'=4,'z'=16,'y'=4,'core'=2] {'y'}, dimensions={0}, use_global_device_ids=true | all-gather | bytes 1228800 | tf_op jit(solution)/shard_map/all_gather | solution.py:275
  79.7 5.6 %vision.1 = bf16[16,40,1280]{2,1,0:T(8,128)(2,1)S(1)} custom-call(bf16[4,2,96,640]{3,2,1,0:T(8,128)(2,1)S(1)} %all_gather.20.video_ref, bf16[2,3,16,640]{3,2,1,0:T(8,128)(2,1)S(1)} %bitcast.29, bf16[1280,640]{1,0:T(8,128)(2,1)S(1)} %copy-done.4, bf16[640,1280]{1,0:T(8,128)(2,1)S(1)} %copy-done.5, bf16[1280,640]{1,0:T(8,128)(2,1)} %collective-permute-done.1.up1, ...), custom_call_target="tpu_custom_call" | custom-call | flops 2516582400 | bytes 9000000 | tf_op jit(solution)/shard_map/vision/pallas_call | solution.py:281
  85.3 25.5 %all_to_all.15.in_ref = bf16[16,40,1280]{2,1,0:T(8,128)(2,1)S(1)} all-to-all(bf16[16,40,1280]{2,1,0:T(8,128)(2,1)S(1)} %vision.1), channel_id=1, replica_groups=mesh['x'=4,'z'=16,'y'=4,'core'=2] {'x','y'}, dimensions={0} | all-to-all | bytes 3276800 | tf_op jit(solution)/shard_map/all_to_all | solution.py:297
  110.8 0.1 slice_reduce_fusion
  110.9 12.2 %all_gather.21.own_ref = bf16[4,96,1280]{2,1,0:T(8,128)(2,1)S(1)} all-gather(bf16[1,96,1280]{2,1,0:T(8,128)(2,1)S(1)} %bitcast.37), channel_id=1, replica_groups=mesh['x'=4,'z'=16,'y'=4,'core'=2] {'y'}, dimensions={0}, use_global_device_ids=true | all-gather | bytes 1228800 | tf_op jit(solution)/shard_map/all_gather | solution.py:308
  123.1 7.5 %collective-permute-start.3 = (bf16[4,96,1280]{2,1,0:T(8,128)(2,1)S(1)}, bf16[4,96,1280]{2,1,0:T(8,128)(2,1)}, u32[]{:S(2)}, u32[]{:S(2)}) collective-permute-start(bf16[4,96,1280]{2,1,0:T(8,128)(2,1)S(1)} %all_gather.21.own_ref), channel_id=1, source_target_pairs={{0,1},{1,0},{2,3},{3,2},{4,5},{5,4},{6,7},{7,6},{8,9},{9,8},{10,11... | collective-permute-start | bytes 2949128 | tf_op jit(solution)/shard_map/ppermute | solution.py:34
  130.7 0.1 select_reduce_fusion
  130.9 0.1 reshape.42
  131.0 0.1 reshape.43
  131.2 0.1 reshape.44
  131.4 0.1 reshape.45
  131.6 0.5 audio_spread.1.audio_ref
  132.0 1.0 collective-permute-done.3.other_ref
  133.0 1.0 copy-done
  134.0 6.5 %project_place.1 = bf16[448,512]{1,0:T(8,128)(2,1)} custom-call(bf16[4,96,1280]{2,1,0:T(8,128)(2,1)S(1)} %all_gather.21.own_ref, bf16[4,96,1280]{2,1,0:T(8,128)(2,1)} %collective-permute-done.3.other_ref, bf16[4,192,512]{2,1,0:T(8,128)(2,1)S(1)} %audio_spread.1.audio_ref, bf16[16,4,100,448]{3,2,1,0:T(8,128)(2,1)} %bitcast.34, ...), custom_call_target="tpu_custom_call" | custom-call | flops 1100000000 | bytes 9000000 | tf_op jit(solution)/shard_map/project_place/pallas_call | solution.py:324
  (33 shorter events, 0.4 us)
Async XLA Ops:
  6.5 18.4 %copy-start.8 = (bf16[384,160]{0,1:T(8,128)(2,1)S(1)}, bf16[384,160]{0,1:T(8,128)(2,1)}, u32[]{:S(2)}) copy-start(bf16[384,160]{0,1:T(8,128)(2,1)} %param.13) | copy-start | bytes 368644
  6.5 18.5 %copy-start.1 = (s32[192]{0:T(256)S(1)}, s32[192]{0:T(256)}, u32[]{:S(2)}) copy-start(s32[192]{0:T(256)} %param.20) | copy-start | bytes 2308
  6.5 18.6 %copy-start.2 = (s32[192]{0:T(256)S(1)}, s32[192]{0:T(256)}, u32[]{:S(2)}) copy-start(s32[192]{0:T(256)} %param.21) | copy-start | bytes 2308
  6.5 18.6 %copy-start.3 = (s32[192]{0:T(256)S(1)}, s32[192]{0:T(256)}, u32[]{:S(2)}) copy-start(s32[192]{0:T(256)} %param.23) | copy-start | bytes 2308
  7.3 5.3 %collective-permute-start = (bf16[1,128]{1,0:T(2,128)(2,1)S(1)}, bf16[1,128]{1,0:T(2,128)(2,1)S(1)}, u32[]{:S(2)}, u32[]{:S(2)}) collective-permute-start(bf16[1,128]{1,0:T(2,128)(2,1)S(1)} %slice.12), channel_id=1, source_target_pairs={{0,8},{8,16},{16,24},{24,32},{32,40},{40,48},{48,56},{56,64},{64,7... | collective-permute-start | bytes 776 | tf_op jit(solution)/shard_map/ppermute | solution.py:238
  13.4 18.1 %all-to-all-start = ((bf16[4,100,448]{2,1,0:T(8,128)(2,1)}), bf16[4,100,448]{2,1,0:T(8,128)(2,1)}, u32[]{:S(2)}, u32[]{:S(2)}) async-start(bf16[4,100,448]{2,1,0:T(8,128)(2,1)} %broadcast_in_dim.9), calls=%async_computation | async-start | bytes 851968 | tf_op jit(solution)/shard_map/all_to_all | solution.py:243
  24.9 108.1 %all-gather.4.cloned.1.call-start = ((), (), s32[]{:S(2)}) async-start(), calls=%async_computation.3 | async-start | bytes 7241728 | tf_op jit(solution)/shard_map/all_gather | solution.py:266
  25.1 0.9 copy-start.6
  26.1 0.9 copy-start.7
  27.0 13.0 %copy-start.4 = (bf16[1280,640]{1,0:T(8,128)(2,1)S(1)}, bf16[1280,640]{1,0:T(8,128)(2,1)}, u32[]{:S(2)}) copy-start(bf16[1280,640]{1,0:T(8,128)(2,1)} %up0.1) | copy-start | bytes 4915204
  27.0 18.4 %copy-start.5 = (bf16[640,1280]{1,0:T(8,128)(2,1)S(1)}, bf16[640,1280]{1,0:T(8,128)(2,1)}, u32[]{:S(2)}) copy-start(bf16[640,1280]{1,0:T(8,128)(2,1)} %down0.1) | copy-start | bytes 4915204
  31.5 22.0 %all-to-all-start.1 = ((bf16[16,16,640]{2,1,0:T(8,128)(2,1)}), bf16[16,16,640]{2,1,0:T(8,128)(2,1)}, u32[]{:S(2)}, u32[]{:S(2)}) async-start(bf16[16,16,640]{2,1,0:T(8,128)(2,1)} %bitcast.4), calls=%async_computation.1 | async-start | bytes 655360 | tf_op jit(solution)/shard_map/all_to_all | solution.py:267
  40.0 39.7 %collective-permute-start.1 = (bf16[1280,640]{1,0:T(8,128)(2,1)S(1)}, bf16[1280,640]{1,0:T(8,128)(2,1)}, u32[]{:S(2)}, u32[]{:S(2)}) collective-permute-start(bf16[1280,640]{1,0:T(8,128)(2,1)S(1)} %copy-done.4), channel_id=1, source_target_pairs={{0,1},{1,0},{2,3},{3,2},{4,5},{5,4},{6,7},{7,6},{8,9},{9,8},{10,11... | collective-permute-start | bytes 4915208 | tf_op jit(solution)/shard_map/ppermute | solution.py:34
  45.4 34.3 %collective-permute-start.2 = (bf16[640,1280]{1,0:T(8,128)(2,1)S(1)}, bf16[640,1280]{1,0:T(8,128)(2,1)}, u32[]{:S(2)}, u32[]{:S(2)}) collective-permute-start(bf16[640,1280]{1,0:T(8,128)(2,1)S(1)} %copy-done.5), channel_id=1, source_target_pairs={{0,1},{1,0},{2,3},{3,2},{4,5},{5,4},{6,7},{7,6},{8,9},{9,8},{10,11... | collective-permute-start | bytes 4915208 | tf_op jit(solution)/shard_map/ppermute | solution.py:34
  110.8 20.0 %copy-start.9 = (s32[192]{0:T(256)S(1)}, s32[192]{0:T(256)}, u32[]{:S(2)}) copy-start(s32[192]{0:T(256)} %param.22) | copy-start | bytes 2308
  123.1 9.9 %collective-permute-start.3 = (bf16[4,96,1280]{2,1,0:T(8,128)(2,1)S(1)}, bf16[4,96,1280]{2,1,0:T(8,128)(2,1)}, u32[]{:S(2)}, u32[]{:S(2)}) collective-permute-start(bf16[4,96,1280]{2,1,0:T(8,128)(2,1)S(1)} %all_gather.21.own_ref), channel_id=1, source_target_pairs={{0,1},{1,0},{2,3},{3,2},{4,5},{5,4},{6,7},{7,6},{8,9},{9,8},{10,11... | collective-permute-start | bytes 2949128 | tf_op jit(solution)/shard_map/ppermute | solution.py:34
  133.0 1.0 copy-start
Sparse Core Ops, SparseCore 0:
  31.6 95.2 all-gather.3

commit v4 on v3

--- a/solution.py
+++ b/solution.py
@@ -50,8 +50,12 @@
     return lax.broadcasted_iota(I32, shape, axis)
 
 
-def params(mib=48):
+def params(mib):
     return pltpu.CompilerParams(vmem_limit_bytes=mib * 1024 * 1024)
+
+
+def whole(shape):
+    return pl.BlockSpec(shape, lambda *i: (0,) * len(shape))
 
 
 def one_hot(condition):
@@ -59,7 +63,7 @@
 
 
 def prep_kernel(
-    order_ref, offset_ref, video_ref, patch_ref, mel_ref, rim_ref, conv_ref, out_ref
+    order_ref, offset_ref, video_ref, patch_ref, mel_ref, rim_ref, conv_ref, out_ref, wide_mel, shifted
 ):
     rows, width = out_ref.shape
     spans, count = 3, patch_ref.shape[1]
@@ -95,16 +99,15 @@
         picked = dot_nt(one_hot(column == target + s), patch).astype(BF)
         total += dot(picked, one_hot(place == source + s * block))
 
-    total_frames = mel_ref.shape[0]
-    frames = total_frames // 4
-    frame, at = iota((frames, total_frames), 1), 4 * iota((frames, total_frames), 0)
-    mel = mel_ref[...]
-    before, f0, f1, f2, f3 = (dot(one_hot(frame == at + k), mel).astype(BF) for k in range(-1, 4))
-    first_row = iota((frames, 1), 0) == 0
-    before = jnp.where(first_row, rim_ref[...].astype(F32), before.astype(F32)).astype(BF)
-    c0, c1, c2 = (conv_ref[k * 128 : (k + 1) * 128, :] for k in range(3))
-    even = dot(before, c0) + dot(f0, c1) + dot(f1, c2)
-    odd = dot(f1, c0) + dot(f2, c1) + dot(f3, c2)
+    frames = mel_ref.shape[0] // 4
+    wide_mel[...] = mel_ref[...].astype(F32)
+    f0, f1, f2, f3 = (wide_mel[pl.ds(k, frames, stride=4), :] for k in range(4))
+    shifted[0:1, :] = rim_ref[...].astype(F32)
+    shifted[1:frames, :] = wide_mel[pl.ds(3, frames - 1, stride=4), :]
+    before, f0, f1, f2, f3 = (f.astype(BF) for f in (shifted[...], f0, f1, f2, f3))
+    c0, c1, c2 = (conv_ref[:, k * 128 : (k + 1) * 128] for k in range(3))
+    even = dot_nt(before, c0) + dot_nt(f0, c1) + dot_nt(f1, c2)
+    odd = dot_nt(f1, c0) + dot_nt(f2, c1) + dot_nt(f3, c2)
     pooled = (0.5 * (gelu(even) + gelu(odd))).astype(BF)
     column = iota((rows, frames), 1)
     start = start + of_kind(kept)
@@ -177,36 +180,58 @@
 
 
 def tail_kernel(
-    own_ref, other_ref, audio_ref, weight_ref, place_ref, text_ref, out_ref, video, audio, spread
+    own_ref,
+    other_ref,
+    audio_own_ref,
+    audio_other_ref,
+    low_ref,
+    high_ref,
+    place_ref,
+    text_ref,
+    out_ref,
+    video,
+    audio,
+    spread,
+    marks,
+    text,
+    sem,
 ):
     step = pl.program_id(0)
+    fetch = pltpu.make_async_copy(text_ref, text, sem)
 
     @pl.when(step == 0)
     def _():
+        fetch.start()
         video[...] = jnp.zeros_like(video)
         audio[...] = jnp.zeros_like(audio)
         spread[...] = jnp.zeros_like(spread)
-
-    nz, _, rows, columns = weight_ref.shape
+        marks[...] = one_hot(place_ref[...] == iota(marks.shape, 0))
+
+    near, _, rows, columns = low_ref.shape
     rows_a = rows // 5
     rows_m = rows - rows_a
-    merge_w = weight_ref[:, 0, :rows_m, :].reshape(nz * rows_m, columns)
-    for z in range(nz):
-        spread[z * PAD_A : z * PAD_A + rows_a, :] = weight_ref[z, 0, rows_m:, :]
     both = jnp.concatenate([own_ref[0], other_ref[0]], axis=0)
-    video[...] += dot(both, merge_w)
-    audio[...] += dot(audio_ref[0], spread[...])
+    depth = near * rows_m
+    total = video[...]
+    for i, ref in enumerate((low_ref, high_ref)):
+        merge_w = ref[:, 0, :rows_m, :].reshape(depth, columns)
+        total += dot(both[:, i * depth : (i + 1) * depth], merge_w)
+        for z in range(near):
+            a = (i * near + z) * PAD_A
+            spread[a : a + rows_a, :] = ref[z, 0, rows_m:, :]
+    video[...] = total
+    tokens = jnp.concatenate([audio_own_ref[0], audio_other_ref[0]], axis=0)
+    audio[...] += dot(tokens, spread[...])
 
     @pl.when(step == 3)
     def _():
         media = jnp.concatenate([video[...], audio[...]], axis=0).astype(BF)
-        count, length = media.shape[0], out_ref.shape[1]
-        marks = one_hot(place_ref[...] == iota((length, count), 0))
         placed = lax.dot_general(
-            media, marks, (((0,), (1,)), ((), ())), preferred_element_type=F32
+            media, marks[...], (((0,), (1,)), ((), ())), preferred_element_type=F32
         )
-        taken = dot_nt(jnp.ones((8, count), BF), marks)[0:1, :]
-        out_ref[...] = jnp.where(taken > 0.5, placed, text_ref[...].astype(F32)).astype(BF)
+        taken = dot_nt(jnp.ones((8, media.shape[0]), BF), marks[...])[0:1, :]
+        fetch.wait()
+        out_ref[...] = jnp.where(taken > 0.5, placed, text[...].astype(F32)).astype(BF)
 
 
 def local(
@@ -238,45 +263,72 @@
     rim = lax.ppermute(mel_frames[-1:], TM, [(i, i + 1) for i in range(owners - 1)])
 
     own = jnp.concatenate([merger, audio_proj], axis=0)
-    rim, own = lax.optimization_barrier((rim, own))
-    everywhere = jnp.broadcast_to(own[None], (nx,) + own.shape)
+    everywhere = jnp.stack([own] * nx)
+    rim, everywhere = lax.optimization_barrier((rim, everywhere))
     block = lax.all_to_all(everywhere, "x", 0, 0, tiled=True)
 
     starts = span_starts(span_order, offsets)
-    outgoing = pl.pallas_call(
-        prep_kernel,
-        name="prep",
-        out_shape=jax.ShapeDtypeStruct((nz * 16, width), BF),
-        in_specs=[VMEM] * 7,
-        out_specs=VMEM,
-        compiler_params=params(),
-        cost_estimate=pl.CostEstimate(
-            flops=2000000000, bytes_accessed=8000000, transcendentals=500000
-        ),
-    )(
+    prep_in = (
         span_order.reshape(1, -1),
         offsets.reshape(1, -1),
         video_count.reshape(1, -1),
         patches.T,
         mel_frames,
         rim,
-        conv_weight,
+        conv_weight.T,
     )
+    outgoing = pl.pallas_call(
+        prep_kernel,
+        name="prep",
+        out_shape=jax.ShapeDtypeStruct((nz * 16, width), BF),
+        grid=(1,),
+        in_specs=[whole(v.shape) for v in prep_in],
+        out_specs=whole((nz * 16, width)),
+        scratch_shapes=[
+            pltpu.VMEM(mel_frames.shape, F32),
+            pltpu.VMEM((spans * AT, mel_frames.shape[1]), F32),
+        ],
+        compiler_params=params(60),
+        cost_estimate=pl.CostEstimate(
+            flops=2000000000, bytes_accessed=8000000, transcendentals=500000
+        ),
+    )(*prep_in)
     block, outgoing = lax.optimization_barrier((block, outgoing))
     weights = lax.all_gather(block, "z", axis=0, tiled=False)
     arrived = lax.all_to_all(outgoing.reshape(nz, 16, width), "z", 0, 0, tiled=True)
 
+    videos, half_z = nx * spans, nz // 2
+    seq_count = text_rows.shape[0]
+    video_where = jnp.mod(position - starts, owners)
+    video_place = jnp.where(video_where < video_count, (starts + video_where) // owners, seq_count)
+    audio_where = jnp.mod(position - starts - video_count, owners)
+    audio_place = jnp.where(
+        audio_where < audio_count, (starts + video_count + audio_where) // owners, seq_count
+    )
+
+
+    def ordered(places, axes):
+        places = places.reshape(nx, 2, half_z, spans)
+        places = jnp.where(my_core == 0, places, places[:, ::-1])
+        return jnp.transpose(places, axes).reshape(-1)
+
+    video_place = ordered(video_place, (1, 0, 2, 3))
+    audio_place = ordered(audio_place, (1, 3, 0, 2))
+    places = jnp.concatenate([video_place, audio_place])
+    text = text_rows[:, 0, :].T
+
+    arrived, places = lax.optimization_barrier((arrived, places.reshape(1, -1)))
+
     up_other, down_other = swap(vit_up), swap(vit_down)
     cores = lax.all_gather(arrived, "core", axis=0, tiled=False)
-    videos, half_z = nx * spans, nz // 2
-    pair = lax.dynamic_slice_in_dim(cores, my_core * half_z, half_z, axis=1)[:, :, :videos]
-    pair = pair.reshape(2, half_z, nx, spans, width)
+    near = lax.dynamic_slice_in_dim(cores, my_core * half_z, half_z, axis=1)
+    pair = near[:, :, :videos].reshape(2, half_z, nx, spans, width)
     video_pair = jnp.transpose(pair, (0, 2, 1, 3, 4)).reshape(2, half, width)
     video_y = lax.all_gather(video_pair, "y", axis=0, tiled=False)
-    audio_own = jnp.transpose(cores[:, :, videos : videos + spans], (0, 2, 1, 3))
+    audio_own = jnp.transpose(near[:, :, videos : videos + spans], (0, 2, 1, 3))
 
     some = half // nx
-    rows_sent = some + nz
+    rows_sent = some + half_z
     flops = 2 * 4 * half * full * 4 * vit_up.shape[1]
     partial_sum = pl.pallas_call(
         vision_kernel,
@@ -290,7 +342,7 @@
             pltpu.VMEM((2,) + vit_down.shape, BF),
             pltpu.SemaphoreType.DMA((4,)),
         ],
-        compiler_params=params(),
+        compiler_params=params(28),
         cost_estimate=pl.CostEstimate(flops=flops, bytes_accessed=9000000, transcendentals=500000),
     )(video_y, audio_own, vit_up, vit_down, up_other, down_other)
 
@@ -298,59 +350,54 @@
     audio_tokens = pl.pallas_call(
         audio_kernel,
         name="audio_spread",
-        out_shape=jax.ShapeDtypeStruct((ny, tokens, nz * PAD_A), BF),
+        out_shape=jax.ShapeDtypeStruct((ny, half, nz * PAD_A), BF),
         in_specs=[VMEM],
         out_specs=VMEM,
-        compiler_params=params(),
+        compiler_params=params(8),
     )(incoming)
+    audio_theirs = swap(audio_tokens)
     summed = jnp.sum(incoming.reshape(nx, ny, rows_sent, full)[:, :, :some].astype(F32), axis=1)
     vit_out = summed.astype(BF).reshape(half, full)
     vit_mine = lax.all_gather(vit_out, "y", axis=0, tiled=False)
     vit_theirs = swap(vit_mine)
 
-    seq_count = text_rows.shape[0]
-    video_where = jnp.mod(position - starts, owners)
-    video_place = jnp.where(video_where < video_count, (starts + video_where) // owners, seq_count)
-    audio_where = jnp.mod(position - starts - video_count, owners)
-    audio_place = jnp.where(
-        audio_where < audio_count, (starts + video_count + audio_where) // owners, seq_count
-    )
-
-    video_place = video_place.reshape(nx, 2, half_z, spans)
-    video_place = jnp.where(my_core == 0, video_place, video_place[:, ::-1])
-    video_place = jnp.transpose(video_place, (1, 0, 2, 3)).reshape(-1)
-    audio_place = audio_place.reshape(owners, spans).T.reshape(-1)
-    places = jnp.concatenate([video_place, audio_place])
     result = pl.pallas_call(
         tail_kernel,
         name="project_place",
         out_shape=jax.ShapeDtypeStruct((columns, seq_count), BF),
         grid_spec=pl.GridSpec(
-            grid=(4,),
+            grid=(nx,),
             in_specs=[
                 pl.BlockSpec((1, half, full), lambda s: (s, 0, 0)),
                 pl.BlockSpec((1, half, full), lambda s: (s, 0, 0)),
-                pl.BlockSpec((1, tokens, nz * PAD_A), lambda s: (s, 0, 0)),
-                pl.BlockSpec((nz, 1, rows_w, columns), lambda s: (0, s, 0, 0)),
-                pl.BlockSpec((1, 2 * tokens), lambda s: (0, 0)),
-                pl.BlockSpec((columns, seq_count), lambda s: (0, 0)),
+                pl.BlockSpec((1, half, nz * PAD_A), lambda s: (s, 0, 0)),
+                pl.BlockSpec((1, half, nz * PAD_A), lambda s: (s, 0, 0)),
+                pl.BlockSpec((half_z, 1, rows_w, columns), lambda s: (0, s, 0, 0)),
+                pl.BlockSpec((half_z, 1, rows_w, columns), lambda s: (1, s, 0, 0)),
+                whole((1, 2 * tokens)),
+                ANY,
             ],
-            out_specs=pl.BlockSpec((columns, seq_count), lambda s: (0, 0)),
+            out_specs=whole((columns, seq_count)),
             scratch_shapes=[
                 pltpu.VMEM((tokens, columns), F32),
                 pltpu.VMEM((tokens, columns), F32),
                 pltpu.VMEM((nz * PAD_A, columns), BF),
+                pltpu.VMEM((seq_count, 2 * tokens), BF),
+                pltpu.VMEM((columns, seq_count), BF),
+                pltpu.SemaphoreType.DMA,
             ],
         ),
-        compiler_params=params(),
+        compiler_params=params(48),
         cost_estimate=pl.CostEstimate(flops=1100000000, bytes_accessed=9000000, transcendentals=0),
     )(
         vit_mine,
         vit_theirs,
         audio_tokens,
+        audio_theirs,
         weights.reshape(nz, nx, rows_w, columns),
-        places.reshape(1, -1),
-        text_rows[:, 0, :].T,
+        weights.reshape(nz, nx, rows_w, columns),
+        places,
+        text,
     )
     return result.T[:, None, :]
 

time: 148 us -> 144 us (0.973)
  blocking collectives: 63.4 us -> 58.8 us
  local copies, waits for them, and re-layouts: 5.52 us -> 3.26 us
  starting transfers between devices: 39.2 us -> 41 us
    all_to_all x1, blocking collectives: 25.5 us -> 20.5 us  [local(): incoming = lax.all_to_all(partial_sum, ('x', 'y'), 0, 0, tiled=True)]
    unnamed x22 -> x18, local copies, waits for them, and re-layouts: 3.05 us -> 0.85 us
    ppermute x3 -> x4, starting transfers between devices: 14.8 us -> 16.7 us  [swap(): return lax.ppermute(value, 'core', [(0, 1), (1, 0)])]
  transfers between devices with their start and end apart: 7 -> 8, of which waited for: 3 -> 3; matrix products, arithmetic and copies ran while one was open for 2% -> 2% of each run, Pallas kernels for 7% -> 8%
where the time goes in v4:
time: 144 us
  blocking collectives  58.8 us (41%)
  starting transfers between devices  41 us (28%)
  Pallas kernels  17.5 us (12%)
  between operations  13.7 us (10%)
  waiting for transfers between devices  8.33 us (6%)
  local copies, waits for them, and re-layouts  3.26 us (2%)
    all_to_all x1, blocking collectives, local(): incoming = lax.all_to_all(partial_sum, ('x', 'y'), 0, 0, tiled=True)  20.5 us
    ppermute x4, starting transfers between devices, swap(): return lax.ppermute(value, 'core', [(0, 1), (1, 0)])  16.7 us
    all_gather x1, blocking collectives, local(): video_y = lax.all_gather(video_pair, 'y', axis=0, tiled=False)  13.6 us
    all_gather x1, blocking collectives, local(): vit_mine = lax.all_gather(vit_out, 'y', axis=0, tiled=False)  12.5 us
    all_gather x1, blocking collectives, local(): cores = lax.all_gather(arrived, 'core', axis=0, tiled=False)  12.1 us
    all_to_all x1, starting transfers between devices, local(): block = lax.all_to_all(everywhere, 'x', 0, 0, tiled=True)  11.6 us
    all_to_all x1, starting transfers between devices, local(): lax.all_to_all(outgoing.reshape(nz, 16, width), 'z', 0, 0, tiled=True)  8.35 us
    pallas_call x1, Pallas kernels, local(): pl.pallas_call(tail_kernel, name='project_place', out_shape=jax.ShapeDtyp...  6.52 us
  transfers between devices with their start and end apart: 8, of which 3 were waited for; matrix products, arithmetic and copies ran while one was open for 2% of the time, Pallas kernels for 8%

profile of v4, /device:TPU:1, one launch (start us, length us, event | category | flops | bytes accessed | tf_op | source)
XLA Modules:
  0.0 143.9 jit_solution(4560576497802048417)
XLA Ops:
  6.5 0.7 slice.12
  7.2 4.4 %collective-permute-start = (bf16[1,128]{1,0:T(2,128)(2,1)S(1)}, bf16[1,128]{1,0:T(2,128)(2,1)S(1)}, u32[]{:S(2)}, u32[]{:S(2)}) collective-permute-start(bf16[1,128]{1,0:T(2,128)(2,1)S(1)} %slice.12), channel_id=1, source_target_pairs={{0,8},{8,16},{16,24},{24,32},{32,40},{40,48},{48,56},{56,64},{64,7... | collective-permute-start | bytes 776 | tf_op jit(solution)/shard_map/ppermute | solution.py:263
  11.6 0.9 pad_maximum_fusion
  12.5 0.8 stack.2
  13.3 11.6 %all-to-all-start = ((bf16[4,100,448]{2,1,0:T(8,128)(2,1)}), bf16[4,100,448]{2,1,0:T(8,128)(2,1)S(1)}, u32[]{:S(2)}, u32[]{:S(2)}) async-start(bf16[4,100,448]{2,1,0:T(8,128)(2,1)} %stack.2), calls=%async_computation | async-start | bytes 851968 | tf_op jit(solution)/shard_map/all_to_all | solution.py:268
  24.9 4.9 %prep.1 = bf16[256,640]{1,0:T(8,128)(2,1)} custom-call(s32[1,192]{1,0:T(1,128)} %bitcast.40, s32[1,192]{1,0:T(1,128)} %bitcast.41, s32[1,192]{1,0:T(1,128)} %bitcast.42, bf16[160,768]{1,0:T(8,128)(2,1)} %bitcast.43, bf16[600,128]{1,0:T(8,128)(2,1)} %mel_ref.1, bf16[1,128]{1,0:T(2,128)(2,1)} %copy-done.7, bf16[160,384]{1,0:T(8,128)(2,1)} %bitcast.44), custom_call_target="tpu_custom_call" | custom-call | flops 2000000000 | bytes 8000000 | tf_op jit(solution)/shard_map/prep/pallas_call | solution.py:280
  29.8 1.5 %all-to-all-done = bf16[4,100,448]{2,1,0:T(8,128)(2,1)S(1)} async-done(((bf16[4,100,448]{2,1,0:T(8,128)(2,1)}), bf16[4,100,448]{2,1,0:T(8,128)(2,1)S(1)}, u32[]{:S(2)}, u32[]{:S(2)}) %all-to-all-start) | async-done | bytes 358432 | tf_op jit(solution)/shard_map/all_to_all | solution.py:268
  31.3 0.8 copy-done.2
  32.1 8.3 %all-to-all-start.1 = ((bf16[16,16,640]{2,1,0:T(8,128)(2,1)}), bf16[16,16,640]{2,1,0:T(8,128)(2,1)S(1)}, u32[]{:S(2)}, u32[]{:S(2)}) async-start(bf16[16,16,640]{2,1,0:T(8,128)(2,1)} %bitcast.39), calls=%async_computation.1 | async-start | bytes 655360 | tf_op jit(solution)/shard_map/all_to_all | solution.py:298
  40.5 5.4 %collective-permute-start.1 = (bf16[1280,640]{1,0:T(8,128)(2,1)S(1)}, bf16[1280,640]{1,0:T(8,128)(2,1)}, u32[]{:S(2)}, u32[]{:S(2)}) collective-permute-start(bf16[1280,640]{1,0:T(8,128)(2,1)S(1)} %copy-done.1), channel_id=1, source_target_pairs={{0,1},{1,0},{2,3},{3,2},{4,5},{5,4},{6,7},{7,6},{8,9},{9,8},{10,11... | collective-permute-start | bytes 4915208 | tf_op jit(solution)/shard_map/ppermute | solution.py:34
  45.9 1.9 %collective-permute-start.2 = (bf16[640,1280]{1,0:T(8,128)(2,1)}, bf16[640,1280]{1,0:T(8,128)(2,1)}, u32[]{:S(2)}, u32[]{:S(2)}) collective-permute-start(bf16[640,1280]{1,0:T(8,128)(2,1)} %down0.1), channel_id=1, source_target_pairs={{0,1},{1,0},{2,3},{3,2},{4,5},{5,4},{6,7},{7,6},{8,9},{9,8},{10,11... | collective-permute-start | bytes 4915208 | tf_op jit(solution)/shard_map/ppermute | solution.py:34
  47.9 0.1 select_reduce_fusion
  48.1 0.1 reshape.41
  48.2 0.1 reshape.43
  48.4 0.1 reshape.42
  48.5 0.1 copy.25
  48.6 0.1 reshape.44
  48.7 0.1 pad_add_fusion
  48.8 5.1 %all-to-all-done.1 = bf16[16,16,640]{2,1,0:T(8,128)(2,1)S(1)} async-done(((bf16[16,16,640]{2,1,0:T(8,128)(2,1)}), bf16[16,16,640]{2,1,0:T(8,128)(2,1)S(1)}, u32[]{:S(2)}, u32[]{:S(2)}) %all-to-all-start.1) | async-done | bytes 327712 | tf_op jit(solution)/shard_map/all_to_all | solution.py:298
  53.9 12.1 %all-gather = bf16[32,16,640]{2,1,0:T(8,128)(2,1)S(1)} all-gather(bf16[16,16,640]{2,1,0:T(8,128)(2,1)S(1)} %all-to-all-done.1), channel_id=2, replica_groups=mesh['x'=4,'z'=16,'y'=4,'core'=2] {'core'}, dimensions={0}, use_global_device_ids=true | all-gather | bytes 983040 | tf_op jit(solution)/shard_map/all_gather | solution.py:323
  66.1 0.2 copy.27
  66.3 0.1 constant_dynamic-slice_fusion.1
  66.4 13.6 %all_gather.20.video_ref = bf16[4,2,96,640]{3,2,1,0:T(8,128)(2,1)S(1)} all-gather(bf16[1,2,96,640]{3,2,1,0:T(8,128)(2,1)S(1)} %copy.28), channel_id=1, replica_groups=mesh['x'=4,'z'=16,'y'=4,'core'=2] {'y'}, dimensions={0}, use_global_device_ids=true | all-gather | bytes 1228800 | tf_op jit(solution)/shard_map/all_gather | solution.py:327
  80.0 5.7 %vision.1 = bf16[16,32,1280]{2,1,0:T(8,128)(2,1)S(1)} custom-call(bf16[4,2,96,640]{3,2,1,0:T(8,128)(2,1)S(1)} %all_gather.20.video_ref, bf16[2,3,8,640]{3,2,1,0:T(8,128)(2,1)S(1)} %bitcast.31, bf16[1280,640]{1,0:T(8,128)(2,1)S(1)} %copy-done.1, bf16[640,1280]{1,0:T(8,128)(2,1)} %down0.1, bf16[1280,640]{1,0:T(8,128)(2,1)} %collective-permute-done.1.up1, ...), custom_call_target="tpu_custom_call" | custom-call | flops 2516582400 | bytes 9000000 | tf_op jit(solution)/shard_map/vision/pallas_call | solution.py:333
  85.8 20.5 %all_to_all.15.in_ref = bf16[16,32,1280]{2,1,0:T(8,128)(2,1)S(1)} all-to-all(bf16[16,32,1280]{2,1,0:T(8,128)(2,1)S(1)} %vision.1), channel_id=1, replica_groups=mesh['x'=4,'z'=16,'y'=4,'core'=2] {'x','y'}, dimensions={0} | all-to-all | bytes 2621440 | tf_op jit(solution)/shard_map/all_to_all | solution.py:349
  106.3 0.1 slice_reduce_fusion
  106.4 12.5 %all_gather.21.own_ref = bf16[4,96,1280]{2,1,0:T(8,128)(2,1)S(1)} all-gather(bf16[1,96,1280]{2,1,0:T(8,128)(2,1)S(1)} %bitcast.36), channel_id=1, replica_groups=mesh['x'=4,'z'=16,'y'=4,'core'=2] {'y'}, dimensions={0}, use_global_device_ids=true | all-gather | bytes 1228800 | tf_op jit(solution)/shard_map/all_gather | solution.py:361
  119.0 7.4 %collective-permute-start.3 = (bf16[4,96,1280]{2,1,0:T(8,128)(2,1)S(1)}, bf16[4,96,1280]{2,1,0:T(8,128)(2,1)S(1)}, u32[]{:S(2)}, u32[]{:S(2)}) collective-permute-start(bf16[4,96,1280]{2,1,0:T(8,128)(2,1)S(1)} %all_gather.21.own_ref), channel_id=1, source_target_pairs={{0,1},{1,0},{2,3},{3,2},{4,5},{5,4},{6,7},{7,6},{8,9},{9,8},{10,11... | collective-permute-start | bytes 2949128 | tf_op jit(solution)/shard_map/ppermute | solution.py:34
  126.4 0.4 audio_spread.1.audio_own_ref
  126.9 1.9 %collective-permute-start.4 = (bf16[4,96,512]{2,1,0:T(8,128)(2,1)S(1)}, bf16[4,96,512]{2,1,0:T(8,128)(2,1)S(1)}, u32[]{:S(2)}, u32[]{:S(2)}) collective-permute-start(bf16[4,96,512]{2,1,0:T(8,128)(2,1)S(1)} %audio_spread.1.audio_own_ref), channel_id=1, source_target_pairs={{0,1},{1,0},{2,3},{3,2},{4,5},{5,4},{6,7},{7,6},{8,9},{9,8},{10,11... | collective-permute-start | bytes 1179656 | tf_op jit(solution)/shard_map/ppermute | solution.py:34
  128.8 1.7 %collective-permute-done.4.audio_other_ref = bf16[4,96,512]{2,1,0:T(8,128)(2,1)S(1)} collective-permute-done((bf16[4,96,512]{2,1,0:T(8,128)(2,1)S(1)}, bf16[4,96,512]{2,1,0:T(8,128)(2,1)S(1)}, u32[]{:S(2)}, u32[]{:S(2)}) %collective-permute-start.4) | collective-permute-done | bytes 393248 | tf_op jit(solution)/shard_map/ppermute | solution.py:34
  130.5 6.5 %project_place.1 = bf16[448,512]{1,0:T(8,128)(2,1)} custom-call(bf16[4,96,1280]{2,1,0:T(8,128)(2,1)S(1)} %all_gather.21.own_ref, bf16[4,96,1280]{2,1,0:T(8,128)(2,1)S(1)} %collective-permute-done.3.other_ref, bf16[4,96,512]{2,1,0:T(8,128)(2,1)S(1)} %audio_spread.1.audio_own_ref, bf16[4,96,512]{2,1,0:T(8,128)(2,1)S(1)} %collective-permute-done.4.audio_other_ref, ...), custom_call_target="tpu_custom_call" | custom-call | flops 1100000000 | bytes 9000000 | tf_op jit(solution)/shard_map/project_place/pallas_call | solution.py:364
  (30 shorter events, 0.2 us)
Async XLA Ops:
  7.2 5.3 %collective-permute-start = (bf16[1,128]{1,0:T(2,128)(2,1)S(1)}, bf16[1,128]{1,0:T(2,128)(2,1)S(1)}, u32[]{:S(2)}, u32[]{:S(2)}) collective-permute-start(bf16[1,128]{1,0:T(2,128)(2,1)S(1)} %slice.12), channel_id=1, source_target_pairs={{0,8},{8,16},{16,24},{24,32},{32,40},{40,48},{48,56},{56,64},{64,7... | collective-permute-start | bytes 776 | tf_op jit(solution)/shard_map/ppermute | solution.py:263
  12.5 12.4 %copy-start.7 = (bf16[1,128]{1,0:T(2,128)(2,1)}, bf16[1,128]{1,0:T(2,128)(2,1)S(1)}, u32[]{:S(2)}) copy-start(bf16[1,128]{1,0:T(2,128)(2,1)S(1)} %collective-permute-done.rim_ref) | copy-start | bytes 772
  13.3 18.0 %all-to-all-start = ((bf16[4,100,448]{2,1,0:T(8,128)(2,1)}), bf16[4,100,448]{2,1,0:T(8,128)(2,1)S(1)}, u32[]{:S(2)}, u32[]{:S(2)}) async-start(bf16[4,100,448]{2,1,0:T(8,128)(2,1)} %stack.2), calls=%async_computation | async-start | bytes 851968 | tf_op jit(solution)/shard_map/all_to_all | solution.py:268
  24.9 105.6 %all-gather.4.cloned.1.call-start = ((), (), s32[]{:S(2)}) async-start(), calls=%async_computation.3 | async-start | bytes 7241728 | tf_op jit(solution)/shard_map/all_gather | solution.py:297
  24.9 15.6 %copy-start.1 = (bf16[1280,640]{1,0:T(8,128)(2,1)S(1)}, bf16[1280,640]{1,0:T(8,128)(2,1)}, u32[]{:S(2)}) copy-start(bf16[1280,640]{1,0:T(8,128)(2,1)} %up0.1) | copy-start | bytes 4915204
  24.9 23.0 %copy-start.3 = (s32[192]{0:T(256)S(1)}, s32[192]{0:T(256)}, u32[]{:S(2)}) copy-start(s32[192]{0:T(256)} %param.20) | copy-start | bytes 2308
  24.9 23.0 %copy-start.4 = (s32[192]{0:T(256)S(1)}, s32[192]{0:T(256)}, u32[]{:S(2)}) copy-start(s32[192]{0:T(256)} %param.21) | copy-start | bytes 2308
  24.9 23.1 %copy-start.5 = (s32[192]{0:T(256)S(1)}, s32[192]{0:T(256)}, u32[]{:S(2)}) copy-start(s32[192]{0:T(256)} %param.23) | copy-start | bytes 2308
  24.9 23.1 %copy-start.6 = (s32[192]{0:T(256)S(1)}, s32[192]{0:T(256)}, u32[]{:S(2)}) copy-start(s32[192]{0:T(256)} %param.22) | copy-start | bytes 2308
  31.3 0.8 copy-start.2
  32.1 21.8 %all-to-all-start.1 = ((bf16[16,16,640]{2,1,0:T(8,128)(2,1)}), bf16[16,16,640]{2,1,0:T(8,128)(2,1)S(1)}, u32[]{:S(2)}, u32[]{:S(2)}) async-start(bf16[16,16,640]{2,1,0:T(8,128)(2,1)} %bitcast.39), calls=%async_computation.1 | async-start | bytes 655360 | tf_op jit(solution)/shard_map/all_to_all | solution.py:298
  40.5 39.5 %collective-permute-start.1 = (bf16[1280,640]{1,0:T(8,128)(2,1)S(1)}, bf16[1280,640]{1,0:T(8,128)(2,1)}, u32[]{:S(2)}, u32[]{:S(2)}) collective-permute-start(bf16[1280,640]{1,0:T(8,128)(2,1)S(1)} %copy-done.1), channel_id=1, source_target_pairs={{0,1},{1,0},{2,3},{3,2},{4,5},{5,4},{6,7},{7,6},{8,9},{9,8},{10,11... | collective-permute-start | bytes 4915208 | tf_op jit(solution)/shard_map/ppermute | solution.py:34
  45.9 34.1 %collective-permute-start.2 = (bf16[640,1280]{1,0:T(8,128)(2,1)}, bf16[640,1280]{1,0:T(8,128)(2,1)}, u32[]{:S(2)}, u32[]{:S(2)}) collective-permute-start(bf16[640,1280]{1,0:T(8,128)(2,1)} %down0.1), channel_id=1, source_target_pairs={{0,1},{1,0},{2,3},{3,2},{4,5},{5,4},{6,7},{7,6},{8,9},{9,8},{10,11... | collective-permute-start | bytes 4915208 | tf_op jit(solution)/shard_map/ppermute | solution.py:34
  106.4 24.1 %copy-start = (bf16[512,1,448]{0,2,1:T(8,128)(2,1)S(1)}, bf16[512,1,448]{0,2,1:T(8,128)(2,1)}, u32[]{:S(2)}) copy-start(bf16[512,1,448]{0,2,1:T(8,128)(2,1)} %param.19) | copy-start | bytes 1376260
  119.0 11.5 %collective-permute-start.3 = (bf16[4,96,1280]{2,1,0:T(8,128)(2,1)S(1)}, bf16[4,96,1280]{2,1,0:T(8,128)(2,1)S(1)}, u32[]{:S(2)}, u32[]{:S(2)}) collective-permute-start(bf16[4,96,1280]{2,1,0:T(8,128)(2,1)S(1)} %all_gather.21.own_ref), channel_id=1, source_target_pairs={{0,1},{1,0},{2,3},{3,2},{4,5},{5,4},{6,7},{7,6},{8,9},{9,8},{10,11... | collective-permute-start | bytes 2949128 | tf_op jit(solution)/shard_map/ppermute | solution.py:34
  126.9 3.6 %collective-permute-start.4 = (bf16[4,96,512]{2,1,0:T(8,128)(2,1)S(1)}, bf16[4,96,512]{2,1,0:T(8,128)(2,1)S(1)}, u32[]{:S(2)}, u32[]{:S(2)}) collective-permute-start(bf16[4,96,512]{2,1,0:T(8,128)(2,1)S(1)} %audio_spread.1.audio_own_ref), channel_id=1, source_target_pairs={{0,1},{1,0},{2,3},{3,2},{4,5},{5,4},{6,7},{7,6},{8,9},{9,8},{10,11... | collective-permute-start | bytes 1179656 | tf_op jit(solution)/shard_map/ppermute | solution.py:34
Sparse Core Ops, SparseCore 0:
  32.2 95.2 all-gather.3

commit v5 on v4

--- a/solution.py
+++ b/solution.py
@@ -91,14 +91,6 @@
     start = of_kind(first)
     token = (kind << 6) + ((to_x * nz + far - start) & (VT - 1))
     target = jnp.where(is_video, token * 4, -8)
-    column = iota((rows, count), 1)
-    source = iota((block, width), 0)
-    place = iota((block, width), 1)
-    total = jnp.zeros((rows, width), F32)
-    for s in range(4):
-        picked = dot_nt(one_hot(column == target + s), patch).astype(BF)
-        total += dot(picked, one_hot(place == source + s * block))
-
     frames = mel_ref.shape[0] // 4
     wide_mel[...] = mel_ref[...].astype(F32)
     f0, f1, f2, f3 = (wide_mel[pl.ds(k, frames, stride=4), :] for k in range(4))
@@ -109,14 +101,15 @@
     even = dot_nt(before, c0) + dot_nt(f0, c1) + dot_nt(f1, c2)
     odd = dot_nt(f1, c0) + dot_nt(f2, c1) + dot_nt(f3, c2)
     pooled = (0.5 * (gelu(even) + gelu(odd))).astype(BF)
-    column = iota((rows, frames), 1)
     start = start + of_kind(kept)
+    is_audio = (slot >= videos) & (kind < spans)
+    patch_column, column = iota((rows, count), 1), iota((rows, frames), 1)
     for i in range(nx):
         index = jnp.minimum((i * nz + far - start) & (VT - 1), AT - 1) + kind * AT
-        index = jnp.where(is_video | (kind >= spans), -8, index)
-        picked = dot(one_hot(column == index), pooled).astype(BF)
-        total += dot(picked, one_hot(place == source + i * block))
-    out_ref[...] = total.astype(BF)
+        index = jnp.where(is_audio, index, -8)
+        video = dot_nt(one_hot(patch_column == target + i), patch)
+        audio = dot(one_hot(column == index), pooled)
+        out_ref[:, i * block : (i + 1) * block] = (video + audio).astype(BF)
 
 
 def vision_kernel(

time: 144 us -> 144 us (level)
  waiting for transfers between devices: 8.33 us -> 10.1 us
  Pallas kernels: 17.5 us -> 15.8 us
    pallas_call x1, Pallas kernels: 4.86 us -> 3.11 us  [local(): pl.pallas_call(prep_kernel, name='prep', out_shape=jax.ShapeDtypeStruct((...]
    all_to_all x1, waiting for transfers between devices: 1.52 us -> 3.26 us  [local(): block = lax.all_to_all(everywhere, 'x', 0, 0, tiled=True)]
  transfers between devices with their start and end apart: 8 -> 8, of which waited for: 3 -> 3; matrix products, arithmetic and copies ran while one was open for 2% -> 2% of each run, Pallas kernels for 8% -> 6%
where the time goes in v5:
time: 144 us; the launch traced here: 143 us
  blocking collectives  57.6 us (40%)
  starting transfers between devices  41.3 us (29%)
  Pallas kernels  15.8 us (11%)
  between operations  13.7 us (10%)
  waiting for transfers between devices  10.1 us (7%)
  local copies, waits for them, and re-layouts  3.26 us (2%)
    all_to_all x1, blocking collectives, local(): incoming = lax.all_to_all(partial_sum, ('x', 'y'), 0, 0, tiled=True)  19.5 us
    ppermute x4, starting transfers between devices, swap(): return lax.ppermute(value, 'core', [(0, 1), (1, 0)])  17 us
    all_gather x1, blocking collectives, local(): video_y = lax.all_gather(video_pair, 'y', axis=0, tiled=False)  13.6 us
    all_gather x1, blocking collectives, local(): vit_mine = lax.all_gather(vit_out, 'y', axis=0, tiled=False)  12.4 us
    all_gather x1, blocking collectives, local(): cores = lax.all_gather(arrived, 'core', axis=0, tiled=False)  12.1 us
    all_to_all x1, starting transfers between devices, local(): block = lax.all_to_all(everywhere, 'x', 0, 0, tiled=True)  11.6 us
    all_to_all x1, starting transfers between devices, local(): lax.all_to_all(outgoing.reshape(nz, 16, width), 'z', 0, 0, tiled=True)  8.35 us
    pallas_call x1, Pallas kernels, local(): pl.pallas_call(tail_kernel, name='project_place', out_shape=jax.ShapeDtyp...  6.52 us
  transfers between devices with their start and end apart: 8, of which 3 were waited for; matrix products, arithmetic and copies ran while one was open for 2% of the time, Pallas kernels for 6%

profile of v5, /device:TPU:1, one launch (start us, length us, event | category | flops | bytes accessed | tf_op | source)
XLA Modules:
  0.0 143.0 jit_solution(3792209163836758109)
XLA Ops:
  6.5 0.7 slice.12
  7.2 4.4 %collective-permute-start = (bf16[1,128]{1,0:T(2,128)(2,1)S(1)}, bf16[1,128]{1,0:T(2,128)(2,1)S(1)}, u32[]{:S(2)}, u32[]{:S(2)}) collective-permute-start(bf16[1,128]{1,0:T(2,128)(2,1)S(1)} %slice.12), channel_id=1, source_target_pairs={{0,8},{8,16},{16,24},{24,32},{32,40},{40,48},{48,56},{56,64},{64,7... | collective-permute-start | bytes 776 | tf_op jit(solution)/shard_map/ppermute | solution.py:256
  11.6 0.9 pad_maximum_fusion
  12.5 0.8 stack.2
  13.3 11.6 %all-to-all-start = ((bf16[4,100,448]{2,1,0:T(8,128)(2,1)}), bf16[4,100,448]{2,1,0:T(8,128)(2,1)S(1)}, u32[]{:S(2)}, u32[]{:S(2)}) async-start(bf16[4,100,448]{2,1,0:T(8,128)(2,1)} %stack.2), calls=%async_computation | async-start | bytes 851968 | tf_op jit(solution)/shard_map/all_to_all | solution.py:261
  24.9 3.1 %prep.1 = bf16[256,640]{1,0:T(8,128)(2,1)} custom-call(s32[1,192]{1,0:T(1,128)} %bitcast.40, s32[1,192]{1,0:T(1,128)} %bitcast.41, s32[1,192]{1,0:T(1,128)} %bitcast.42, bf16[160,768]{1,0:T(8,128)(2,1)} %bitcast.43, bf16[600,128]{1,0:T(8,128)(2,1)} %mel_ref.1, bf16[1,128]{1,0:T(2,128)(2,1)} %copy-done.7, bf16[160,384]{1,0:T(8,128)(2,1)} %bitcast.44), custom_call_target="tpu_custom_call" | custom-call | flops 2000000000 | bytes 8000000 | tf_op jit(solution)/shard_map/prep/pallas_call | solution.py:273
  28.1 3.3 %all-to-all-done = bf16[4,100,448]{2,1,0:T(8,128)(2,1)S(1)} async-done(((bf16[4,100,448]{2,1,0:T(8,128)(2,1)}), bf16[4,100,448]{2,1,0:T(8,128)(2,1)S(1)}, u32[]{:S(2)}, u32[]{:S(2)}) %all-to-all-start) | async-done | bytes 358432 | tf_op jit(solution)/shard_map/all_to_all | solution.py:261
  31.3 0.8 copy-done.2
  32.1 8.3 %all-to-all-start.1 = ((bf16[16,16,640]{2,1,0:T(8,128)(2,1)}), bf16[16,16,640]{2,1,0:T(8,128)(2,1)S(1)}, u32[]{:S(2)}, u32[]{:S(2)}) async-start(bf16[16,16,640]{2,1,0:T(8,128)(2,1)} %bitcast.39), calls=%async_computation.1 | async-start | bytes 655360 | tf_op jit(solution)/shard_map/all_to_all | solution.py:291
  40.5 5.4 %collective-permute-start.1 = (bf16[1280,640]{1,0:T(8,128)(2,1)S(1)}, bf16[1280,640]{1,0:T(8,128)(2,1)}, u32[]{:S(2)}, u32[]{:S(2)}) collective-permute-start(bf16[1280,640]{1,0:T(8,128)(2,1)S(1)} %copy-done.1), channel_id=1, source_target_pairs={{0,1},{1,0},{2,3},{3,2},{4,5},{5,4},{6,7},{7,6},{8,9},{9,8},{10,11... | collective-permute-start | bytes 4915208 | tf_op jit(solution)/shard_map/ppermute | solution.py:34
  45.9 1.9 %collective-permute-start.2 = (bf16[640,1280]{1,0:T(8,128)(2,1)}, bf16[640,1280]{1,0:T(8,128)(2,1)}, u32[]{:S(2)}, u32[]{:S(2)}) collective-permute-start(bf16[640,1280]{1,0:T(8,128)(2,1)} %down0.1), channel_id=1, source_target_pairs={{0,1},{1,0},{2,3},{3,2},{4,5},{5,4},{6,7},{7,6},{8,9},{9,8},{10,11... | collective-permute-start | bytes 4915208 | tf_op jit(solution)/shard_map/ppermute | solution.py:34
  47.9 0.1 select_reduce_fusion
  48.1 0.1 reshape.41
  48.2 0.1 reshape.43
  48.4 0.1 reshape.42
  48.5 0.1 copy.25
  48.6 0.1 reshape.44
  48.7 0.1 pad_add_fusion
  48.8 5.1 %all-to-all-done.1 = bf16[16,16,640]{2,1,0:T(8,128)(2,1)S(1)} async-done(((bf16[16,16,640]{2,1,0:T(8,128)(2,1)}), bf16[16,16,640]{2,1,0:T(8,128)(2,1)S(1)}, u32[]{:S(2)}, u32[]{:S(2)}) %all-to-all-start.1) | async-done | bytes 327712 | tf_op jit(solution)/shard_map/all_to_all | solution.py:291
  53.9 12.1 %all-gather = bf16[32,16,640]{2,1,0:T(8,128)(2,1)S(1)} all-gather(bf16[16,16,640]{2,1,0:T(8,128)(2,1)S(1)} %all-to-all-done.1), channel_id=2, replica_groups=mesh['x'=4,'z'=16,'y'=4,'core'=2] {'core'}, dimensions={0}, use_global_device_ids=true | all-gather | bytes 983040 | tf_op jit(solution)/shard_map/all_gather | solution.py:316
  66.1 0.2 copy.27
  66.3 0.1 constant_dynamic-slice_fusion.1
  66.4 13.6 %all_gather.20.video_ref = bf16[4,2,96,640]{3,2,1,0:T(8,128)(2,1)S(1)} all-gather(bf16[1,2,96,640]{3,2,1,0:T(8,128)(2,1)S(1)} %copy.28), channel_id=1, replica_groups=mesh['x'=4,'z'=16,'y'=4,'core'=2] {'y'}, dimensions={0}, use_global_device_ids=true | all-gather | bytes 1228800 | tf_op jit(solution)/shard_map/all_gather | solution.py:320
  80.0 5.7 %vision.1 = bf16[16,32,1280]{2,1,0:T(8,128)(2,1)S(1)} custom-call(bf16[4,2,96,640]{3,2,1,0:T(8,128)(2,1)S(1)} %all_gather.20.video_ref, bf16[2,3,8,640]{3,2,1,0:T(8,128)(2,1)S(1)} %bitcast.31, bf16[1280,640]{1,0:T(8,128)(2,1)S(1)} %copy-done.1, bf16[640,1280]{1,0:T(8,128)(2,1)} %down0.1, bf16[1280,640]{1,0:T(8,128)(2,1)} %collective-permute-done.1.up1, ...), custom_call_target="tpu_custom_call" | custom-call | flops 2516582400 | bytes 9000000 | tf_op jit(solution)/shard_map/vision/pallas_call | solution.py:326
  85.8 19.5 %all_to_all.15.in_ref = bf16[16,32,1280]{2,1,0:T(8,128)(2,1)S(1)} all-to-all(bf16[16,32,1280]{2,1,0:T(8,128)(2,1)S(1)} %vision.1), channel_id=1, replica_groups=mesh['x'=4,'z'=16,'y'=4,'core'=2] {'x','y'}, dimensions={0} | all-to-all | bytes 2621440 | tf_op jit(solution)/shard_map/all_to_all | solution.py:342
  105.2 0.1 slice_reduce_fusion
  105.4 12.4 %all_gather.21.own_ref = bf16[4,96,1280]{2,1,0:T(8,128)(2,1)S(1)} all-gather(bf16[1,96,1280]{2,1,0:T(8,128)(2,1)S(1)} %bitcast.36), channel_id=1, replica_groups=mesh['x'=4,'z'=16,'y'=4,'core'=2] {'y'}, dimensions={0}, use_global_device_ids=true | all-gather | bytes 1228800 | tf_op jit(solution)/shard_map/all_gather | solution.py:354
  117.8 7.7 %collective-permute-start.3 = (bf16[4,96,1280]{2,1,0:T(8,128)(2,1)S(1)}, bf16[4,96,1280]{2,1,0:T(8,128)(2,1)S(1)}, u32[]{:S(2)}, u32[]{:S(2)}) collective-permute-start(bf16[4,96,1280]{2,1,0:T(8,128)(2,1)S(1)} %all_gather.21.own_ref), channel_id=1, source_target_pairs={{0,1},{1,0},{2,3},{3,2},{4,5},{5,4},{6,7},{7,6},{8,9},{9,8},{10,11... | collective-permute-start | bytes 2949128 | tf_op jit(solution)/shard_map/ppermute | solution.py:34
  125.5 0.4 audio_spread.1.audio_own_ref
  126.0 1.9 %collective-permute-start.4 = (bf16[4,96,512]{2,1,0:T(8,128)(2,1)S(1)}, bf16[4,96,512]{2,1,0:T(8,128)(2,1)S(1)}, u32[]{:S(2)}, u32[]{:S(2)}) collective-permute-start(bf16[4,96,512]{2,1,0:T(8,128)(2,1)S(1)} %audio_spread.1.audio_own_ref), channel_id=1, source_target_pairs={{0,1},{1,0},{2,3},{3,2},{4,5},{5,4},{6,7},{7,6},{8,9},{9,8},{10,11... | collective-permute-start | bytes 1179656 | tf_op jit(solution)/shard_map/ppermute | solution.py:34
  127.9 1.7 %collective-permute-done.4.audio_other_ref = bf16[4,96,512]{2,1,0:T(8,128)(2,1)S(1)} collective-permute-done((bf16[4,96,512]{2,1,0:T(8,128)(2,1)S(1)}, bf16[4,96,512]{2,1,0:T(8,128)(2,1)S(1)}, u32[]{:S(2)}, u32[]{:S(2)}) %collective-permute-start.4) | collective-permute-done | bytes 393248 | tf_op jit(solution)/shard_map/ppermute | solution.py:34
  129.6 6.5 %project_place.1 = bf16[448,512]{1,0:T(8,128)(2,1)} custom-call(bf16[4,96,1280]{2,1,0:T(8,128)(2,1)S(1)} %all_gather.21.own_ref, bf16[4,96,1280]{2,1,0:T(8,128)(2,1)S(1)} %collective-permute-done.3.other_ref, bf16[4,96,512]{2,1,0:T(8,128)(2,1)S(1)} %audio_spread.1.audio_own_ref, bf16[4,96,512]{2,1,0:T(8,128)(2,1)S(1)} %collective-permute-done.4.audio_other_ref, ...), custom_call_target="tpu_custom_call" | custom-call | flops 1100000000 | bytes 9000000 | tf_op jit(solution)/shard_map/project_place/pallas_call | solution.py:357
  (30 shorter events, 0.2 us)
Async XLA Ops:
  7.2 5.3 %collective-permute-start = (bf16[1,128]{1,0:T(2,128)(2,1)S(1)}, bf16[1,128]{1,0:T(2,128)(2,1)S(1)}, u32[]{:S(2)}, u32[]{:S(2)}) collective-permute-start(bf16[1,128]{1,0:T(2,128)(2,1)S(1)} %slice.12), channel_id=1, source_target_pairs={{0,8},{8,16},{16,24},{24,32},{32,40},{40,48},{48,56},{56,64},{64,7... | collective-permute-start | bytes 776 | tf_op jit(solution)/shard_map/ppermute | solution.py:256
  12.5 12.4 %copy-start.7 = (bf16[1,128]{1,0:T(2,128)(2,1)}, bf16[1,128]{1,0:T(2,128)(2,1)S(1)}, u32[]{:S(2)}) copy-start(bf16[1,128]{1,0:T(2,128)(2,1)S(1)} %collective-permute-done.rim_ref) | copy-start | bytes 772
  13.3 18.0 %all-to-all-start = ((bf16[4,100,448]{2,1,0:T(8,128)(2,1)}), bf16[4,100,448]{2,1,0:T(8,128)(2,1)S(1)}, u32[]{:S(2)}, u32[]{:S(2)}) async-start(bf16[4,100,448]{2,1,0:T(8,128)(2,1)} %stack.2), calls=%async_computation | async-start | bytes 851968 | tf_op jit(solution)/shard_map/all_to_all | solution.py:261
  24.9 104.7 %all-gather.4.cloned.1.call-start = ((), (), s32[]{:S(2)}) async-start(), calls=%async_computation.3 | async-start | bytes 7241728 | tf_op jit(solution)/shard_map/all_gather | solution.py:290
  24.9 15.6 %copy-start.1 = (bf16[1280,640]{1,0:T(8,128)(2,1)S(1)}, bf16[1280,640]{1,0:T(8,128)(2,1)}, u32[]{:S(2)}) copy-start(bf16[1280,640]{1,0:T(8,128)(2,1)} %up0.1) | copy-start | bytes 4915204
  24.9 23.0 %copy-start.3 = (s32[192]{0:T(256)S(1)}, s32[192]{0:T(256)}, u32[]{:S(2)}) copy-start(s32[192]{0:T(256)} %param.20) | copy-start | bytes 2308
  24.9 23.0 %copy-start.4 = (s32[192]{0:T(256)S(1)}, s32[192]{0:T(256)}, u32[]{:S(2)}) copy-start(s32[192]{0:T(256)} %param.21) | copy-start | bytes 2308
  24.9 23.1 %copy-start.5 = (s32[192]{0:T(256)S(1)}, s32[192]{0:T(256)}, u32[]{:S(2)}) copy-start(s32[192]{0:T(256)} %param.23) | copy-start | bytes 2308
  24.9 23.1 %copy-start.6 = (s32[192]{0:T(256)S(1)}, s32[192]{0:T(256)}, u32[]{:S(2)}) copy-start(s32[192]{0:T(256)} %param.22) | copy-start | bytes 2308
  31.3 0.8 copy-start.2
  32.1 21.8 %all-to-all-start.1 = ((bf16[16,16,640]{2,1,0:T(8,128)(2,1)}), bf16[16,16,640]{2,1,0:T(8,128)(2,1)S(1)}, u32[]{:S(2)}, u32[]{:S(2)}) async-start(bf16[16,16,640]{2,1,0:T(8,128)(2,1)} %bitcast.39), calls=%async_computation.1 | async-start | bytes 655360 | tf_op jit(solution)/shard_map/all_to_all | solution.py:291
  40.5 39.5 %collective-permute-start.1 = (bf16[1280,640]{1,0:T(8,128)(2,1)S(1)}, bf16[1280,640]{1,0:T(8,128)(2,1)}, u32[]{:S(2)}, u32[]{:S(2)}) collective-permute-start(bf16[1280,640]{1,0:T(8,128)(2,1)S(1)} %copy-done.1), channel_id=1, source_target_pairs={{0,1},{1,0},{2,3},{3,2},{4,5},{5,4},{6,7},{7,6},{8,9},{9,8},{10,11... | collective-permute-start | bytes 4915208 | tf_op jit(solution)/shard_map/ppermute | solution.py:34
  45.9 34.1 %collective-permute-start.2 = (bf16[640,1280]{1,0:T(8,128)(2,1)}, bf16[640,1280]{1,0:T(8,128)(2,1)}, u32[]{:S(2)}, u32[]{:S(2)}) collective-permute-start(bf16[640,1280]{1,0:T(8,128)(2,1)} %down0.1), channel_id=1, source_target_pairs={{0,1},{1,0},{2,3},{3,2},{4,5},{5,4},{6,7},{7,6},{8,9},{9,8},{10,11... | collective-permute-start | bytes 4915208 | tf_op jit(solution)/shard_map/ppermute | solution.py:34
  105.4 24.2 %copy-start = (bf16[512,1,448]{0,2,1:T(8,128)(2,1)S(1)}, bf16[512,1,448]{0,2,1:T(8,128)(2,1)}, u32[]{:S(2)}) copy-start(bf16[512,1,448]{0,2,1:T(8,128)(2,1)} %param.19) | copy-start | bytes 1376260
  117.8 11.8 %collective-permute-start.3 = (bf16[4,96,1280]{2,1,0:T(8,128)(2,1)S(1)}, bf16[4,96,1280]{2,1,0:T(8,128)(2,1)S(1)}, u32[]{:S(2)}, u32[]{:S(2)}) collective-permute-start(bf16[4,96,1280]{2,1,0:T(8,128)(2,1)S(1)} %all_gather.21.own_ref), channel_id=1, source_target_pairs={{0,1},{1,0},{2,3},{3,2},{4,5},{5,4},{6,7},{7,6},{8,9},{9,8},{10,11... | collective-permute-start | bytes 2949128 | tf_op jit(solution)/shard_map/ppermute | solution.py:34
  126.0 3.6 %collective-permute-start.4 = (bf16[4,96,512]{2,1,0:T(8,128)(2,1)S(1)}, bf16[4,96,512]{2,1,0:T(8,128)(2,1)S(1)}, u32[]{:S(2)}, u32[]{:S(2)}) collective-permute-start(bf16[4,96,512]{2,1,0:T(8,128)(2,1)S(1)} %audio_spread.1.audio_own_ref), channel_id=1, source_target_pairs={{0,1},{1,0},{2,3},{3,2},{4,5},{5,4},{6,7},{7,6},{8,9},{9,8},{10,11... | collective-permute-start | bytes 1179656 | tf_op jit(solution)/shard_map/ppermute | solution.py:34
Sparse Core Ops, SparseCore 0:
  32.2 95.2 all-gather.3

commit v6 on v5

--- a/solution.py
+++ b/solution.py
@@ -257,7 +257,6 @@
 
     own = jnp.concatenate([merger, audio_proj], axis=0)
     everywhere = jnp.stack([own] * nx)
-    rim, everywhere = lax.optimization_barrier((rim, everywhere))
     block = lax.all_to_all(everywhere, "x", 0, 0, tiled=True)
 
     starts = span_starts(span_order, offsets)

time: 144 us -> 144 us (level)
  blocking collectives: 57.6 us -> 59.8 us
    all_to_all x1, starting transfers between devices: 8.35 us -> 16.5 us  [local(): lax.all_to_all(outgoing.reshape(nz, 16, width), 'z', 0, 0, tiled=True)]
    all_to_all x1, starting transfers between devices: 11.6 us -> 4.84 us  [local(): block = lax.all_to_all(everywhere, 'x', 0, 0, tiled=True)]
    all_to_all x1, waiting for transfers between devices: 3.26 us -> 0.01 us  [local(): block = lax.all_to_all(everywhere, 'x', 0, 0, tiled=True)]
    all_to_all x1, blocking collectives: 19.5 us -> 22 us  [local(): incoming = lax.all_to_all(partial_sum, ('x', 'y'), 0, 0, tiled=True)]
    all_to_all x1, waiting for transfers between devices: 5.1 us -> 6.83 us  [local(): lax.all_to_all(outgoing.reshape(nz, 16, width), 'z', 0, 0, tiled=True)]
    ppermute x4, starting transfers between devices: 17 us -> 15.4 us  [swap(): return lax.ppermute(value, 'core', [(0, 1), (1, 0)])]
  transfers between devices with their start and end apart: 8 -> 8, of which waited for: 3 -> 3; matrix products, arithmetic and copies ran while one was open for 2% -> 1% of each run, Pallas kernels for 6% -> 6%
where the time goes in v6:
time: 144 us
  blocking collectives  59.8 us (42%)
  starting transfers between devices  40.3 us (28%)
  Pallas kernels  15.8 us (11%)
  between operations  13.6 us (9%)
  waiting for transfers between devices  9.25 us (6%)
  local copies, waits for them, and re-layouts  3.78 us (3%)
    all_to_all x1, blocking collectives, local(): incoming = lax.all_to_all(partial_sum, ('x', 'y'), 0, 0, tiled=True)  22 us
    all_to_all x1, starting transfers between devices, local(): lax.all_to_all(outgoing.reshape(nz, 16, width), 'z', 0, 0, tiled=True)  16.5 us
    ppermute x4, starting transfers between devices, swap(): return lax.ppermute(value, 'core', [(0, 1), (1, 0)])  15.4 us
    all_gather x1, blocking collectives, local(): video_y = lax.all_gather(video_pair, 'y', axis=0, tiled=False)  13.5 us
    all_gather x1, blocking collectives, local(): vit_mine = lax.all_gather(vit_out, 'y', axis=0, tiled=False)  12.5 us
    all_gather x1, blocking collectives, local(): cores = lax.all_gather(arrived, 'core', axis=0, tiled=False)  11.7 us
    all_to_all x1, waiting for transfers between devices, local(): lax.all_to_all(outgoing.reshape(nz, 16, width), 'z', 0, 0, tiled=True)  6.83 us
    pallas_call x1, Pallas kernels, local(): pl.pallas_call(tail_kernel, name='project_place', out_shape=jax.ShapeDtyp...  6.52 us
  transfers between devices with their start and end apart: 8, of which 3 were waited for; matrix products, arithmetic and copies ran while one was open for 1% of the time, Pallas kernels for 6%

profile of v6, /device:TPU:1, one launch (start us, length us, event | category | flops | bytes accessed | tf_op | source)
XLA Modules:
  0.0 143.8 jit_solution(7760202887642871945)
XLA Ops:
  6.5 0.9 pad_maximum_fusion
  7.5 0.8 stack.2
  8.2 4.8 %all-to-all-start = ((bf16[4,100,448]{2,1,0:T(8,128)(2,1)}), bf16[4,100,448]{2,1,0:T(8,128)(2,1)S(1)}, u32[]{:S(2)}, u32[]{:S(2)}) async-start(bf16[4,100,448]{2,1,0:T(8,128)(2,1)} %stack.2), calls=%async_computation | async-start | bytes 851968 | tf_op jit(solution)/shard_map/all_to_all | solution.py:260
  13.1 0.7 slice.12
  13.8 3.5 %collective-permute-start = (bf16[1,128]{1,0:T(2,128)(2,1)S(1)}, bf16[1,128]{1,0:T(2,128)(2,1)S(1)}, u32[]{:S(2)}, u32[]{:S(2)}) collective-permute-start(bf16[1,128]{1,0:T(2,128)(2,1)S(1)} %slice.12), channel_id=1, source_target_pairs={{0,8},{8,16},{16,24},{24,32},{32,40},{40,48},{48,56},{56,64},{64,7... | collective-permute-start | bytes 776 | tf_op jit(solution)/shard_map/ppermute | solution.py:256
  17.3 0.7 collective-permute-done.rim_ref
  18.0 0.5 copy-done.7
  18.6 3.1 %prep.1 = bf16[256,640]{1,0:T(8,128)(2,1)} custom-call(s32[1,192]{1,0:T(1,128)} %bitcast.40, s32[1,192]{1,0:T(1,128)} %bitcast.41, s32[1,192]{1,0:T(1,128)} %bitcast.42, bf16[160,768]{1,0:T(8,128)(2,1)} %bitcast.43, bf16[600,128]{1,0:T(8,128)(2,1)} %mel_ref.1, bf16[1,128]{1,0:T(2,128)(2,1)} %copy-done.7, bf16[160,384]{1,0:T(8,128)(2,1)} %bitcast.44), custom_call_target="tpu_custom_call" | custom-call | flops 2000000000 | bytes 8000000 | tf_op jit(solution)/shard_map/prep/pallas_call | solution.py:272
  21.7 0.8 copy-done.2
  22.5 16.5 %all-to-all-start.1 = ((bf16[16,16,640]{2,1,0:T(8,128)(2,1)}), bf16[16,16,640]{2,1,0:T(8,128)(2,1)S(1)}, u32[]{:S(2)}, u32[]{:S(2)}) async-start(bf16[16,16,640]{2,1,0:T(8,128)(2,1)} %bitcast.39), calls=%async_computation.1 | async-start | bytes 655360 | tf_op jit(solution)/shard_map/all_to_all | solution.py:290
  39.0 4.0 %collective-permute-start.1 = (bf16[1280,640]{1,0:T(8,128)(2,1)S(1)}, bf16[1280,640]{1,0:T(8,128)(2,1)}, u32[]{:S(2)}, u32[]{:S(2)}) collective-permute-start(bf16[1280,640]{1,0:T(8,128)(2,1)S(1)} %copy-done.1), channel_id=1, source_target_pairs={{0,1},{1,0},{2,3},{3,2},{4,5},{5,4},{6,7},{7,6},{8,9},{9,8},{10,11... | collective-permute-start | bytes 4915208 | tf_op jit(solution)/shard_map/ppermute | solution.py:34
  43.0 1.9 %collective-permute-start.2 = (bf16[640,1280]{1,0:T(8,128)(2,1)}, bf16[640,1280]{1,0:T(8,128)(2,1)}, u32[]{:S(2)}, u32[]{:S(2)}) collective-permute-start(bf16[640,1280]{1,0:T(8,128)(2,1)} %down0.1), channel_id=1, source_target_pairs={{0,1},{1,0},{2,3},{3,2},{4,5},{5,4},{6,7},{7,6},{8,9},{9,8},{10,11... | collective-permute-start | bytes 4915208 | tf_op jit(solution)/shard_map/ppermute | solution.py:34
  44.9 0.1 select_reduce_fusion
  45.1 0.1 reshape.41
  45.2 0.1 reshape.43
  45.4 0.1 reshape.42
  45.6 0.1 copy.25
  45.7 0.1 reshape.44
  45.8 0.1 pad_add_fusion
  45.9 6.8 %all-to-all-done.1 = bf16[16,16,640]{2,1,0:T(8,128)(2,1)S(1)} async-done(((bf16[16,16,640]{2,1,0:T(8,128)(2,1)}), bf16[16,16,640]{2,1,0:T(8,128)(2,1)S(1)}, u32[]{:S(2)}, u32[]{:S(2)}) %all-to-all-start.1) | async-done | bytes 327712 | tf_op jit(solution)/shard_map/all_to_all | solution.py:290
  52.7 11.7 %all-gather = bf16[32,16,640]{2,1,0:T(8,128)(2,1)S(1)} all-gather(bf16[16,16,640]{2,1,0:T(8,128)(2,1)S(1)} %all-to-all-done.1), channel_id=2, replica_groups=mesh['x'=4,'z'=16,'y'=4,'core'=2] {'core'}, dimensions={0}, use_global_device_ids=true | all-gather | bytes 983040 | tf_op jit(solution)/shard_map/all_gather | solution.py:315
  64.5 0.2 copy.27
  64.8 13.5 %all_gather.20.video_ref = bf16[4,2,96,640]{3,2,1,0:T(8,128)(2,1)S(1)} all-gather(bf16[1,2,96,640]{3,2,1,0:T(8,128)(2,1)S(1)} %copy.28), channel_id=1, replica_groups=mesh['x'=4,'z'=16,'y'=4,'core'=2] {'y'}, dimensions={0}, use_global_device_ids=true | all-gather | bytes 1228800 | tf_op jit(solution)/shard_map/all_gather | solution.py:319
  78.4 5.7 %vision.1 = bf16[16,32,1280]{2,1,0:T(8,128)(2,1)S(1)} custom-call(bf16[4,2,96,640]{3,2,1,0:T(8,128)(2,1)S(1)} %all_gather.20.video_ref, bf16[2,3,8,640]{3,2,1,0:T(8,128)(2,1)S(1)} %bitcast.31, bf16[1280,640]{1,0:T(8,128)(2,1)S(1)} %copy-done.1, bf16[640,1280]{1,0:T(8,128)(2,1)} %down0.1, bf16[1280,640]{1,0:T(8,128)(2,1)} %collective-permute-done.1.up1, ...), custom_call_target="tpu_custom_call" | custom-call | flops 2516582400 | bytes 9000000 | tf_op jit(solution)/shard_map/vision/pallas_call | solution.py:325
  84.1 22.0 %all_to_all.15.in_ref = bf16[16,32,1280]{2,1,0:T(8,128)(2,1)S(1)} all-to-all(bf16[16,32,1280]{2,1,0:T(8,128)(2,1)S(1)} %vision.1), channel_id=1, replica_groups=mesh['x'=4,'z'=16,'y'=4,'core'=2] {'x','y'}, dimensions={0} | all-to-all | bytes 2621440 | tf_op jit(solution)/shard_map/all_to_all | solution.py:341
  106.1 0.1 slice_reduce_fusion
  106.3 12.5 %all_gather.21.own_ref = bf16[4,96,1280]{2,1,0:T(8,128)(2,1)S(1)} all-gather(bf16[1,96,1280]{2,1,0:T(8,128)(2,1)S(1)} %bitcast.36), channel_id=1, replica_groups=mesh['x'=4,'z'=16,'y'=4,'core'=2] {'y'}, dimensions={0}, use_global_device_ids=true | all-gather | bytes 1228800 | tf_op jit(solution)/shard_map/all_gather | solution.py:353
  118.8 7.6 %collective-permute-start.3 = (bf16[4,96,1280]{2,1,0:T(8,128)(2,1)S(1)}, bf16[4,96,1280]{2,1,0:T(8,128)(2,1)S(1)}, u32[]{:S(2)}, u32[]{:S(2)}) collective-permute-start(bf16[4,96,1280]{2,1,0:T(8,128)(2,1)S(1)} %all_gather.21.own_ref), channel_id=1, source_target_pairs={{0,1},{1,0},{2,3},{3,2},{4,5},{5,4},{6,7},{7,6},{8,9},{9,8},{10,11... | collective-permute-start | bytes 2949128 | tf_op jit(solution)/shard_map/ppermute | solution.py:34
  126.4 0.4 audio_spread.1.audio_own_ref
  126.8 1.9 %collective-permute-start.4 = (bf16[4,96,512]{2,1,0:T(8,128)(2,1)S(1)}, bf16[4,96,512]{2,1,0:T(8,128)(2,1)S(1)}, u32[]{:S(2)}, u32[]{:S(2)}) collective-permute-start(bf16[4,96,512]{2,1,0:T(8,128)(2,1)S(1)} %audio_spread.1.audio_own_ref), channel_id=1, source_target_pairs={{0,1},{1,0},{2,3},{3,2},{4,5},{5,4},{6,7},{7,6},{8,9},{9,8},{10,11... | collective-permute-start | bytes 1179656 | tf_op jit(solution)/shard_map/ppermute | solution.py:34
  128.7 1.7 %collective-permute-done.4.audio_other_ref = bf16[4,96,512]{2,1,0:T(8,128)(2,1)S(1)} collective-permute-done((bf16[4,96,512]{2,1,0:T(8,128)(2,1)S(1)}, bf16[4,96,512]{2,1,0:T(8,128)(2,1)S(1)}, u32[]{:S(2)}, u32[]{:S(2)}) %collective-permute-start.4) | collective-permute-done | bytes 393248 | tf_op jit(solution)/shard_map/ppermute | solution.py:34
  130.4 6.5 %project_place.1 = bf16[448,512]{1,0:T(8,128)(2,1)} custom-call(bf16[4,96,1280]{2,1,0:T(8,128)(2,1)S(1)} %all_gather.21.own_ref, bf16[4,96,1280]{2,1,0:T(8,128)(2,1)S(1)} %collective-permute-done.3.other_ref, bf16[4,96,512]{2,1,0:T(8,128)(2,1)S(1)} %audio_spread.1.audio_own_ref, bf16[4,96,512]{2,1,0:T(8,128)(2,1)S(1)} %collective-permute-done.4.audio_other_ref, ...), custom_call_target="tpu_custom_call" | custom-call | flops 1100000000 | bytes 9000000 | tf_op jit(solution)/shard_map/project_place/pallas_call | solution.py:356
  (30 shorter events, 0.3 us)
Async XLA Ops:
  8.2 13.5 %all-to-all-start = ((bf16[4,100,448]{2,1,0:T(8,128)(2,1)}), bf16[4,100,448]{2,1,0:T(8,128)(2,1)S(1)}, u32[]{:S(2)}, u32[]{:S(2)}) async-start(bf16[4,100,448]{2,1,0:T(8,128)(2,1)} %stack.2), calls=%async_computation | async-start | bytes 851968 | tf_op jit(solution)/shard_map/all_to_all | solution.py:260
  13.1 117.3 %all-gather.4.cloned.1.call-start = ((), (), s32[]{:S(2)}) async-start(), calls=%async_computation.3 | async-start | bytes 7241728 | tf_op jit(solution)/shard_map/all_gather | solution.py:289
  13.8 4.2 %collective-permute-start = (bf16[1,128]{1,0:T(2,128)(2,1)S(1)}, bf16[1,128]{1,0:T(2,128)(2,1)S(1)}, u32[]{:S(2)}, u32[]{:S(2)}) collective-permute-start(bf16[1,128]{1,0:T(2,128)(2,1)S(1)} %slice.12), channel_id=1, source_target_pairs={{0,8},{8,16},{16,24},{24,32},{32,40},{40,48},{48,56},{56,64},{64,7... | collective-permute-start | bytes 776 | tf_op jit(solution)/shard_map/ppermute | solution.py:256
  18.0 0.5 copy-start.7
  18.5 20.4 %copy-start.1 = (bf16[1280,640]{1,0:T(8,128)(2,1)S(1)}, bf16[1280,640]{1,0:T(8,128)(2,1)}, u32[]{:S(2)}) copy-start(bf16[1280,640]{1,0:T(8,128)(2,1)} %up0.1) | copy-start | bytes 4915204
  18.6 26.4 %copy-start.3 = (s32[192]{0:T(256)S(1)}, s32[192]{0:T(256)}, u32[]{:S(2)}) copy-start(s32[192]{0:T(256)} %param.20) | copy-start | bytes 2308
  18.6 26.4 %copy-start.4 = (s32[192]{0:T(256)S(1)}, s32[192]{0:T(256)}, u32[]{:S(2)}) copy-start(s32[192]{0:T(256)} %param.21) | copy-start | bytes 2308
  18.6 26.5 %copy-start.5 = (s32[192]{0:T(256)S(1)}, s32[192]{0:T(256)}, u32[]{:S(2)}) copy-start(s32[192]{0:T(256)} %param.23) | copy-start | bytes 2308
  18.6 26.5 %copy-start.6 = (s32[192]{0:T(256)S(1)}, s32[192]{0:T(256)}, u32[]{:S(2)}) copy-start(s32[192]{0:T(256)} %param.22) | copy-start | bytes 2308
  21.7 0.8 copy-start.2
  22.5 30.2 %all-to-all-start.1 = ((bf16[16,16,640]{2,1,0:T(8,128)(2,1)}), bf16[16,16,640]{2,1,0:T(8,128)(2,1)S(1)}, u32[]{:S(2)}, u32[]{:S(2)}) async-start(bf16[16,16,640]{2,1,0:T(8,128)(2,1)} %bitcast.39), calls=%async_computation.1 | async-start | bytes 655360 | tf_op jit(solution)/shard_map/all_to_all | solution.py:290
  39.0 39.4 %collective-permute-start.1 = (bf16[1280,640]{1,0:T(8,128)(2,1)S(1)}, bf16[1280,640]{1,0:T(8,128)(2,1)}, u32[]{:S(2)}, u32[]{:S(2)}) collective-permute-start(bf16[1280,640]{1,0:T(8,128)(2,1)S(1)} %copy-done.1), channel_id=1, source_target_pairs={{0,1},{1,0},{2,3},{3,2},{4,5},{5,4},{6,7},{7,6},{8,9},{9,8},{10,11... | collective-permute-start | bytes 4915208 | tf_op jit(solution)/shard_map/ppermute | solution.py:34
  43.0 35.4 %collective-permute-start.2 = (bf16[640,1280]{1,0:T(8,128)(2,1)}, bf16[640,1280]{1,0:T(8,128)(2,1)}, u32[]{:S(2)}, u32[]{:S(2)}) collective-permute-start(bf16[640,1280]{1,0:T(8,128)(2,1)} %down0.1), channel_id=1, source_target_pairs={{0,1},{1,0},{2,3},{3,2},{4,5},{5,4},{6,7},{7,6},{8,9},{9,8},{10,11... | collective-permute-start | bytes 4915208 | tf_op jit(solution)/shard_map/ppermute | solution.py:34
  106.3 24.1 %copy-start = (bf16[512,1,448]{0,2,1:T(8,128)(2,1)S(1)}, bf16[512,1,448]{0,2,1:T(8,128)(2,1)}, u32[]{:S(2)}) copy-start(bf16[512,1,448]{0,2,1:T(8,128)(2,1)} %param.19) | copy-start | bytes 1376260
  118.8 11.6 %collective-permute-start.3 = (bf16[4,96,1280]{2,1,0:T(8,128)(2,1)S(1)}, bf16[4,96,1280]{2,1,0:T(8,128)(2,1)S(1)}, u32[]{:S(2)}, u32[]{:S(2)}) collective-permute-start(bf16[4,96,1280]{2,1,0:T(8,128)(2,1)S(1)} %all_gather.21.own_ref), channel_id=1, source_target_pairs={{0,1},{1,0},{2,3},{3,2},{4,5},{5,4},{6,7},{7,6},{8,9},{9,8},{10,11... | collective-permute-start | bytes 2949128 | tf_op jit(solution)/shard_map/ppermute | solution.py:34
  126.8 3.6 %collective-permute-start.4 = (bf16[4,96,512]{2,1,0:T(8,128)(2,1)S(1)}, bf16[4,96,512]{2,1,0:T(8,128)(2,1)S(1)}, u32[]{:S(2)}, u32[]{:S(2)}) collective-permute-start(bf16[4,96,512]{2,1,0:T(8,128)(2,1)S(1)} %audio_spread.1.audio_own_ref), channel_id=1, source_target_pairs={{0,1},{1,0},{2,3},{3,2},{4,5},{5,4},{6,7},{7,6},{8,9},{9,8},{10,11... | collective-permute-start | bytes 1179656 | tf_op jit(solution)/shard_map/ppermute | solution.py:34
Sparse Core Ops, SparseCore 0:
  22.6 103.2 all-gather.3

commit v7 on v5

--- a/solution.py
+++ b/solution.py
@@ -177,8 +177,7 @@
     other_ref,
     audio_own_ref,
     audio_other_ref,
-    low_ref,
-    high_ref,
+    weight_ref,
     place_ref,
     text_ref,
     out_ref,
@@ -200,19 +199,13 @@
         spread[...] = jnp.zeros_like(spread)
         marks[...] = one_hot(place_ref[...] == iota(marks.shape, 0))
 
-    near, _, rows, columns = low_ref.shape
+    nz, _, rows, columns = weight_ref.shape
     rows_a = rows // 5
     rows_m = rows - rows_a
     both = jnp.concatenate([own_ref[0], other_ref[0]], axis=0)
-    depth = near * rows_m
-    total = video[...]
-    for i, ref in enumerate((low_ref, high_ref)):
-        merge_w = ref[:, 0, :rows_m, :].reshape(depth, columns)
-        total += dot(both[:, i * depth : (i + 1) * depth], merge_w)
-        for z in range(near):
-            a = (i * near + z) * PAD_A
-            spread[a : a + rows_a, :] = ref[z, 0, rows_m:, :]
-    video[...] = total
+    video[...] += dot(both, weight_ref[:, 0, :rows_m, :].reshape(nz * rows_m, columns))
+    for z in range(nz):
+        spread[z * PAD_A : z * PAD_A + rows_a, :] = weight_ref[z, 0, rows_m:, :]
     tokens = jnp.concatenate([audio_own_ref[0], audio_other_ref[0]], axis=0)
     audio[...] += dot(tokens, spread[...])
 
@@ -365,8 +358,7 @@
                 pl.BlockSpec((1, half, full), lambda s: (s, 0, 0)),
                 pl.BlockSpec((1, half, nz * PAD_A), lambda s: (s, 0, 0)),
                 pl.BlockSpec((1, half, nz * PAD_A), lambda s: (s, 0, 0)),
-                pl.BlockSpec((half_z, 1, rows_w, columns), lambda s: (0, s, 0, 0)),
-                pl.BlockSpec((half_z, 1, rows_w, columns), lambda s: (1, s, 0, 0)),
+                pl.BlockSpec((nz, 1, rows_w, columns), lambda s: (0, s, 0, 0)),
                 whole((1, 2 * tokens)),
                 ANY,
             ],
@@ -388,7 +380,6 @@
         audio_tokens,
         audio_theirs,
         weights.reshape(nz, nx, rows_w, columns),
-        weights.reshape(nz, nx, rows_w, columns),
         places,
         text,
     )

time: 144 us -> 143 us (level)
  no operation moved by 1% of the time
where the time goes in v7:
time: 143 us
  blocking collectives  57.6 us (40%)
  starting transfers between devices  41.3 us (29%)
  Pallas kernels  15.7 us (11%)
  between operations  13.7 us (10%)
  waiting for transfers between devices  10.1 us (7%)
  local copies, waits for them, and re-layouts  3.26 us (2%)
    all_to_all x1, blocking collectives, local(): incoming = lax.all_to_all(partial_sum, ('x', 'y'), 0, 0, tiled=True)  19.5 us
    ppermute x4, starting transfers between devices, swap(): return lax.ppermute(value, 'core', [(0, 1), (1, 0)])  17 us
    all_gather x1, blocking collectives, local(): video_y = lax.all_gather(video_pair, 'y', axis=0, tiled=False)  13.6 us
    all_gather x1, blocking collectives, local(): vit_mine = lax.all_gather(vit_out, 'y', axis=0, tiled=False)  12.4 us
    all_gather x1, blocking collectives, local(): cores = lax.all_gather(arrived, 'core', axis=0, tiled=False)  12.1 us
    all_to_all x1, starting transfers between devices, local(): block = lax.all_to_all(everywhere, 'x', 0, 0, tiled=True)  11.6 us
    all_to_all x1, starting transfers between devices, local(): lax.all_to_all(outgoing.reshape(nz, 16, width), 'z', 0, 0, tiled=True)  8.35 us
    pallas_call x1, Pallas kernels, local(): pl.pallas_call(tail_kernel, name='project_place', out_shape=jax.ShapeDtyp...  6.46 us
  transfers between devices with their start and end apart: 8, of which 3 were waited for; matrix products, arithmetic and copies ran while one was open for 2% of the time, Pallas kernels for 6%

profile of v7, /device:TPU:1, one launch (start us, length us, event | category | flops | bytes accessed | tf_op | source)
XLA Modules:
  0.0 142.9 jit_solution(13159349553364418902)
XLA Ops:
  6.5 0.7 slice.12
  7.2 4.4 %collective-permute-start = (bf16[1,128]{1,0:T(2,128)(2,1)S(1)}, bf16[1,128]{1,0:T(2,128)(2,1)S(1)}, u32[]{:S(2)}, u32[]{:S(2)}) collective-permute-start(bf16[1,128]{1,0:T(2,128)(2,1)S(1)} %slice.12), channel_id=1, source_target_pairs={{0,8},{8,16},{16,24},{24,32},{32,40},{40,48},{48,56},{56,64},{64,7... | collective-permute-start | bytes 776 | tf_op jit(solution)/shard_map/ppermute | solution.py:249
  11.6 0.9 pad_maximum_fusion
  12.5 0.8 stack.2
  13.3 11.6 %all-to-all-start = ((bf16[4,100,448]{2,1,0:T(8,128)(2,1)}), bf16[4,100,448]{2,1,0:T(8,128)(2,1)S(1)}, u32[]{:S(2)}, u32[]{:S(2)}) async-start(bf16[4,100,448]{2,1,0:T(8,128)(2,1)} %stack.2), calls=%async_computation | async-start | bytes 851968 | tf_op jit(solution)/shard_map/all_to_all | solution.py:254
  24.9 3.1 %prep.1 = bf16[256,640]{1,0:T(8,128)(2,1)} custom-call(s32[1,192]{1,0:T(1,128)} %bitcast.39, s32[1,192]{1,0:T(1,128)} %bitcast.40, s32[1,192]{1,0:T(1,128)} %bitcast.41, bf16[160,768]{1,0:T(8,128)(2,1)} %bitcast.42, bf16[600,128]{1,0:T(8,128)(2,1)} %mel_ref.1, bf16[1,128]{1,0:T(2,128)(2,1)} %copy-done.7, bf16[160,384]{1,0:T(8,128)(2,1)} %bitcast.43), custom_call_target="tpu_custom_call" | custom-call | flops 2000000000 | bytes 8000000 | tf_op jit(solution)/shard_map/prep/pallas_call | solution.py:266
  28.1 3.3 %all-to-all-done = bf16[4,100,448]{2,1,0:T(8,128)(2,1)S(1)} async-done(((bf16[4,100,448]{2,1,0:T(8,128)(2,1)}), bf16[4,100,448]{2,1,0:T(8,128)(2,1)S(1)}, u32[]{:S(2)}, u32[]{:S(2)}) %all-to-all-start) | async-done | bytes 358432 | tf_op jit(solution)/shard_map/all_to_all | solution.py:254
  31.3 0.8 copy-done.2
  32.1 8.3 %all-to-all-start.1 = ((bf16[16,16,640]{2,1,0:T(8,128)(2,1)}), bf16[16,16,640]{2,1,0:T(8,128)(2,1)S(1)}, u32[]{:S(2)}, u32[]{:S(2)}) async-start(bf16[16,16,640]{2,1,0:T(8,128)(2,1)} %bitcast.38), calls=%async_computation.1 | async-start | bytes 655360 | tf_op jit(solution)/shard_map/all_to_all | solution.py:284
  40.5 5.4 %collective-permute-start.1 = (bf16[1280,640]{1,0:T(8,128)(2,1)S(1)}, bf16[1280,640]{1,0:T(8,128)(2,1)}, u32[]{:S(2)}, u32[]{:S(2)}) collective-permute-start(bf16[1280,640]{1,0:T(8,128)(2,1)S(1)} %copy-done.1), channel_id=1, source_target_pairs={{0,1},{1,0},{2,3},{3,2},{4,5},{5,4},{6,7},{7,6},{8,9},{9,8},{10,11... | collective-permute-start | bytes 4915208 | tf_op jit(solution)/shard_map/ppermute | solution.py:34
  45.9 1.9 %collective-permute-start.2 = (bf16[640,1280]{1,0:T(8,128)(2,1)}, bf16[640,1280]{1,0:T(8,128)(2,1)}, u32[]{:S(2)}, u32[]{:S(2)}) collective-permute-start(bf16[640,1280]{1,0:T(8,128)(2,1)} %down0.1), channel_id=1, source_target_pairs={{0,1},{1,0},{2,3},{3,2},{4,5},{5,4},{6,7},{7,6},{8,9},{9,8},{10,11... | collective-permute-start | bytes 4915208 | tf_op jit(solution)/shard_map/ppermute | solution.py:34
  47.9 0.1 select_reduce_fusion
  48.1 0.1 reshape.41
  48.2 0.1 reshape.43
  48.4 0.1 reshape.42
  48.5 0.1 copy.25
  48.6 0.1 reshape.44
  48.7 0.1 pad_add_fusion
  48.8 5.1 %all-to-all-done.1 = bf16[16,16,640]{2,1,0:T(8,128)(2,1)S(1)} async-done(((bf16[16,16,640]{2,1,0:T(8,128)(2,1)}), bf16[16,16,640]{2,1,0:T(8,128)(2,1)S(1)}, u32[]{:S(2)}, u32[]{:S(2)}) %all-to-all-start.1) | async-done | bytes 327712 | tf_op jit(solution)/shard_map/all_to_all | solution.py:284
  53.9 12.1 %all-gather = bf16[32,16,640]{2,1,0:T(8,128)(2,1)S(1)} all-gather(bf16[16,16,640]{2,1,0:T(8,128)(2,1)S(1)} %all-to-all-done.1), channel_id=2, replica_groups=mesh['x'=4,'z'=16,'y'=4,'core'=2] {'core'}, dimensions={0}, use_global_device_ids=true | all-gather | bytes 983040 | tf_op jit(solution)/shard_map/all_gather | solution.py:309
  66.1 0.2 copy.27
  66.3 0.1 constant_dynamic-slice_fusion.1
  66.4 13.6 %all_gather.20.video_ref = bf16[4,2,96,640]{3,2,1,0:T(8,128)(2,1)S(1)} all-gather(bf16[1,2,96,640]{3,2,1,0:T(8,128)(2,1)S(1)} %copy.28), channel_id=1, replica_groups=mesh['x'=4,'z'=16,'y'=4,'core'=2] {'y'}, dimensions={0}, use_global_device_ids=true | all-gather | bytes 1228800 | tf_op jit(solution)/shard_map/all_gather | solution.py:313
  80.0 5.7 %vision.1 = bf16[16,32,1280]{2,1,0:T(8,128)(2,1)S(1)} custom-call(bf16[4,2,96,640]{3,2,1,0:T(8,128)(2,1)S(1)} %all_gather.20.video_ref, bf16[2,3,8,640]{3,2,1,0:T(8,128)(2,1)S(1)} %bitcast.31, bf16[1280,640]{1,0:T(8,128)(2,1)S(1)} %copy-done.1, bf16[640,1280]{1,0:T(8,128)(2,1)} %down0.1, bf16[1280,640]{1,0:T(8,128)(2,1)} %collective-permute-done.1.up1, ...), custom_call_target="tpu_custom_call" | custom-call | flops 2516582400 | bytes 9000000 | tf_op jit(solution)/shard_map/vision/pallas_call | solution.py:319
  85.8 19.5 %all_to_all.15.in_ref = bf16[16,32,1280]{2,1,0:T(8,128)(2,1)S(1)} all-to-all(bf16[16,32,1280]{2,1,0:T(8,128)(2,1)S(1)} %vision.1), channel_id=1, replica_groups=mesh['x'=4,'z'=16,'y'=4,'core'=2] {'x','y'}, dimensions={0} | all-to-all | bytes 2621440 | tf_op jit(solution)/shard_map/all_to_all | solution.py:335
  105.2 0.1 slice_reduce_fusion
  105.4 12.4 %all_gather.21.own_ref = bf16[4,96,1280]{2,1,0:T(8,128)(2,1)S(1)} all-gather(bf16[1,96,1280]{2,1,0:T(8,128)(2,1)S(1)} %bitcast.35), channel_id=1, replica_groups=mesh['x'=4,'z'=16,'y'=4,'core'=2] {'y'}, dimensions={0}, use_global_device_ids=true | all-gather | bytes 1228800 | tf_op jit(solution)/shard_map/all_gather | solution.py:347
  117.8 7.7 %collective-permute-start.3 = (bf16[4,96,1280]{2,1,0:T(8,128)(2,1)S(1)}, bf16[4,96,1280]{2,1,0:T(8,128)(2,1)S(1)}, u32[]{:S(2)}, u32[]{:S(2)}) collective-permute-start(bf16[4,96,1280]{2,1,0:T(8,128)(2,1)S(1)} %all_gather.21.own_ref), channel_id=1, source_target_pairs={{0,1},{1,0},{2,3},{3,2},{4,5},{5,4},{6,7},{7,6},{8,9},{9,8},{10,11... | collective-permute-start | bytes 2949128 | tf_op jit(solution)/shard_map/ppermute | solution.py:34
  125.5 0.4 audio_spread.1.audio_own_ref
  126.0 1.9 %collective-permute-start.4 = (bf16[4,96,512]{2,1,0:T(8,128)(2,1)S(1)}, bf16[4,96,512]{2,1,0:T(8,128)(2,1)S(1)}, u32[]{:S(2)}, u32[]{:S(2)}) collective-permute-start(bf16[4,96,512]{2,1,0:T(8,128)(2,1)S(1)} %audio_spread.1.audio_own_ref), channel_id=1, source_target_pairs={{0,1},{1,0},{2,3},{3,2},{4,5},{5,4},{6,7},{7,6},{8,9},{9,8},{10,11... | collective-permute-start | bytes 1179656 | tf_op jit(solution)/shard_map/ppermute | solution.py:34
  127.9 1.7 %collective-permute-done.4.audio_other_ref = bf16[4,96,512]{2,1,0:T(8,128)(2,1)S(1)} collective-permute-done((bf16[4,96,512]{2,1,0:T(8,128)(2,1)S(1)}, bf16[4,96,512]{2,1,0:T(8,128)(2,1)S(1)}, u32[]{:S(2)}, u32[]{:S(2)}) %collective-permute-start.4) | collective-permute-done | bytes 393248 | tf_op jit(solution)/shard_map/ppermute | solution.py:34
  129.6 6.5 %project_place.1 = bf16[448,512]{1,0:T(8,128)(2,1)} custom-call(bf16[4,96,1280]{2,1,0:T(8,128)(2,1)S(1)} %all_gather.21.own_ref, bf16[4,96,1280]{2,1,0:T(8,128)(2,1)S(1)} %collective-permute-done.3.other_ref, bf16[4,96,512]{2,1,0:T(8,128)(2,1)S(1)} %audio_spread.1.audio_own_ref, bf16[4,96,512]{2,1,0:T(8,128)(2,1)S(1)} %collective-permute-done.4.audio_other_ref, ...), custom_call_target="tpu_custom_call" | custom-call | flops 1100000000 | bytes 9000000 | tf_op jit(solution)/shard_map/project_place/pallas_call | solution.py:350
  (30 shorter events, 0.2 us)
Async XLA Ops:
  7.2 5.3 %collective-permute-start = (bf16[1,128]{1,0:T(2,128)(2,1)S(1)}, bf16[1,128]{1,0:T(2,128)(2,1)S(1)}, u32[]{:S(2)}, u32[]{:S(2)}) collective-permute-start(bf16[1,128]{1,0:T(2,128)(2,1)S(1)} %slice.12), channel_id=1, source_target_pairs={{0,8},{8,16},{16,24},{24,32},{32,40},{40,48},{48,56},{56,64},{64,7... | collective-permute-start | bytes 776 | tf_op jit(solution)/shard_map/ppermute | solution.py:249
  12.5 12.4 %copy-start.7 = (bf16[1,128]{1,0:T(2,128)(2,1)}, bf16[1,128]{1,0:T(2,128)(2,1)S(1)}, u32[]{:S(2)}) copy-start(bf16[1,128]{1,0:T(2,128)(2,1)S(1)} %collective-permute-done.rim_ref) | copy-start | bytes 772
  13.3 18.0 %all-to-all-start = ((bf16[4,100,448]{2,1,0:T(8,128)(2,1)}), bf16[4,100,448]{2,1,0:T(8,128)(2,1)S(1)}, u32[]{:S(2)}, u32[]{:S(2)}) async-start(bf16[4,100,448]{2,1,0:T(8,128)(2,1)} %stack.2), calls=%async_computation | async-start | bytes 851968 | tf_op jit(solution)/shard_map/all_to_all | solution.py:254
  24.9 104.7 %all-gather.4.cloned.1.call-start = ((), (), s32[]{:S(2)}) async-start(), calls=%async_computation.3 | async-start | bytes 7241728 | tf_op jit(solution)/shard_map/all_gather | solution.py:283
  24.9 15.6 %copy-start.1 = (bf16[1280,640]{1,0:T(8,128)(2,1)S(1)}, bf16[1280,640]{1,0:T(8,128)(2,1)}, u32[]{:S(2)}) copy-start(bf16[1280,640]{1,0:T(8,128)(2,1)} %up0.1) | copy-start | bytes 4915204
  24.9 23.0 %copy-start.3 = (s32[192]{0:T(256)S(1)}, s32[192]{0:T(256)}, u32[]{:S(2)}) copy-start(s32[192]{0:T(256)} %param.20) | copy-start | bytes 2308
  24.9 23.0 %copy-start.4 = (s32[192]{0:T(256)S(1)}, s32[192]{0:T(256)}, u32[]{:S(2)}) copy-start(s32[192]{0:T(256)} %param.21) | copy-start | bytes 2308
  24.9 23.1 %copy-start.5 = (s32[192]{0:T(256)S(1)}, s32[192]{0:T(256)}, u32[]{:S(2)}) copy-start(s32[192]{0:T(256)} %param.23) | copy-start | bytes 2308
  24.9 23.1 %copy-start.6 = (s32[192]{0:T(256)S(1)}, s32[192]{0:T(256)}, u32[]{:S(2)}) copy-start(s32[192]{0:T(256)} %param.22) | copy-start | bytes 2308
  31.3 0.8 copy-start.2
  32.1 21.8 %all-to-all-start.1 = ((bf16[16,16,640]{2,1,0:T(8,128)(2,1)}), bf16[16,16,640]{2,1,0:T(8,128)(2,1)S(1)}, u32[]{:S(2)}, u32[]{:S(2)}) async-start(bf16[16,16,640]{2,1,0:T(8,128)(2,1)} %bitcast.38), calls=%async_computation.1 | async-start | bytes 655360 | tf_op jit(solution)/shard_map/all_to_all | solution.py:284
  40.5 39.5 %collective-permute-start.1 = (bf16[1280,640]{1,0:T(8,128)(2,1)S(1)}, bf16[1280,640]{1,0:T(8,128)(2,1)}, u32[]{:S(2)}, u32[]{:S(2)}) collective-permute-start(bf16[1280,640]{1,0:T(8,128)(2,1)S(1)} %copy-done.1), channel_id=1, source_target_pairs={{0,1},{1,0},{2,3},{3,2},{4,5},{5,4},{6,7},{7,6},{8,9},{9,8},{10,11... | collective-permute-start | bytes 4915208 | tf_op jit(solution)/shard_map/ppermute | solution.py:34
  45.9 34.1 %collective-permute-start.2 = (bf16[640,1280]{1,0:T(8,128)(2,1)}, bf16[640,1280]{1,0:T(8,128)(2,1)}, u32[]{:S(2)}, u32[]{:S(2)}) collective-permute-start(bf16[640,1280]{1,0:T(8,128)(2,1)} %down0.1), channel_id=1, source_target_pairs={{0,1},{1,0},{2,3},{3,2},{4,5},{5,4},{6,7},{7,6},{8,9},{9,8},{10,11... | collective-permute-start | bytes 4915208 | tf_op jit(solution)/shard_map/ppermute | solution.py:34
  105.4 24.2 %copy-start = (bf16[512,1,448]{0,2,1:T(8,128)(2,1)S(1)}, bf16[512,1,448]{0,2,1:T(8,128)(2,1)}, u32[]{:S(2)}) copy-start(bf16[512,1,448]{0,2,1:T(8,128)(2,1)} %param.19) | copy-start | bytes 1376260
  117.8 11.8 %collective-permute-start.3 = (bf16[4,96,1280]{2,1,0:T(8,128)(2,1)S(1)}, bf16[4,96,1280]{2,1,0:T(8,128)(2,1)S(1)}, u32[]{:S(2)}, u32[]{:S(2)}) collective-permute-start(bf16[4,96,1280]{2,1,0:T(8,128)(2,1)S(1)} %all_gather.21.own_ref), channel_id=1, source_target_pairs={{0,1},{1,0},{2,3},{3,2},{4,5},{5,4},{6,7},{7,6},{8,9},{9,8},{10,11... | collective-permute-start | bytes 2949128 | tf_op jit(solution)/shard_map/ppermute | solution.py:34
  126.0 3.6 %collective-permute-start.4 = (bf16[4,96,512]{2,1,0:T(8,128)(2,1)S(1)}, bf16[4,96,512]{2,1,0:T(8,128)(2,1)S(1)}, u32[]{:S(2)}, u32[]{:S(2)}) collective-permute-start(bf16[4,96,512]{2,1,0:T(8,128)(2,1)S(1)} %audio_spread.1.audio_own_ref), channel_id=1, source_target_pairs={{0,1},{1,0},{2,3},{3,2},{4,5},{5,4},{6,7},{7,6},{8,9},{9,8},{10,11... | collective-permute-start | bytes 1179656 | tf_op jit(solution)/shard_map/ppermute | solution.py:34
Sparse Core Ops, SparseCore 0:
  32.2 95.2 all-gather.3
